TPU v7x, 256 devices: a whole 4x4x8 slice. The times are simulated.
256 devices in a mesh: dom: 128 (over y, x, z), col: 2 (over core).
Axes of the slice: x: 4, y: 4, z: 8, core: 2. Of those that a mesh axis runs over, the one named last changes fastest.
Arguments:
- features: bfloat16 [131072, 256], P(('dom', 'col')), may hold values from -6 to 6
- weight: bfloat16 [256, 256], replicated, may hold values from -0.375 to 0.375
- cotangent: bfloat16 [131072, 256], P(('dom', 'col')), may hold values from -6 to 6
- tile_values: bfloat16 [10240, 128, 128], P(('dom', 'col')), may hold values from -0.15625 to 0.15625
- tile_rows: int32 [10240], P(('dom', 'col')), may hold values from 0 to 7
- tile_cols: int32 [10240], P(('dom', 'col')), may hold values from 0 to 131, as said below
- tile_count: int32 [256], P(('dom', 'col')), may hold values from 20 to 40, as said below
- send_blocks: int32 [256, 128], P(('dom', 'col')), may hold values from 0 to 3
Outputs:
- output_rows: bfloat16 [131072, 256], P(('dom', 'col'))
- feature_grad: bfloat16 [131072, 256], P(('dom', 'col'))
- weight_grad: float32 [256, 256], replicated
Inputs may be any that keep to these rules, and one draw needn't show every extreme that they name: `tile_cols`: A value v below 4 names the device's own row block v; a value 4 + s names the row block that the device of partition s with the same col index sends to this partition; no receive slot is named by two tiles of one device. Only the first tile_count slots of a device's tiles are live; some device has all 40 live.
All inputs are finite; a program needn't handle non-finite values.
Results may differ from a plain program's by a relative error of at most 0.0049.
Values may be sent and summed in bfloat16 or wider, within the bound.
No kernel may reach another device: no remote copies, remote signals or barrier semaphores. Data moves between devices by JAX's collectives and lax.ppermute only.
A program may use at most 128 MiB of HBM per device.

v0:
```python
import jax
import jax.numpy as jnp
from jax import lax
from jax.sharding import PartitionSpec as P


def in_one_piece(arrays, axis, split_dim, concat_dim, along):
    ends, at = ([], 0)
    for a in arrays[:-1]:
        at += a.shape[along]
        ends.append(at)
    both = jnp.concatenate(arrays, axis=along)
    return tuple(
        jnp.split(
            lax.all_to_all(both, axis, split_axis=split_dim, concat_axis=concat_dim, tiled=True),
            ends,
            axis=along,
        )
    )


def local(features, weight, cotangent, tile_values, tile_rows, tile_cols, tile_count, send_blocks):
    block_size = tile_values.shape[1]
    half_blocks = features.shape[0] // block_size
    width_in = features.shape[1]
    peer_count = send_blocks.shape[1]
    all_blocks = half_blocks * lax.axis_size("col")
    node_total = features.shape[0] * lax.axis_size("col") * lax.axis_size("dom")
    own_blocks = features.reshape(half_blocks, block_size, width_in)
    outgoing = own_blocks[send_blocks[0]]
    incoming = lax.all_to_all(outgoing, "dom", split_axis=0, concat_axis=0, tiled=True)
    sources = jnp.concatenate([own_blocks, incoming], axis=0)
    live_bool = jnp.arange(tile_values.shape[0], dtype=jnp.int32) < tile_count[0]
    live_mask = live_bool.astype(jnp.bfloat16)
    masked_tiles = tile_values * live_mask[:, None, None]
    picked = sources[tile_cols]
    products = jnp.einsum("tij,tjf->tif", masked_tiles, picked, preferred_element_type=jnp.float32)
    partial_value = jax.ops.segment_sum(products, tile_rows, num_segments=all_blocks)
    summed = lax.psum_scatter(partial_value, "col", scatter_dimension=0, tiled=True)
    hidden = summed.astype(jnp.bfloat16).reshape(half_blocks * block_size, width_in)
    output_rows = jnp.dot(hidden, weight, preferred_element_type=jnp.float32).astype(jnp.bfloat16)
    own_grad = lax.dot_general(
        cotangent, weight, (((1,), (1,)), ((), ())), preferred_element_type=jnp.float32
    ).astype(jnp.bfloat16)
    own_grad = own_grad.reshape(half_blocks, block_size, width_in)
    grad_blocks = lax.all_gather(own_grad, "col", axis=0, tiled=True)
    chosen = grad_blocks[tile_rows]
    is_local = tile_cols < half_blocks
    local_tiles = masked_tiles * is_local.astype(jnp.bfloat16)[:, None, None]
    back_terms = jnp.einsum("tji,tjf->tif", local_tiles, chosen, preferred_element_type=jnp.float32)
    local_ids = jnp.where(is_local, tile_cols, 0)
    own_part = jax.ops.segment_sum(back_terms, local_ids, num_segments=half_blocks)
    slot_ids = half_blocks + jnp.arange(peer_count, dtype=jnp.int32)
    matches = ((tile_cols[:, None] == slot_ids[None, :]) & live_bool[:, None]).astype(jnp.bfloat16)
    slot_tiles = jnp.einsum(
        "ts,tij->sij", matches, tile_values, preferred_element_type=jnp.float32
    ).astype(jnp.bfloat16)
    slot_grads = jnp.einsum(
        "ts,tjf->sjf", matches, chosen, preferred_element_type=jnp.float32
    ).astype(jnp.bfloat16)
    back_tiles, back_grads = in_one_piece((slot_tiles, slot_grads), "dom", 0, 0, 2)
    remote_terms = jnp.einsum(
        "sji,sjf->sif", back_tiles, back_grads, preferred_element_type=jnp.float32
    )
    grad_total = own_part + jax.ops.segment_sum(
        remote_terms, send_blocks[0], num_segments=half_blocks
    )
    feature_grad = grad_total.astype(jnp.bfloat16).reshape(half_blocks * block_size, width_in)
    local_weight = lax.dot_general(
        hidden, cotangent, (((0,), (0,)), ((), ())), preferred_element_type=jnp.float32
    )
    local_weight = local_weight * jnp.float32(1.0 / node_total**0.5)
    weight_grad = lax.psum(local_weight, ("dom", "col"))
    return (output_rows, feature_grad, weight_grad)


def solution(mesh):
    return jax.shard_map(
        local,
        mesh=mesh,
        in_specs=(
            P(("dom", "col"), None),
            P(),
            P(("dom", "col"), None),
            P(("dom", "col"), None, None),
            P(("dom", "col")),
            P(("dom", "col")),
            P(("dom", "col")),
            P(("dom", "col"), None),
        ),
        out_specs=(P(("dom", "col"), None), P(("dom", "col"), None), P()),
        check_vma=False,
    )
```

profile of v0, /device:TPU:1, one launch (start us, length us, event | category | flops | bytes accessed | tf_op | source)
XLA Modules:
  0.0 573.6 jit_solution(5552977802668099284)
XLA Ops:
  7.9 7.4 %gather_fusion = bf16[128,128,256]{2,1,0:T(8,128)(2,1)} fusion(bf16[4,128,256]{2,1,0:T(8,128)(2,1)} %bitcast.25, s32[1024]{0:T(1024)S(1)} %pad_clamp_fusion.2), kind=kCustom, calls=%fused_computation | custom fusion | bytes 16777728 | tf_op jit(solution)/shard_map/gather | solution.py:30
  15.3 17.0 %all-to-all-start = ((bf16[128,128,256]{2,1,0:T(8,128)(2,1)}), bf16[128,128,256]{2,1,0:T(8,128)(2,1)}, u32[]{:S(2)}, u32[]{:S(2)}) async-start(bf16[128,128,256]{2,1,0:T(8,128)(2,1)} %gather_fusion), calls=%async_computation | async-start | bytes 16777216 | tf_op jit(solution)/shard_map/all_to_all | solution.py:31
  33.0 3.8 convolution_convert_fusion.1
  36.8 6.4 %copy.26 = bf16[128,128,128]{2,0,1:T(8,128)(2,1)} copy(bf16[128,128,128]{0,2,1:T(8,128)(2,1)} %convolution_convert_fusion.1) | data formatting | bytes 8388608 | tf_op jit(solution)/shard_map/convert_element_type | solution.py:57
  43.5 3.0 all_gather.3
  47.2 2.5 convolution_convert_fusion
  50.3 2.3 pad_maximum_fusion
  52.6 29.1 %copy.27 = bf16[128,128,384]{2,1,0:T(8,128)(2,1)} copy(bf16[128,128,384]{2,0,1:T(8,128)(2,1)S(1)} %pad_maximum_fusion) | data formatting | bytes 25165824 | tf_op jit(solution)/shard_map/concatenate | solution.py:12
  81.7 136.7 %all-to-all-done = bf16[128,128,256]{2,1,0:T(8,128)(2,1)} async-done(((bf16[128,128,256]{2,1,0:T(8,128)(2,1)}), bf16[128,128,256]{2,1,0:T(8,128)(2,1)}, u32[]{:S(2)}, u32[]{:S(2)}) %all-to-all-start) | async-done | bytes 8388640 | tf_op jit(solution)/shard_map/all_to_all | solution.py:31
  218.4 7.6 %all-to-all-start.1 = ((bf16[128,128,384]{2,1,0:T(8,128)(2,1)}), bf16[128,128,384]{2,1,0:T(8,128)(2,1)}, u32[]{:S(2)}, u32[]{:S(2)}) async-start(bf16[128,128,384]{2,1,0:T(8,128)(2,1)} %copy.27), calls=%async_computation.2 | async-start | bytes 25165824 | tf_op jit(solution)/shard_map/all_to_all | solution.py:15
  226.4 7.5 %pad_maximum_fusion.1 = bf16[132,128,256]{2,1,0:T(8,128)(2,1)} fusion(bf16[128,128,256]{2,1,0:T(8,128)(2,1)} %all-to-all-done, bf16[4,128,256]{2,1,0:T(8,128)(2,1)S(1)} %bitcast.26), kind=kLoop, calls=%fused_computation.7 | loop fusion | flops 4325376 | bytes 17301504 | tf_op jit(solution)/shard_map/concatenate | solution.py:32
  233.9 6.0 %gather_fusion.1 = bf16[40,128,256]{2,1,0:T(8,128)(2,1)} fusion(bf16[132,128,256]{2,1,0:T(8,128)(2,1)} %pad_maximum_fusion.1, s32[1024]{0:T(1024)S(1)} %pad_clamp_fusion.1), kind=kCustom, calls=%fused_computation.1 | custom fusion | bytes 5243040 | tf_op jit(solution)/shard_map/gather | solution.py:36
  239.9 4.9 fusion.8
  245.0 9.0 %scatter_fusion = f32[8,128,256]{2,1,0:T(8,128)S(1)} fusion(f32[8,128,256]{2,1,0:T(8,128)S(1)} %broadcast_in_dim.12, s32[40]{0:T(128)S(1)} %copy-done.10, f32[40,128,256]{2,1,0:T(8,128)} %fusion.8), kind=kCustom, calls=%fused_computation.3 | custom fusion | flops 1310720 | bytes 15728800 | tf_op jit(solution)/shard_map/scatter-add | solution.py:38
  255.1 5.3 fusion.5
  260.4 9.0 %scatter_fusion.1 = f32[4,128,256]{2,1,0:T(8,128)S(1)} fusion(f32[4,128,256]{2,1,0:T(8,128)S(1)} %broadcast.41.clone, s32[40]{0:T(128)S(1)} %get-tuple-element.3, f32[40,128,256]{2,1,0:T(8,128)} %fusion.5), kind=kCustom, calls=%fused_computation.4 | custom fusion | flops 1310720 | bytes 15728800 | tf_op jit(solution)/shard_map/scatter-add | solution.py:52
  269.4 4.2 reduce-scatter.2.cloned.1.call-done
  273.6 1.1 convert_element_type.30
  274.6 1.0 convolution_multiply_fusion
  276.6 223.8 %all-to-all-done.1 = bf16[128,128,384]{2,1,0:T(8,128)(2,1)} async-done(((bf16[128,128,384]{2,1,0:T(8,128)(2,1)}), bf16[128,128,384]{2,1,0:T(8,128)(2,1)}, u32[]{:S(2)}, u32[]{:S(2)}) %all-to-all-start.1) | async-done | bytes 12582944 | tf_op jit(solution)/shard_map/all_to_all | solution.py:15
  500.4 12.8 %fusion = f32[128,128,256]{2,1,0:T(8,128)} fusion(bf16[128,128,384]{2,1,0:T(8,128)(2,1)} %all-to-all-done.1), kind=kOutput, calls=%fused_computation.8 | convolution fusion | flops 1073741824 | bytes 29360128 | tf_op jit(solution)/shard_map/sji,sjf->sif/dot_general | solution.py:62
  513.2 24.1 %scatter_fusion.2 = f32[4,128,256]{2,1,0:T(8,128)S(1)} fusion(f32[4,128,256]{2,1,0:T(8,128)S(1)} %broadcast.41.clone.1, s32[128]{0:T(128)S(1)} %bitcast.31, f32[128,128,256]{2,1,0:T(8,128)} %fusion), kind=kCustom, calls=%fused_computation.5 | custom fusion | flops 4194304 | bytes 50332160 | tf_op jit(solution)/shard_map/scatter-add | solution.py:65
  538.1 27.0 %all-reduce.2.cloned.1.call-done = f32[256,256]{1,0:T(8,128)} async-done(((f32[256,256]{1,0:T(8,128)}), f32[256,256]{1,0:T(8,128)}) %all-reduce.2.cloned.1.call-update) | async-done | bytes 262160 | tf_op jit(solution)/shard_map/psum | solution.py:73
  565.1 1.7 copy.40
  (45 shorter events, 5.6 us)
Async XLA Ops:
  7.2 36.1 %copy-start = (bf16[512,256]{1,0:T(8,128)(2,1)S(1)}, bf16[512,256]{1,0:T(8,128)(2,1)}, u32[]{:S(2)}) copy-start(bf16[512,256]{1,0:T(8,128)(2,1)} %param.10) | copy-start | bytes 786436
  15.3 17.7 %copy-start.5 = (bf16[40,128,128]{2,1,0:T(8,128)(2,1)S(1)}, bf16[40,128,128]{2,1,0:T(8,128)(2,1)}, u32[]{:S(2)}) copy-start(bf16[40,128,128]{2,1,0:T(8,128)(2,1)} %param.11) | copy-start | bytes 3932164
  15.3 17.7 %copy-start.8 = (s32[40]{0:T(128)S(1)}, s32[40]{0:T(128)}, u32[]{:S(2)}) copy-start(s32[40]{0:T(128)} %param.13) | copy-start | bytes 484
  15.3 203.1 %all-to-all-start = ((bf16[128,128,256]{2,1,0:T(8,128)(2,1)}), bf16[128,128,256]{2,1,0:T(8,128)(2,1)}, u32[]{:S(2)}, u32[]{:S(2)}) async-start(bf16[128,128,256]{2,1,0:T(8,128)(2,1)} %gather_fusion), calls=%async_computation | async-start | bytes 16777216 | tf_op jit(solution)/shard_map/all_to_all | solution.py:31
  36.8 6.4 %copy-start.9 = (s32[40]{0:T(128)S(1)}, s32[40]{0:T(128)}, u32[]{:S(2)}) copy-start(s32[40]{0:T(128)} %param.12) | copy-start | bytes 484
  36.8 6.4 %copy-start.7 = (bf16[256,256]{1,0:T(8,128)(2,1)S(1)}, bf16[256,256]{1,0:T(8,128)(2,1)}, u32[]{:S(2)}) copy-start(bf16[256,256]{1,0:T(8,128)(2,1)} %param.9) | copy-start | bytes 393220
  47.2 2.5 copy-start.3
  47.2 3.1 copy-start.4
  81.7 144.7 %copy-start.1 = (bf16[512,256]{1,0:T(8,128)(2,1)S(1)}, bf16[512,256]{1,0:T(8,128)(2,1)}, u32[]{:S(2)}) copy-start(bf16[512,256]{1,0:T(8,128)(2,1)} %param.8) | copy-start | bytes 786436
  218.4 281.9 %all-to-all-start.1 = ((bf16[128,128,384]{2,1,0:T(8,128)(2,1)}), bf16[128,128,384]{2,1,0:T(8,128)(2,1)}, u32[]{:S(2)}, u32[]{:S(2)}) async-start(bf16[128,128,384]{2,1,0:T(8,128)(2,1)} %copy.27), calls=%async_computation.2 | async-start | bytes 25165824 | tf_op jit(solution)/shard_map/all_to_all | solution.py:15
  226.0 47.5 %reduce-scatter.2.cloned.1.call-start = ((), (), s32[]{:S(2)}) async-start(), calls=%async_computation.3 | async-start | bytes 1572864 | tf_op jit(solution)/shard_map/reduce_scatter | solution.py:39
  233.9 6.0 %copy-start.6 = (bf16[40,128,128]{2,1,0:T(8,128)(2,1)S(1)}, bf16[40,128,128]{2,1,0:T(8,128)(2,1)}, u32[]{:S(2)}) copy-start(bf16[40,128,128]{2,1,0:T(8,128)(2,1)} %param.11) | copy-start | bytes 3932164
  239.9 5.0 copy-start.10
  254.0 1.0 copy-start.2
  255.0 310.1 %all-reduce.2.cloned.1.call-start = ((), (), s32[]{:S(2)}) async-start(), calls=%async_computation.4 | async-start | bytes 524288 | tf_op jit(solution)/shard_map/psum | solution.py:73
  276.6 236.6 %copy-start.11 = (s32[1,128]{1,0:T(1,128)S(1)}, s32[1,128]{1,0:T(1,128)}, u32[]{:S(2)}) copy-start(s32[1,128]{1,0:T(1,128)} %param.15) | copy-start | bytes 1540
Sparse Core Ops, SparseCore 0:
  255.1 18.3 reduce-scatter.1
  280.5 284.5 all-reduce.1
where the time goes:
time: 575 us; the launch traced here: 574 us
  waiting for transfers between devices  392 us (68%)
  other arithmetic  54.5 us (9%)
  local copies, waits for them, and re-layouts  53.2 us (9%)
  matrix products  31.4 us (5%)
  starting transfers between devices  24.9 us (4%)
  between operations  14.9 us (3%)
    all_to_all x1, waiting for transfers between devices, in_one_piece(): lax.all_to_all(both, axis, split_axis=split_dim, concat_axis=concat_dim,...  224 us
    all_to_all x1, waiting for transfers between devices, local(): lax.all_to_all(outgoing, 'dom', split_axis=0, concat_axis=0, tiled=True)  137 us
    concatenate x1, local copies, waits for them, and re-layouts, in_one_piece(): both = jnp.concatenate(arrays, axis=along)  29.1 us
    psum x1, waiting for transfers between devices, local(): weight_grad = lax.psum(local_weight, ('dom', 'col'))  27 us
    scatter-add x1, other arithmetic, local(): jax.ops.segment_sum(remote_terms, send_blocks[0], num_segments=half_blocks)  24.1 us
    all_to_all x1, starting transfers between devices, local(): lax.all_to_all(outgoing, 'dom', split_axis=0, concat_axis=0, tiled=True)  17 us
    dot_general x1, matrix products, local(): jnp.einsum('sji,sjf->sif', back_tiles, back_grads, preferred_element_type...  12.8 us
  transfers between devices with their start and end apart: 4, of which 4 were waited for; matrix products, arithmetic and copies ran while one was open for 22% of the time, Pallas kernels for 0%

commit v1 on v0

v1 whole, which is shorter than its diff:
```python
import functools

import jax
import jax.numpy as jnp
from jax import lax
from jax.experimental import pallas as pl
from jax.experimental.pallas import tpu as pltpu
from jax.sharding import Mesh
from jax.sharding import PartitionSpec as P

PLANE = ("y", "x")
DOM = ("y", "x", "z")
SIZES = (4, 4, 8, 2)
BLK = 128
META = 16
VMEM_LIMIT = 60 * 2**20


def pack_kernel(cols, count, tiles, meta, out, tile_sem, meta_sem):
    groups, slots = out.shape[0], (out.shape[1] - META) // BLK

    def tile_copy(t):
        slot = jnp.maximum(cols[t] - 4, 0)
        d, z = lax.div(slot, slots), lax.rem(slot, slots)
        place = out.at[d, pl.ds(pl.multiple_of(z * BLK, BLK), BLK), :]
        return pltpu.make_async_copy(tiles.at[t], place, tile_sem.at[t])

    def start(t, carry):
        @pl.when(cols[t] >= 4)
        def _():
            tile_copy(t).start()

        return carry

    def finish(t, carry):
        @pl.when(cols[t] >= 4)
        def _():
            tile_copy(t).wait()

        return carry

    lax.fori_loop(0, count[0], start, 0)
    last = pltpu.make_async_copy(meta, out.at[:, pl.ds(slots * BLK, META), :], meta_sem)
    last.start()
    lax.fori_loop(0, count[0], finish, 0)
    last.wait()


def pack(cols, count, tiles, meta):
    groups, slots = 16, 8
    smem = pl.BlockSpec(memory_space=pltpu.SMEM)
    hbm = pl.BlockSpec(memory_space=pl.ANY)
    return pl.pallas_call(
        pack_kernel,
        out_shape=jax.ShapeDtypeStruct((groups, slots * BLK + META, BLK), tiles.dtype),
        in_specs=[smem, smem, hbm, hbm],
        out_specs=hbm,
        scratch_shapes=[pltpu.SemaphoreType.DMA((tiles.shape[0],)), pltpu.SemaphoreType.DMA],
        name="pack_tiles",
    )(cols, count, tiles, meta)


def rows_at(k):
    return pl.ds(pl.multiple_of(k * BLK, BLK), BLK)


def hidden_kernel(where, meta, ids, cols, rows, count, sent, feats, tiles, mine, peer, total, sem):
    half = total.shape[0] // 2
    c, z_me, r_me = where[0], where[1], where[2]

    def clear(i, carry):
        total[i] = jnp.zeros(total.shape[1:], total.dtype)
        return carry

    lax.fori_loop(0, 2 * half, clear, 0)

    def place(r, row):
        other = jnp.bitwise_xor(lax.div(row, 4), c)
        return other * half + r * 4 + lax.rem(row, 4)

    def remote(i, carry):
        r, z = lax.div(i, 8), lax.rem(i, 8)

        @pl.when(meta[i] > 0)
        def _():
            block = feats[z, rows_at(ids[z * 16 + r]), :]
            term = jnp.dot(sent[r, rows_at(z), :], block, preferred_element_type=jnp.float32)
            at = place(r, meta[i] - 1)
            total[at] = total[at] + term

        return carry

    lax.fori_loop(0, 128, remote, 0)

    def own(t, carry):
        @pl.when(cols[t] < 4)
        def _():
            block = feats[z_me, rows_at(jnp.minimum(cols[t], 3)), :]
            term = jnp.dot(tiles[t], block, preferred_element_type=jnp.float32)
            at = place(r_me, rows[t])
            total[at] = total[at] + term

        return carry

    lax.fori_loop(0, count[0], own, 0)
    copy = pltpu.make_async_copy(total.at[pl.ds(0, half)], mine, sem)
    copy.start()

    def cast(i, carry):
        peer[i] = total[half + i].astype(peer.dtype)
        return carry

    lax.fori_loop(0, half, cast, 0)
    copy.wait()


def hidden_parts(where, meta, ids, cols, rows, count, sent, feats, tiles):
    smem = pl.BlockSpec(memory_space=pltpu.SMEM)
    vmem = pl.BlockSpec(memory_space=pltpu.VMEM)
    width = feats.shape[2]
    return pl.pallas_call(
        hidden_kernel,
        out_shape=(
            jax.ShapeDtypeStruct((64, BLK, width), jnp.float32),
            jax.ShapeDtypeStruct((64, BLK, width), jnp.bfloat16),
        ),
        in_specs=[smem] * 6 + [vmem] * 3,
        out_specs=(pl.BlockSpec(memory_space=pl.ANY), vmem),
        scratch_shapes=[pltpu.VMEM((128, BLK, width), jnp.float32), pltpu.SemaphoreType.DMA],
        compiler_params=pltpu.CompilerParams(vmem_limit_bytes=VMEM_LIMIT),
        name="hidden_parts",
    )(where, meta, ids, cols, rows, count, sent, feats, tiles)


def grad_kernel(where, meta, ids, cols, rows, count, sent, grad_mine, grad_peer, tiles, out):
    c, z_me, r_me = where[0], where[1], where[2]

    def clear(i, carry):
        out[i] = jnp.zeros(out.shape[1:], out.dtype)
        return carry

    lax.fori_loop(0, out.shape[0], clear, 0)

    def add(at, tile, r, row):
        def go(source):
            term = lax.dot_general(
                tile, source[r * 4 + lax.rem(row, 4)], (((0,), (0,)), ((), ())),
                preferred_element_type=jnp.float32,
            )
            out[at] = out[at] + term

        @pl.when(lax.div(row, 4) == c)
        def _():
            go(grad_mine)

        @pl.when(lax.div(row, 4) != c)
        def _():
            go(grad_peer)

    def remote(i, carry):
        r, z = lax.div(i, 8), lax.rem(i, 8)

        @pl.when(meta[i] > 0)
        def _():
            add(z * 4 + ids[z * 16 + r], sent[r, rows_at(z), :], r, meta[i] - 1)

        return carry

    lax.fori_loop(0, 128, remote, 0)

    def own(t, carry):
        @pl.when(cols[t] < 4)
        def _():
            add(z_me * 4 + jnp.minimum(cols[t], 3), tiles[t], r_me, rows[t])

        return carry

    lax.fori_loop(0, count[0], own, 0)


def grad_parts(where, meta, ids, cols, rows, count, sent, grad_mine, grad_peer, tiles):
    smem = pl.BlockSpec(memory_space=pltpu.SMEM)
    vmem = pl.BlockSpec(memory_space=pltpu.VMEM)
    width = grad_mine.shape[2]
    return pl.pallas_call(
        grad_kernel,
        out_shape=jax.ShapeDtypeStruct((32, BLK, width), jnp.float32),
        in_specs=[smem] * 6 + [vmem] * 4,
        out_specs=vmem,
        compiler_params=pltpu.CompilerParams(vmem_limit_bytes=VMEM_LIMIT),
        name="grad_parts",
    )(where, meta, ids, cols, rows, count, sent, grad_mine, grad_peer, tiles)


def swap_cores(a):
    return lax.ppermute(a, "col", [(0, 1), (1, 0)])


def sum_everywhere(term, c):
    n = term.shape[1]
    halves = term.reshape(2, 128, n)
    keep = lax.dynamic_index_in_dim(halves, c, 0, keepdims=False)
    give = lax.dynamic_index_in_dim(halves, 1 - c, 0, keepdims=False)
    half = keep + swap_cores(give)
    rows = lax.all_to_all(half.reshape(128, 1, n), DOM, 0, 0, tiled=True)
    row = jnp.sum(rows, axis=0, keepdims=True)
    half = lax.all_to_all(jnp.broadcast_to(row, (128, 1, n)), DOM, 0, 0, tiled=True).reshape(128, n)
    other = swap_cores(half)
    first = jnp.where(c == 0, half, other)
    second = jnp.where(c == 0, other, half)
    return jnp.concatenate([first, second], axis=0)


def local(features, weight, cotangent, tile_values, tile_rows, tile_cols, tile_count, send_blocks):
    width = features.shape[1]
    node_total = features.shape[0] * lax.axis_size("col") * lax.axis_size(DOM)
    c = lax.axis_index("col")
    z_me = lax.axis_index("z")
    r_me = lax.axis_index(PLANE)
    where = jnp.stack([c, z_me, r_me]).astype(jnp.int32)

    ids_row = jnp.pad(send_blocks.astype(jnp.bfloat16), ((0, META - 1), (0, width - send_blocks.shape[1])))
    column = lax.all_gather(jnp.concatenate([features, ids_row], axis=0), "z", axis=0)
    own_grad = lax.dot_general(
        cotangent, weight, (((1,), (1,)), ((), ())), preferred_element_type=jnp.float32
    ).astype(jnp.bfloat16)
    grad_mine = lax.all_gather(own_grad.reshape(4, BLK, width), PLANE, axis=0, tiled=True)
    grad_peer = swap_cores(grad_mine)

    live = jnp.arange(tile_cols.shape[0], dtype=jnp.int32) < tile_count[0]
    slots = 4 + jnp.arange(128, dtype=jnp.int32)
    match = (tile_cols[:, None] == slots[None, :]) & live[:, None]
    slot_rows = jnp.sum(jnp.where(match, tile_rows[:, None] + 1, 0), axis=0)
    meta_rows = jnp.pad(
        slot_rows.astype(jnp.bfloat16).reshape(16, 1, 8), ((0, 0), (0, META - 1), (0, BLK - 8))
    )
    sent = lax.all_to_all(pack(tile_cols, tile_count, tile_values, meta_rows), PLANE, 0, 0, tiled=True)

    meta = sent[:, 8 * BLK, :8].astype(jnp.int32).reshape(128)
    ids = column[:, 4 * BLK, :128].astype(jnp.int32).reshape(8, 16, 8)
    ids = lax.dynamic_index_in_dim(ids, z_me, 2, keepdims=False).reshape(128)

    mine, peer = hidden_parts(where, meta, ids, tile_cols, tile_rows, tile_count, sent, column, tile_values)
    both = (mine + swap_cores(peer).astype(jnp.float32)).astype(jnp.bfloat16)
    parts = lax.all_to_all(both.reshape(16, 4 * BLK, width), PLANE, 0, 0, tiled=True)
    hidden = jnp.sum(parts.astype(jnp.float32), axis=0).astype(jnp.bfloat16)
    output_rows = jnp.dot(hidden, weight, preferred_element_type=jnp.float32).astype(jnp.bfloat16)
    local_weight = lax.dot_general(
        hidden, cotangent, (((0,), (0,)), ((), ())), preferred_element_type=jnp.float32
    ) * jnp.float32(1.0 / node_total**0.5)

    back = grad_parts(where, meta, ids, tile_cols, tile_rows, tile_count, sent, grad_mine, grad_peer, tile_values)
    grad_total = lax.psum_scatter(back.reshape(8, 4 * BLK, width), "z", scatter_dimension=0)
    feature_grad = grad_total.astype(jnp.bfloat16)
    weight_grad = sum_everywhere(local_weight, c)
    return (output_rows, feature_grad, weight_grad)


def solution(mesh):
    grid = Mesh(mesh.devices.reshape(SIZES), ("y", "x", "z", "col"))
    every = ("y", "x", "z", "col")
    return jax.shard_map(
        local,
        mesh=grid,
        in_specs=(
            P(every, None),
            P(),
            P(every, None),
            P(every, None, None),
            P(every),
            P(every),
            P(every),
            P(every, None),
        ),
        out_specs=(P(every, None), P(every, None), P()),
        check_vma=False,
    )
```

time: 575 us -> 332 us (0.58)
  waiting for transfers between devices: 392 us -> 174 us
  Pallas kernels: 0 us -> 54 us
  local copies, waits for them, and re-layouts: 53.2 us -> 4.09 us
  other arithmetic: 54.5 us -> 17.9 us
  matrix products: 31.4 us -> 3.06 us
  blocking collectives: 2.98 us -> 21.3 us
  starting transfers between devices: 24.9 us -> 41.9 us
    all_to_all x2 -> x3, waiting for transfers between devices: 361 us -> 71.5 us  [the longest x1 60.1 us: local(): lax.all_to_all(both.reshape(16, 4 * BLK, width), PLANE, 0, 0, tiled=True)]
    all_gather x0 -> x2, waiting for transfers between devices: none -> 102 us  [the longest x1 61.6 us: local(): lax.all_gather(own_grad.reshape(4, BLK, width), PLANE, axis=0, tiled=True)]
    pallas_call x0 -> x3, Pallas kernels: none -> 54 us  [the longest x1 23 us: pack(): pl.pallas_call(pack_kernel, out_shape=jax.ShapeDtypeStruct((groups, slots...]
    scatter-add x3 -> x0, other arithmetic: 42.1 us -> none  [the longest x1 24.1 us: local(): jax.ops.segment_sum(remote_terms, send_blocks[0], num_segments=half_blocks)]
    dot_general x5 -> x0, matrix products: 29.2 us -> none  [the longest x1 12.8 us: local(): jnp.einsum('sji,sjf->sif', back_tiles, back_grads, preferred_element_type...]
    concatenate x1 -> x0, local copies, waits for them, and re-layouts: 29.1 us -> none  [in_one_piece(): both = jnp.concatenate(arrays, axis=along)]
    psum x1 -> x0, waiting for transfers between devices: 27 us -> none  [local(): weight_grad = lax.psum(local_weight, ('dom', 'col'))]
    all_to_all x0 -> x1, blocking collectives: none -> 21.3 us  [sum_everywhere(): rows = lax.all_to_all(half.reshape(128, 1, n), DOM, 0, 0, tiled=True)]
  transfers between devices with their start and end apart: 4 -> 10, of which waited for: 4 -> 6; matrix products, arithmetic and copies ran while one was open for 22% -> 6% of each run, Pallas kernels for 0% -> 16%
where the time goes in v1:
time: 332 us; the launch traced here: 331 us
  waiting for transfers between devices  174 us (52%)
  Pallas kernels  54 us (16%)
  starting transfers between devices  41.9 us (13%)
  blocking collectives  21.3 us (6%)
  other arithmetic  17.9 us (5%)
  between operations  14.6 us (4%)
  local copies, waits for them, and re-layouts  4.09 us (1%)
    all_gather x1, waiting for transfers between devices, local(): lax.all_gather(own_grad.reshape(4, BLK, width), PLANE, axis=0, tiled=True)  61.6 us
    all_to_all x1, waiting for transfers between devices, local(): lax.all_to_all(both.reshape(16, 4 * BLK, width), PLANE, 0, 0, tiled=True)  60.1 us
    all_gather x1, waiting for transfers between devices, local(): lax.all_gather(jnp.concatenate([features, ids_row], axis=0), 'z', axis=0)  40.2 us
    pallas_call x1, Pallas kernels, pack(): pl.pallas_call(pack_kernel, out_shape=jax.ShapeDtypeStruct((groups, slots...  23 us
    all_to_all x1, blocking collectives, sum_everywhere(): rows = lax.all_to_all(half.reshape(128, 1, n), DOM, 0, 0, tiled=True)  21.3 us
    all_to_all x1, starting transfers between devices, local(): lax.all_to_all(pack(tile_cols, tile_count, tile_values, meta_rows), PLANE...  17.3 us
    pallas_call x1, Pallas kernels, hidden_parts(): pl.pallas_call(hidden_kernel, out_shape=(jax.ShapeDtypeStruct((64, BLK, w...  16 us
    pallas_call x1, Pallas kernels, grad_parts(): pl.pallas_call(grad_kernel, out_shape=jax.ShapeDtypeStruct((32, BLK, widt...  15.1 us
  transfers between devices with their start and end apart: 10, of which 6 were waited for; matrix products, arithmetic and copies ran while one was open for 6% of the time, Pallas kernels for 16%

profile of v1, /device:TPU:1, one launch (start us, length us, event | category | flops | bytes accessed | tf_op | source)
XLA Modules:
  0.0 331.3 jit_solution(5296565261525152435)
XLA Ops:
  7.2 0.9 copy-done
  8.1 1.9 convolution_convert_fusion
  11.3 0.7 select_reduce_fusion
  12.9 23.0 %pack_tiles.1 = bf16[16,1040,128]{2,1,0:T(8,128)(2,1)} custom-call(s32[40]{0:T(128)} %cols.5, s32[1]{0:T(128)} %copy.24.count, bf16[40,128,128]{2,1,0:T(8,128)(2,1)} %tiles.5, bf16[16,16,128]{2,1,0:T(8,128)(2,1)} %pad.8.meta), custom_call_target="tpu_custom_call" | custom-call | tf_op jit(solution)/shard_map/pack_tiles/pallas_call | solution.py:53
  35.9 17.3 %all-to-all-start = ((bf16[16,1040,128]{2,1,0:T(8,128)(2,1)}), bf16[16,1040,128]{2,1,0:T(8,128)(2,1)}, u32[]{:S(2)}, u32[]{:S(2)}) async-start(bf16[16,1040,128]{2,1,0:T(8,128)(2,1)} %pack_tiles.1), calls=%async_computation | async-start | bytes 8519680 | tf_op jit(solution)/shard_map/all_to_all | solution.py:237
  54.0 61.6 %all-gather.4.cloned.1.call-done.grad_mine = bf16[64,128,256]{2,1,0:T(8,128)(2,1)} async-done(((bf16[4,128,256]{2,1,0:T(8,128)(2,1)}), bf16[64,128,256]{2,1,0:T(8,128)(2,1)}) %all-gather.4.cloned.1.call-update) | async-done | bytes 4194320 | tf_op jit(solution)/shard_map/all_gather | solution.py:227
  115.6 0.8 collective-permute-start.1
  117.0 40.2 %all-gather.6.cloned.1.call-done = bf16[4224,256]{1,0:T(8,128)(2,1)} async-done(((bf16[528,256]{1,0:T(8,128)(2,1)}), bf16[4224,256]{1,0:T(8,128)(2,1)}) %all-gather.6.cloned.1.call-update) | async-done | bytes 2162704 | tf_op jit(solution)/shard_map/all_gather | solution.py:223
  159.0 0.8 fusion.2
  160.4 16.0 %hidden_parts.1 = (f32[64,128,256]{2,1,0:T(8,128)}, bf16[64,128,256]{2,1,0:T(8,128)(2,1)}) custom-call(s32[3]{0:T(128)} %pad_add_fusion.where, s32[128]{0:T(128)} %reshape.72.meta, s32[128]{0:T(128)} %reshape.65.ids, s32[40]{0:T(128)} %cols.5, s32[40]{0:T(128)} %rows.3, s32[1]{0:T(128)} %copy.24.count, bf16[16,1040,128]{2,1,0:T(8,128)(2,1)} %all-to-all-done.sent, ...), custom_call_target="tpu_custom_call" | custom-call | tf_op jit(solution)/shard_map/hidden_parts/pallas_call | solution.py:121
  176.3 3.6 %collective-permute-start = (bf16[64,128,256]{2,1,0:T(8,128)(2,1)}, bf16[64,128,256]{2,1,0:T(8,128)(2,1)}, u32[]{:S(2)}, u32[]{:S(2)}) collective-permute-start(bf16[64,128,256]{2,1,0:T(8,128)(2,1)} %get-tuple-element.6), channel_id=1, source_target_pairs={{0,1},{1,0},{2,3},{3,2},{4,5},{5,4},{6,7},{7,6},{8,9},{9,8},{10,11... | collective-permute-start | bytes 12582920 | tf_op jit(solution)/shard_map/ppermute | solution.py:196
  179.9 15.1 %grad_parts.1 = f32[32,128,256]{2,1,0:T(8,128)} custom-call(s32[3]{0:T(128)} %pad_add_fusion.where, s32[128]{0:T(128)} %reshape.72.meta, s32[128]{0:T(128)} %reshape.65.ids, s32[40]{0:T(128)} %cols.5, s32[40]{0:T(128)} %rows.3, s32[1]{0:T(128)} %copy.24.count, bf16[16,1040,128]{2,1,0:T(8,128)(2,1)} %all-to-all-done.sent, ...), custom_call_target="tpu_custom_call" | custom-call | tf_op jit(solution)/shard_map/grad_parts/pallas_call | solution.py:185
  195.1 8.1 %add_convert_fusion = bf16[64,128,256]{2,1,0:T(8,128)(2,1)} fusion(f32[64,128,256]{2,1,0:T(8,128)} %get-tuple-element.5, bf16[64,128,256]{2,1,0:T(8,128)(2,1)} %collective-permute-done), kind=kLoop, calls=%fused_computation | loop fusion | flops 6291456 | bytes 16777216 | tf_op jit(solution)/shard_map/convert_element_type | solution.py:244
  203.2 8.6 %all-to-all-start.1 = ((bf16[16,512,256]{2,1,0:T(8,128)(2,1)}), bf16[16,512,256]{2,1,0:T(8,128)(2,1)}, u32[]{:S(2)}, u32[]{:S(2)}) async-start(bf16[16,512,256]{2,1,0:T(8,128)(2,1)} %bitcast.30), calls=%async_computation.1 | async-start | bytes 8388608 | tf_op jit(solution)/shard_map/all_to_all | solution.py:245
  211.8 60.1 %all-to-all-done.1 = bf16[16,512,256]{2,1,0:T(8,128)(2,1)} async-done(((bf16[16,512,256]{2,1,0:T(8,128)(2,1)}), bf16[16,512,256]{2,1,0:T(8,128)(2,1)}, u32[]{:S(2)}, u32[]{:S(2)}) %all-to-all-start.1) | async-done | bytes 4194336 | tf_op jit(solution)/shard_map/all_to_all | solution.py:245
  271.9 2.9 reduce_sum.31
  275.0 2.7 collective-permute-start.2
  277.7 1.0 collective-permute-done.2
  278.8 21.3 %all_to_all.20 = f32[128,1,256]{2,1,0:T(1,128)S(1)} all-to-all(f32[128,1,256]{2,1,0:T(1,128)S(1)} %reshape.70), channel_id=1, replica_groups=mesh['y'=4,'x'=4,'z'=8,'col'=2] {'y','x','z'}, dimensions={0} | all-to-all | bytes 262144 | tf_op jit(solution)/shard_map/all_to_all | solution.py:205
  301.1 6.2 %all-to-all-start.3 = ((f32[128,1,256]{2,1,0:T(1,128)}), f32[128,1,256]{2,1,0:T(1,128)S(1)}, u32[]{:S(2)}, u32[]{:S(2)}) async-start(f32[128,1,256]{2,1,0:T(1,128)} %broadcast_in_dim.24), calls=%async_computation.4 | async-start | bytes 262144 | tf_op jit(solution)/shard_map/all_to_all | solution.py:207
  307.2 11.4 %all-to-all-done.3 = f32[128,1,256]{2,1,0:T(1,128)S(1)} async-done(((f32[128,1,256]{2,1,0:T(1,128)}), f32[128,1,256]{2,1,0:T(1,128)S(1)}, u32[]{:S(2)}, u32[]{:S(2)}) %all-to-all-start.3) | async-done | bytes 131104 | tf_op jit(solution)/shard_map/all_to_all | solution.py:207
  318.7 2.6 collective-permute-start.3
  321.3 0.9 convolution_convert_fusion.1
  323.0 1.8 convert_bitcast_fusion
  (41 shorter events, 7.3 us)
Async XLA Ops:
  7.2 1.0 copy-start
  7.2 108.5 %all-gather.4.cloned.1.call-start = ((), (), s32[]{:S(2)}) async-start(), calls=%async_computation.5 | async-start | bytes 4456448 | tf_op jit(solution)/shard_map/all_gather | solution.py:227
  35.9 17.3 %copy-start.3 = (s32[1,128]{1,0:T(1,128)S(1)}, s32[1,128]{1,0:T(1,128)}, u32[]{:S(2)}) copy-start(s32[1,128]{1,0:T(1,128)} %param.15) | copy-start | bytes 1540
  35.9 17.3 %copy-start.2 = (bf16[512,256]{1,0:T(8,128)(2,1)S(1)}, bf16[512,256]{1,0:T(8,128)(2,1)}, u32[]{:S(2)}) copy-start(bf16[512,256]{1,0:T(8,128)(2,1)} %param.8) | copy-start | bytes 786436
  35.9 123.1 %all-to-all-start = ((bf16[16,1040,128]{2,1,0:T(8,128)(2,1)}), bf16[16,1040,128]{2,1,0:T(8,128)(2,1)}, u32[]{:S(2)}, u32[]{:S(2)}) async-start(bf16[16,1040,128]{2,1,0:T(8,128)(2,1)} %pack_tiles.1), calls=%async_computation | async-start | bytes 8519680 | tf_op jit(solution)/shard_map/all_to_all | solution.py:237
  53.1 104.1 %all-gather.6.cloned.1.call-start = ((), (), s32[]{:S(2)}) async-start(), calls=%async_computation.7 | async-start | bytes 2433024 | tf_op jit(solution)/shard_map/all_gather | solution.py:223
  54.0 269.0 %reduce-scatter.2.cloned.1.call-start = ((), (), s32[]{:S(2)}) async-start(), calls=%async_computation.6 | async-start | bytes 4718592 | tf_op jit(solution)/shard_map/reduce_scatter | solution.py:253
  115.6 64.3 %collective-permute-start.1 = (bf16[64,128,256]{2,1,0:T(8,128)(2,1)}, bf16[64,128,256]{2,1,0:T(8,128)(2,1)}, u32[]{:S(2)}, u32[]{:S(2)}) collective-permute-start(bf16[64,128,256]{2,1,0:T(8,128)(2,1)} %all-gather.4.cloned.1.call-done.grad_mine), channel_id=1, source_target_pairs={{0,1},{1,0},{2,3},{3,2},{4,5},{5,4},{6,7},{7,6},{8,9},{9,8},{10,11... | collective-permute-start | bytes 12582920 | tf_op jit(solution)/shard_map/ppermute | solution.py:196
  176.3 18.7 %collective-permute-start = (bf16[64,128,256]{2,1,0:T(8,128)(2,1)}, bf16[64,128,256]{2,1,0:T(8,128)(2,1)}, u32[]{:S(2)}, u32[]{:S(2)}) collective-permute-start(bf16[64,128,256]{2,1,0:T(8,128)(2,1)} %get-tuple-element.6), channel_id=1, source_target_pairs={{0,1},{1,0},{2,3},{3,2},{4,5},{5,4},{6,7},{7,6},{8,9},{9,8},{10,11... | collective-permute-start | bytes 12582920 | tf_op jit(solution)/shard_map/ppermute | solution.py:196
  203.2 68.7 %all-to-all-start.1 = ((bf16[16,512,256]{2,1,0:T(8,128)(2,1)}), bf16[16,512,256]{2,1,0:T(8,128)(2,1)}, u32[]{:S(2)}, u32[]{:S(2)}) async-start(bf16[16,512,256]{2,1,0:T(8,128)(2,1)} %bitcast.30), calls=%async_computation.1 | async-start | bytes 8388608 | tf_op jit(solution)/shard_map/all_to_all | solution.py:245
  211.8 109.5 %copy-start.1 = (bf16[256,256]{1,0:T(8,128)(2,1)S(1)}, bf16[256,256]{1,0:T(8,128)(2,1)}, u32[]{:S(2)}) copy-start(bf16[256,256]{1,0:T(8,128)(2,1)} %param.9) | copy-start | bytes 393220
  275.0 3.7 %collective-permute-start.2 = (f32[128,256]{1,0:T(8,128)S(1)}, f32[128,256]{1,0:T(8,128)S(1)}, u32[]{:S(2)}, u32[]{:S(2)}) collective-permute-start(f32[128,256]{1,0:T(8,128)S(1)} %dynamic-slice_bitcast_fusion), channel_id=1, source_target_pairs={{0,1},{1,0},{2,3},{3,2},{4,5},{5,4},{6,7},{7,6},{8,9},{9,8},{10,11... | collective-permute-start | bytes 393224 | tf_op jit(solution)/shard_map/ppermute | solution.py:196
  301.1 17.6 %all-to-all-start.3 = ((f32[128,1,256]{2,1,0:T(1,128)}), f32[128,1,256]{2,1,0:T(1,128)S(1)}, u32[]{:S(2)}, u32[]{:S(2)}) async-start(f32[128,1,256]{2,1,0:T(1,128)} %broadcast_in_dim.24), calls=%async_computation.4 | async-start | bytes 262144 | tf_op jit(solution)/shard_map/all_to_all | solution.py:207
  318.7 3.6 %collective-permute-start.3 = (f32[128,256]{1,0:T(8,128)S(1)}, f32[128,256]{1,0:T(8,128)S(1)}, u32[]{:S(2)}, u32[]{:S(2)}) collective-permute-start(f32[128,256]{1,0:T(8,128)S(1)} %bitcast.36), channel_id=1, source_target_pairs={{0,1},{1,0},{2,3},{3,2},{4,5},{5,4},{6,7},{7,6},{8,9},{9,8},{10,11... | collective-permute-start | bytes 393224 | tf_op jit(solution)/shard_map/ppermute | solution.py:196
Sparse Core Ops, SparseCore 0:
  11.0 104.5 all-gather.3
  117.4 39.7 all-gather.5
  195.2 55.2 reduce-scatter.1

commit v2 on v1

v2 whole, which is shorter than its diff:
```python
import functools

import jax
import jax.numpy as jnp
from jax import lax
from jax.experimental import pallas as pl
from jax.experimental.pallas import tpu as pltpu
from jax.sharding import Mesh
from jax.sharding import PartitionSpec as P

PLANE = ("y", "x")
DOM = ("y", "x", "z")
SIZES = (4, 4, 8, 2)
BLK = 128
META = 16


def pack_kernel(cols, rows, count, tiles, out):
    slots = out.shape[1] // BLK
    here = pl.ds(slots * BLK, META)
    lane = lax.broadcasted_iota(jnp.int32, (META, BLK), 1)
    line = lax.broadcasted_iota(jnp.int32, (META, BLK), 0)

    def clear(d, carry):
        out[d, here, :] = jnp.zeros((META, BLK), out.dtype)
        return carry

    lax.fori_loop(0, out.shape[0], clear, 0)

    def one(t, carry):
        @pl.when(cols[t] >= 4)
        def _():
            slot = jnp.maximum(cols[t] - 4, 0)
            d, z = lax.div(slot, slots), lax.rem(slot, slots)
            out[d, rows_at(z), :] = tiles[t]
            mark = jnp.where((lane == z) & (line == 0), rows[t] + 1, 0)
            out[d, here, :] = (out[d, here, :].astype(jnp.float32) + mark.astype(jnp.float32)).astype(out.dtype)

        return carry

    lax.fori_loop(0, count[0], one, 0)


def pack(cols, rows, count, tiles):
    groups, slots = 16, 8
    smem = pl.BlockSpec(memory_space=pltpu.SMEM)
    vmem = pl.BlockSpec(memory_space=pltpu.VMEM)
    return pl.pallas_call(
        pack_kernel,
        out_shape=jax.ShapeDtypeStruct((groups, slots * BLK + META, BLK), tiles.dtype),
        in_specs=[smem, smem, smem, vmem],
        out_specs=vmem,
        compiler_params=pltpu.CompilerParams(vmem_limit_bytes=12 * 2**20),
        cost_estimate=cost(3),
        name="pack_tiles",
    )(cols, rows, count, tiles)


def cost(us):
    return pl.CostEstimate(flops=us * 10**6, bytes_accessed=us * 10**4, transcendentals=0)


def rows_at(k):
    return pl.ds(pl.multiple_of(k * BLK, BLK), BLK)


def hidden_kernel(first, where, meta, ids, cols, rows, count, sent, feats, tiles, *rest):
    out, total = rest[-2:]
    c, z_me, r_me = where[0], where[1], where[2]
    half = 1 - c if first else c

    def begin(i, carry):
        total[i] = jnp.zeros(total.shape[1:], total.dtype) if first else rest[0][i].astype(total.dtype)
        return carry

    lax.fori_loop(0, total.shape[0], begin, 0)

    def add(tile, block, r, row):
        at = r * 4 + lax.rem(row, 4)
        total[at] = total[at] + jnp.dot(tile, block, preferred_element_type=jnp.float32)

    def remote(i, carry):
        r, z = lax.div(i, 8), lax.rem(i, 8)
        row = meta[i] - 1

        @pl.when((meta[i] > 0) & (lax.div(row, 4) == half))
        def _():
            add(sent[r, rows_at(z), :], feats[z, rows_at(ids[z * 16 + r]), :], r, row)

        return carry

    lax.fori_loop(0, 128, remote, 0)

    def own(t, carry):
        @pl.when((cols[t] < 4) & (lax.div(rows[t], 4) == half))
        def _():
            add(tiles[t], feats[z_me, rows_at(jnp.minimum(cols[t], 3)), :], r_me, rows[t])

        return carry

    lax.fori_loop(0, count[0], own, 0)

    def cast(i, carry):
        out[i] = total[i].astype(out.dtype)
        return carry

    lax.fori_loop(0, total.shape[0], cast, 0)


def hidden_parts(where, meta, ids, cols, rows, count, sent, feats, tiles, *arrived):
    smem = pl.BlockSpec(memory_space=pltpu.SMEM)
    vmem = pl.BlockSpec(memory_space=pltpu.VMEM)
    width = feats.shape[2]
    return pl.pallas_call(
        functools.partial(hidden_kernel, not arrived),
        out_shape=jax.ShapeDtypeStruct((64, BLK, width), jnp.bfloat16),
        in_specs=[smem] * 6 + [vmem] * (3 + len(arrived)),
        out_specs=vmem,
        scratch_shapes=[pltpu.VMEM((64, BLK, width), jnp.float32)],
        compiler_params=pltpu.CompilerParams(vmem_limit_bytes=28 * 2**20),
        cost_estimate=cost(10),
        name="hidden_sums" if arrived else "hidden_for_other_core",
    )(where, meta, ids, cols, rows, count, sent, feats, tiles, *arrived)


def add_grads(half, where, meta, ids, cols, rows, count, sent, grads, tiles, total):
    z_me, r_me = where[1], where[2]

    def add(at, tile, r, row):
        term = lax.dot_general(
            tile, grads[r * 4 + lax.rem(row, 4)], (((0,), (0,)), ((), ())), preferred_element_type=jnp.float32
        )
        total[at] = total[at] + term

    def remote(i, carry):
        r, z = lax.div(i, 8), lax.rem(i, 8)
        row = meta[i] - 1

        @pl.when((meta[i] > 0) & (lax.div(row, 4) == half))
        def _():
            step = jnp.bitwise_and(z - z_me + 8, 7)
            add(step * 4 + ids[z * 16 + r], sent[r, rows_at(z), :], r, row)

        return carry

    lax.fori_loop(0, 128, remote, 0)

    def own(t, carry):
        @pl.when((cols[t] < 4) & (lax.div(rows[t], 4) == half))
        def _():
            add(jnp.minimum(cols[t], 3), tiles[t], r_me, rows[t])

        return carry

    lax.fori_loop(0, count[0], own, 0)


def grad_kernel(where, meta, ids, cols, rows, count, sent, mine, peer, tiles, *outs):
    total = outs[-1]

    def begin(i, carry):
        total[i] = jnp.zeros(total.shape[1:], total.dtype)
        return carry

    lax.fori_loop(0, total.shape[0], begin, 0)
    add_grads(where[0], where, meta, ids, cols, rows, count, sent, mine, tiles, total)
    add_grads(1 - where[0], where, meta, ids, cols, rows, count, sent, peer, tiles, total)
    for k in range(4):
        outs[0][rows_at(k), :] = total[k]
    for step in range(1, 8):
        for k in range(4):
            outs[step][rows_at(k), :] = total[step * 4 + k].astype(outs[step].dtype)


def grad_parts(where, meta, ids, cols, rows, count, sent, mine, peer, tiles):
    smem = pl.BlockSpec(memory_space=pltpu.SMEM)
    vmem = pl.BlockSpec(memory_space=pltpu.VMEM)
    width = mine.shape[2]
    return pl.pallas_call(
        grad_kernel,
        out_shape=[jax.ShapeDtypeStruct((4 * BLK, width), jnp.float32)]
        + [jax.ShapeDtypeStruct((4 * BLK, width), jnp.bfloat16)] * 7,
        in_specs=[smem] * 6 + [vmem] * 4,
        out_specs=[vmem] * 8,
        scratch_shapes=[pltpu.VMEM((32, BLK, width), jnp.float32)],
        compiler_params=pltpu.CompilerParams(vmem_limit_bytes=28 * 2**20),
        cost_estimate=cost(8),
        name="grad_sums",
    )(where, meta, ids, cols, rows, count, sent, mine, peer, tiles)


def term_kernel(scale, parts, cots, term):
    term[...] = jnp.zeros(term.shape, term.dtype)

    def product(i, carry):
        term[...] += lax.dot_general(
            parts[i], cots[i], (((0,), (0,)), ((), ())), preferred_element_type=jnp.float32
        )
        return carry

    lax.fori_loop(0, parts.shape[0], product, 0)
    term[...] = term[...] * scale


def weight_term(parts, cots, scale):
    vmem = pl.BlockSpec(memory_space=pltpu.VMEM)
    width = parts.shape[2]
    return pl.pallas_call(
        functools.partial(term_kernel, scale),
        out_shape=jax.ShapeDtypeStruct((width, width), jnp.float32),
        in_specs=[vmem] * 2,
        out_specs=vmem,
        compiler_params=pltpu.CompilerParams(vmem_limit_bytes=12 * 2**20),
        cost_estimate=cost(8),
        name="weight_term",
    )(parts, cots)


def output_kernel(parts, weight, *rest):
    output = rest[-1]
    total = parts[0].astype(jnp.float32)
    for i in range(1, parts.shape[0]):
        total = total + parts[i].astype(jnp.float32)
    hidden = total.astype(jnp.bfloat16)
    output[...] = jnp.dot(hidden, weight[...], preferred_element_type=jnp.float32).astype(output.dtype)


def output_from(parts, weight, *after):
    vmem = pl.BlockSpec(memory_space=pltpu.VMEM)
    return pl.pallas_call(
        output_kernel,
        out_shape=jax.ShapeDtypeStruct(parts.shape[1:], jnp.bfloat16),
        in_specs=[vmem] * 2 + [pl.BlockSpec(memory_space=pl.ANY)] * len(after),
        out_specs=vmem,
        compiler_params=pltpu.CompilerParams(vmem_limit_bytes=16 * 2**20),
        cost_estimate=cost(4),
        name="output_rows",
    )(parts, weight, *after)


def feature_kernel(own, *rest):
    weight, out = rest[-2:]
    total = own[...]
    for part in rest[:-2]:
        total = total + part[...].astype(jnp.float32)
    high = total.astype(jnp.bfloat16)
    low = (total - high.astype(jnp.float32)).astype(jnp.bfloat16)
    dims = (((1,), (1,)), ((), ()))
    grad = lax.dot_general(high, weight[...], dims, preferred_element_type=jnp.float32)
    grad = grad + lax.dot_general(low, weight[...], dims, preferred_element_type=jnp.float32)
    out[...] = grad.astype(out.dtype)


def feature_from(own, parts, weight):
    vmem = pl.BlockSpec(memory_space=pltpu.VMEM)
    return pl.pallas_call(
        feature_kernel,
        out_shape=jax.ShapeDtypeStruct(own.shape, jnp.bfloat16),
        in_specs=[vmem] * (2 + len(parts)),
        out_specs=vmem,
        compiler_params=pltpu.CompilerParams(vmem_limit_bytes=16 * 2**20),
        cost_estimate=cost(4),
        name="feature_gradient",
    )(own, *parts, weight)


def later_kernel(array, after, out):
    del after
    out[...] = array[...]


def later(array, after):
    vmem = pl.BlockSpec(memory_space=pltpu.VMEM)
    return pl.pallas_call(
        later_kernel,
        out_shape=jax.ShapeDtypeStruct(array.shape, array.dtype),
        in_specs=[vmem, pl.BlockSpec(memory_space=pl.ANY)],
        out_specs=vmem,
        compiler_params=pltpu.CompilerParams(vmem_limit_bytes=4 * 2**20),
        cost_estimate=cost(1),
        name="in_order",
    )(array, after)


def same_later_kernel(array, after, out):
    del array, after, out


def same_later(array, after):
    hbm = pl.BlockSpec(memory_space=pl.ANY)
    return pl.pallas_call(
        same_later_kernel,
        out_shape=jax.ShapeDtypeStruct(array.shape, array.dtype),
        in_specs=[hbm, hbm],
        out_specs=hbm,
        input_output_aliases={0: 0},
        cost_estimate=cost(1),
        name="in_order_in_place",
    )(array, after)


def swap_cores(a):
    return lax.ppermute(a, "col", [(0, 1), (1, 0)])


def sum_four(a, axis):
    me = lax.axis_index(axis)
    from_step = [a] + [lax.ppermute(a, axis, [(i, (i + step) % 4) for i in range(4)]) for step in (1, 2, 3)]
    total = None
    for source in range(4):
        step = jnp.bitwise_and(me - source + 4, 3)
        low = jnp.where(step == 0, from_step[0], from_step[1])
        high = jnp.where(step == 2, from_step[2], from_step[3])
        part = jnp.where(step < 2, low, high)
        total = part if total is None else total + part
    return total


def sum_everywhere(term, c, after):
    halves = term.reshape(2, 128, term.shape[1])
    keep = lax.dynamic_index_in_dim(halves, c, 0, keepdims=False)
    give = lax.dynamic_index_in_dim(halves, 1 - c, 0, keepdims=False)
    half = keep + swap_cores(give)
    for step in (1, 2, 4):
        half = half + lax.ppermute(half, "z", [(i, i ^ step) for i in range(8)])
    half = sum_four(sum_four(later(half, after), "x"), "y")
    other = swap_cores(half)
    first = jnp.where(c == 0, half, other)
    second = jnp.where(c == 0, other, half)
    return jnp.concatenate([first, second], axis=0)


def local(features, weight, cotangent, tile_values, tile_rows, tile_cols, tile_count, send_blocks):
    width = features.shape[1]
    node_total = features.shape[0] * lax.axis_size("col") * lax.axis_size(DOM)
    c = lax.axis_index("col")
    z_me = lax.axis_index("z")
    r_me = lax.axis_index(PLANE)
    where = jnp.stack([c, z_me, r_me]).astype(jnp.int32)

    ids_row = jnp.pad(send_blocks.astype(jnp.bfloat16), ((0, META - 1), (0, width - send_blocks.shape[1])))
    column = lax.all_gather(jnp.concatenate([features, ids_row], axis=0), "z", axis=0)
    packed = pack(tile_cols, tile_rows, tile_count, tile_values)
    sent = lax.all_to_all(packed, PLANE, 0, 0, tiled=True)
    cot_mine = lax.all_gather(later(cotangent, sent).reshape(4, BLK, width), PLANE, axis=0, tiled=True)

    meta = sent[:, 8 * BLK, :8].astype(jnp.int32).reshape(128)
    ids = column[:, 4 * BLK, :128].astype(jnp.int32).reshape(8, 16, 8)
    ids = lax.dynamic_index_in_dim(ids, z_me, 2, keepdims=False).reshape(128)

    operands = (where, meta, ids, tile_cols, tile_rows, tile_count, sent, column, tile_values)
    both = hidden_parts(*operands, swap_cores(hidden_parts(*operands)))
    parts = lax.all_to_all(both.reshape(16, 4 * BLK, width), PLANE, 0, 0, tiled=True)
    cot_mine = same_later(cot_mine, both)
    own, *away = grad_parts(*operands[:7], cot_mine, swap_cores(cot_mine), tile_values)
    by_partition = (16, 4 * BLK, width)
    term = weight_term(both.reshape(by_partition), cot_mine.reshape(by_partition), float(1.0 / node_total**0.5))
    arrived = [
        lax.ppermute(part, "z", [(z, (z + step) % 8) for z in range(8)])
        for step, part in sorted(enumerate(away, 1), key=lambda e: -min(e[0], 8 - e[0]))
    ]
    feature_grad = feature_from(own, arrived, weight)
    weight_grad = sum_everywhere(term, c, own)
    output_rows = output_from(parts, weight, feature_grad, weight_grad)
    return (output_rows, feature_grad, weight_grad)


def solution(mesh):
    grid = Mesh(mesh.devices.reshape(SIZES), ("y", "x", "z", "col"))
    every = ("y", "x", "z", "col")
    return jax.shard_map(
        local,
        mesh=grid,
        in_specs=(
            P(every, None),
            P(),
            P(every, None),
            P(every, None, None),
            P(every),
            P(every),
            P(every),
            P(every, None),
        ),
        out_specs=(P(every, None), P(every, None), P()),
        check_vma=False,
    )
```

time: 332 us -> 275 us (0.83)
  waiting for transfers between devices: 174 us -> 134 us
  blocking collectives: 21.3 us -> 0 us
  starting transfers between devices: 41.9 us -> 60.9 us
  other arithmetic: 17.9 us -> 3.6 us
  local copies, waits for them, and re-layouts: 4.09 us -> 17.8 us
  Pallas kernels: 54 us -> 43.2 us
    all_to_all x1, waiting for transfers between devices: 60.1 us -> 0.01 us  [local(): lax.all_to_all(both.reshape(16, 4 * BLK, width), PLANE, 0, 0, tiled=True)]
    all_to_all x2 -> x1, waiting for transfers between devices: 11.4 us -> 62.1 us  [local(): sent = lax.all_to_all(packed, PLANE, 0, 0, tiled=True)]
    all_gather x1, waiting for transfers between devices: 40.2 us -> 0.01 us  [local(): lax.all_gather(jnp.concatenate([features, ids_row], axis=0), 'z', axis=0)]
    ppermute x0 -> x16, starting transfers between devices: none -> 37.6 us  [the longest x7 18.1 us: local(): lax.ppermute(part, 'z', [(z, (z + step) % 8) for z in range(8)])]
    ppermute x0 -> x16, waiting for transfers between devices: none -> 35.5 us  [the longest x7 18.7 us: local(): lax.ppermute(part, 'z', [(z, (z + step) % 8) for z in range(8)])]
    all_gather x1, waiting for transfers between devices: 61.6 us -> 28.1 us  [local(): lax.all_gather(later(cotangent, sent).reshape(4, BLK, width), PLANE, axis...]
    pallas_call x1, Pallas kernels: 23 us -> 1.08 us  [pack(): pl.pallas_call(pack_kernel, out_shape=jax.ShapeDtypeStruct((groups, slots...]
    all_to_all x1 -> x0, blocking collectives: 21.3 us -> none  [sum_everywhere(): rows = lax.all_to_all(half.reshape(128, 1, n), DOM, 0, 0, tiled=True)]
  transfers between devices with their start and end apart: 10 -> 24, of which waited for: 6 -> 13; matrix products, arithmetic and copies ran while one was open for 6% -> 2% of each run, Pallas kernels for 16% -> 14%
where the time goes in v2:
time: 275 us; the launch traced here: 274 us
  waiting for transfers between devices  134 us (49%)
  starting transfers between devices  60.9 us (22%)
  Pallas kernels  43.2 us (16%)
  local copies, waits for them, and re-layouts  17.8 us (6%)
  between operations  15 us (5%)
  other arithmetic  3.6 us (1%)
    all_to_all x1, waiting for transfers between devices, local(): sent = lax.all_to_all(packed, PLANE, 0, 0, tiled=True)  62.1 us
    all_gather x1, waiting for transfers between devices, local(): lax.all_gather(later(cotangent, sent).reshape(4, BLK, width), PLANE, axis...  28.1 us
    ppermute x7, waiting for transfers between devices, local(): lax.ppermute(part, 'z', [(z, (z + step) % 8) for z in range(8)])  18.7 us
    ppermute x7, starting transfers between devices, local(): lax.ppermute(part, 'z', [(z, (z + step) % 8) for z in range(8)])  18.1 us
    unnamed x44, local copies, waits for them, and re-layouts  17.2 us
    pallas_call x2, Pallas kernels, hidden_parts(): pl.pallas_call(functools.partial(hidden_kernel, not arrived), out_shape=j...  16.8 us
    pallas_call x1, Pallas kernels, grad_parts(): pl.pallas_call(grad_kernel, out_shape=[jax.ShapeDtypeStruct((4 * BLK, wid...  15.5 us
    ppermute x3, waiting for transfers between devices, sum_everywhere(): half = half + lax.ppermute(half, 'z', [(i, i ^ step) for i in range(8)])  12.9 us
  transfers between devices with their start and end apart: 24, of which 13 were waited for; matrix products, arithmetic and copies ran while one was open for 2% of the time, Pallas kernels for 14%

profile of v2, /device:TPU:1, one launch (start us, length us, event | category | flops | bytes accessed | tf_op | source)
XLA Modules:
  0.0 274.1 jit_solution(8196910525791913113)
XLA Ops:
  13.6 7.8 %all-to-all-start = ((bf16[16,1040,128]{2,1,0:T(8,128)(2,1)}), bf16[16,1040,128]{2,1,0:T(8,128)(2,1)}, u32[]{:S(2)}, u32[]{:S(2)}) async-start(bf16[16,1040,128]{2,1,0:T(8,128)(2,1)} %copy-done.6), calls=%async_computation | async-start | bytes 8519680 | tf_op jit(solution)/shard_map/all_to_all | solution.py:344
  22.3 62.1 %all-to-all-done.sent.after = bf16[16,1040,128]{2,1,0:T(8,128)(2,1)} async-done(((bf16[16,1040,128]{2,1,0:T(8,128)(2,1)}), bf16[16,1040,128]{2,1,0:T(8,128)(2,1)}, u32[]{:S(2)}, u32[]{:S(2)}) %all-to-all-start) | async-done | bytes 4259872 | tf_op jit(solution)/shard_map/all_to_all | solution.py:344
  89.0 8.9 %hidden_for_other_core.1 = bf16[64,128,256]{2,1,0:T(8,128)(2,1)S(1)} custom-call(s32[3]{0:T(128)S(1)} %pad_add_fusion.where, s32[128]{0:T(128)S(1)} %reshape.36.meta, s32[128]{0:T(128)S(1)} %reshape.31.ids, s32[40]{0:T(128)S(1)} %copy-done.14, s32[40]{0:T(128)S(1)} %copy-done.16, s32[1]{0:T(128)S(6)} %copy.14.count, ...), custom_call_target="tpu_custom_call" | custom-call | flops 10000000 | bytes 100000 | tf_op jit(solution)/shard_map/hidden_for_other_core/pallas_call | solution.py:114
  99.3 6.8 %collective-permute-done.rest_0_ = bf16[64,128,256]{2,1,0:T(8,128)(2,1)S(1)} collective-permute-done((bf16[64,128,256]{2,1,0:T(8,128)(2,1)S(1)}, bf16[64,128,256]{2,1,0:T(8,128)(2,1)S(1)}, u32[]{:S(2)}, u32[]{:S(2)}) %collective-permute-start) | collective-permute-done | bytes 4194336 | tf_op jit(solution)/shard_map/ppermute | solution.py:303
  106.0 7.9 %hidden_sums.1.after = bf16[64,128,256]{2,1,0:T(8,128)(2,1)S(1)} custom-call(s32[3]{0:T(128)S(1)} %pad_add_fusion.where, s32[128]{0:T(128)S(1)} %reshape.36.meta, s32[128]{0:T(128)S(1)} %reshape.31.ids, s32[40]{0:T(128)S(1)} %copy-done.14, s32[40]{0:T(128)S(1)} %copy-done.16, s32[1]{0:T(128)S(6)} %copy.14.count, ...), custom_call_target="tpu_custom_call" | custom-call | flops 10000000 | bytes 100000 | tf_op jit(solution)/shard_map/hidden_sums/pallas_call | solution.py:114
  115.9 28.1 %all-gather.4.cloned.1.call-done.array = bf16[64,128,256]{2,1,0:T(8,128)(2,1)} async-done(((bf16[4,128,256]{2,1,0:T(8,128)(2,1)}), bf16[64,128,256]{2,1,0:T(8,128)(2,1)}) %all-gather.4.cloned.1.call-update) | async-done | bytes 4194320 | tf_op jit(solution)/shard_map/all_gather | solution.py:345
  144.7 5.0 %all-to-all-start.1 = ((bf16[16,512,256]{2,1,0:T(8,128)(2,1)}), bf16[16,512,256]{2,1,0:T(8,128)(2,1)}, u32[]{:S(2)}, u32[]{:S(2)}) async-start(bf16[16,512,256]{2,1,0:T(8,128)(2,1)} %bitcast.12), calls=%async_computation.1 | async-start | bytes 8388608 | tf_op jit(solution)/shard_map/all_to_all | solution.py:353
  154.2 4.4 %weight_term.1 = f32[256,256]{1,0:T(8,128)S(1)} custom-call(bf16[16,512,256]{2,1,0:T(8,128)(2,1)S(1)} %bitcast.13, bf16[16,512,256]{2,1,0:T(8,128)(2,1)S(1)} %bitcast.14), custom_call_target="tpu_custom_call" | custom-call | flops 8000000 | bytes 80000 | tf_op jit(solution)/shard_map/weight_term/pallas_call | solution.py:208
  161.4 3.6 %collective-permute-done.10 = f32[128,256]{1,0:T(8,128)S(1)} collective-permute-done((f32[128,256]{1,0:T(8,128)S(1)}, f32[128,256]{1,0:T(8,128)S(1)}, u32[]{:S(2)}, u32[]{:S(2)}) %collective-permute-start.10) | collective-permute-done | bytes 131104 | tf_op jit(solution)/shard_map/ppermute | solution.py:325
  167.4 5.9 %collective-permute-done.11 = f32[128,256]{1,0:T(8,128)S(1)} collective-permute-done((f32[128,256]{1,0:T(8,128)S(1)}, f32[128,256]{1,0:T(8,128)S(1)}, u32[]{:S(2)}, u32[]{:S(2)}) %collective-permute-start.11) | collective-permute-done | bytes 131104 | tf_op jit(solution)/shard_map/ppermute | solution.py:325
  173.4 6.5 %collective-permute-start.12 = (f32[128,256]{1,0:T(8,128)S(1)}, f32[128,256]{1,0:T(8,128)S(1)}, u32[]{:S(2)}, u32[]{:S(2)}) collective-permute-start(f32[128,256]{1,0:T(8,128)S(1)} %add.97), channel_id=1, source_target_pairs={{0,8},{2,10},{4,12},{6,14},{8,0},{10,2},{12,4},{14,6},{1,9},{3,11}... | collective-permute-start | bytes 393224 | tf_op jit(solution)/shard_map/ppermute | solution.py:325
  179.9 3.3 %collective-permute-done.12 = f32[128,256]{1,0:T(8,128)S(1)} collective-permute-done((f32[128,256]{1,0:T(8,128)S(1)}, f32[128,256]{1,0:T(8,128)S(1)}, u32[]{:S(2)}, u32[]{:S(2)}) %collective-permute-start.12) | collective-permute-done | bytes 131104 | tf_op jit(solution)/shard_map/ppermute | solution.py:325
  185.4 15.5 %grad_sums.1 = (f32[512,256]{1,0:T(8,128)S(1)}, bf16[512,256]{1,0:T(8,128)(2,1)S(1)}, bf16[512,256]{1,0:T(8,128)(2,1)}, bf16[512,256]{1,0:T(8,128)(2,1)S(1)}, bf...) custom-call(s32[3]{0:T(128)S(1)} %pad_add_fusion.where, ...), custom_call_target="tpu_custom_call" | custom-call | flops 8000000 | bytes 80000 | tf_op jit(solution)/shard_map/grad_sums/pallas_call | solution.py:179
  201.3 4.3 %collective-permute-start.14 = (f32[128,256]{1,0:T(8,128)S(1)}, f32[128,256]{1,0:T(8,128)S(1)}, u32[]{:S(2)}, u32[]{:S(2)}) collective-permute-start(f32[128,256]{1,0:T(8,128)S(1)} %in_order.3), channel_id=1, source_target_pairs={{0,32},{16,48},{32,0},{48,16},{1,33},{17,49},{33,1},{49,17},{2,34}... | collective-permute-start | bytes 393224 | tf_op jit(solution)/shard_map/ppermute | solution.py:308
  205.6 5.0 %collective-permute-start.2 = (bf16[512,256]{1,0:T(8,128)(2,1)S(1)}, bf16[512,256]{1,0:T(8,128)(2,1)S(1)}, u32[]{:S(2)}, u32[]{:S(2)}) collective-permute-start(bf16[512,256]{1,0:T(8,128)(2,1)S(1)} %get-tuple-element.12), channel_id=1, source_target_pairs={{0,8},{2,10},{4,12},{6,14},{8,0},{10,2},{12,4},{14,6},{1,9},{3,11}... | collective-permute-start | bytes 786440 | tf_op jit(solution)/shard_map/ppermute | solution.py:359
  210.5 4.5 %collective-permute-start.3 = (bf16[512,256]{1,0:T(8,128)(2,1)S(1)}, bf16[512,256]{1,0:T(8,128)(2,1)S(1)}, u32[]{:S(2)}, u32[]{:S(2)}) collective-permute-start(bf16[512,256]{1,0:T(8,128)(2,1)S(1)} %get-tuple-element.13), channel_id=1, source_target_pairs={{0,6},{2,8},{4,10},{6,12},{8,14},{10,0},{12,2},{14,4},{1,7},{3,9},... | collective-permute-start | bytes 786440 | tf_op jit(solution)/shard_map/ppermute | solution.py:359
  215.0 3.1 %collective-permute-done.14 = f32[128,256]{1,0:T(8,128)S(1)} collective-permute-done((f32[128,256]{1,0:T(8,128)S(1)}, f32[128,256]{1,0:T(8,128)S(1)}, u32[]{:S(2)}, u32[]{:S(2)}) %collective-permute-start.14) | collective-permute-done | bytes 131104 | tf_op jit(solution)/shard_map/ppermute | solution.py:308
  218.3 2.6 collective-permute-start.17
  224.3 4.3 %collective-permute-start.4 = (bf16[512,256]{1,0:T(8,128)(2,1)}, bf16[512,256]{1,0:T(8,128)(2,1)S(1)}, u32[]{:S(2)}, u32[]{:S(2)}) collective-permute-start(bf16[512,256]{1,0:T(8,128)(2,1)} %get-tuple-element.14), channel_id=1, source_target_pairs={{0,10},{2,12},{4,14},{6,0},{8,2},{10,4},{12,6},{14,8},{1,11},{3,13... | collective-permute-start | bytes 786440 | tf_op jit(solution)/shard_map/ppermute | solution.py:359
  230.1 2.8 %collective-permute-start.6 = (bf16[512,256]{1,0:T(8,128)(2,1)S(1)}, bf16[512,256]{1,0:T(8,128)(2,1)S(1)}, u32[]{:S(2)}, u32[]{:S(2)}) collective-permute-start(bf16[512,256]{1,0:T(8,128)(2,1)S(1)} %get-tuple-element.16), channel_id=1, source_target_pairs={{0,12},{2,14},{4,0},{6,2},{8,4},{10,6},{12,8},{14,10},{1,13},{3,15... | collective-permute-start | bytes 786440 | tf_op jit(solution)/shard_map/ppermute | solution.py:359
  233.6 7.9 %collective-permute-done.3.rest_1_ = bf16[512,256]{1,0:T(8,128)(2,1)S(1)} collective-permute-done((bf16[512,256]{1,0:T(8,128)(2,1)S(1)}, bf16[512,256]{1,0:T(8,128)(2,1)S(1)}, u32[]{:S(2)}, u32[]{:S(2)}) %collective-permute-start.3) | collective-permute-done | bytes 262176 | tf_op jit(solution)/shard_map/ppermute | solution.py:359
  244.2 7.9 %collective-permute-start.19 = (f32[128,256]{1,0:T(8,128)S(1)}, f32[128,256]{1,0:T(8,128)S(1)}, u32[]{:S(2)}, u32[]{:S(2)}) collective-permute-start(f32[128,256]{1,0:T(8,128)S(1)} %select_add_fusion), channel_id=1, source_target_pairs={{0,1},{1,0},{2,3},{3,2},{4,5},{5,4},{6,7},{7,6},{8,9},{9,8},{10,11... | collective-permute-start | bytes 393224 | tf_op jit(solution)/shard_map/ppermute | solution.py:303
  253.8 7.6 %collective-permute-done.8.rest_6_ = bf16[512,256]{1,0:T(8,128)(2,1)S(1)} collective-permute-done((bf16[512,256]{1,0:T(8,128)(2,1)S(1)}, bf16[512,256]{1,0:T(8,128)(2,1)S(1)}, u32[]{:S(2)}, u32[]{:S(2)}) %collective-permute-start.8) | collective-permute-done | bytes 262176 | tf_op jit(solution)/shard_map/ppermute | solution.py:359
  263.6 3.6 %output_rows.1 = bf16[512,256]{1,0:T(8,128)(2,1)} custom-call(bf16[16,512,256]{2,1,0:T(8,128)(2,1)} %all-to-all-done.1.parts, bf16[256,256]{1,0:T(8,128)(2,1)S(1)} %copy-done.11, bf16[512,256]{1,0:T(8,128)(2,1)S(1)} %copy-done.10, f32[256,256]{1,0:T(8,128)S(1)} %pad_maximum_fusion.rest_1_), custom_call_target="tpu_custom_call" | custom-call | flops 4000000 | bytes 40000 | tf_op jit(solution)/shard_map/output_rows/pallas_call | solution.py:230
  (98 shorter events, 39.6 us)
Async XLA Ops:
  13.6 70.9 %all-to-all-start = ((bf16[16,1040,128]{2,1,0:T(8,128)(2,1)}), bf16[16,1040,128]{2,1,0:T(8,128)(2,1)}, u32[]{:S(2)}, u32[]{:S(2)}) async-start(bf16[16,1040,128]{2,1,0:T(8,128)(2,1)} %copy-done.6), calls=%async_computation | async-start | bytes 8519680 | tf_op jit(solution)/shard_map/all_to_all | solution.py:344
  21.5 63.8 %all-gather.6.cloned.1.call-start = ((), (), s32[]{:S(2)}) async-start(), calls=%async_computation.3 | async-start | bytes 2433024 | tf_op jit(solution)/shard_map/all_gather | solution.py:342
  22.3 121.8 %all-gather.4.cloned.1.call-start = ((), (), s32[]{:S(2)}) async-start(), calls=%async_computation.2 | async-start | bytes 4456448 | tf_op jit(solution)/shard_map/all_gather | solution.py:345
  97.9 8.1 %collective-permute-start = (bf16[64,128,256]{2,1,0:T(8,128)(2,1)S(1)}, bf16[64,128,256]{2,1,0:T(8,128)(2,1)S(1)}, u32[]{:S(2)}, u32[]{:S(2)}) collective-permute-start(bf16[64,128,256]{2,1,0:T(8,128)(2,1)S(1)} %hidden_for_other_core.1), channel_id=1, source_target_pairs={{0,1},{1,0},{2,3},{3,2},{4,5},{5,4},{6,7},{7,6},{8,9},{9,8},{10,11... | collective-permute-start | bytes 12582920 | tf_op jit(solution)/shard_map/ppermute | solution.py:303
  144.0 39.2 %collective-permute-start.1 = (bf16[64,128,256]{2,1,0:T(8,128)(2,1)}, bf16[64,128,256]{2,1,0:T(8,128)(2,1)}, u32[]{:S(2)}, u32[]{:S(2)}) collective-permute-start(bf16[64,128,256]{2,1,0:T(8,128)(2,1)} %in_order_in_place.1.mine), channel_id=1, source_target_pairs={{0,1},{1,0},{2,3},{3,2},{4,5},{5,4},{6,7},{7,6},{8,9},{9,8},{10,11... | collective-permute-start | bytes 12582920 | tf_op jit(solution)/shard_map/ppermute | solution.py:303
  144.7 117.9 %all-to-all-start.1 = ((bf16[16,512,256]{2,1,0:T(8,128)(2,1)}), bf16[16,512,256]{2,1,0:T(8,128)(2,1)}, u32[]{:S(2)}, u32[]{:S(2)}) async-start(bf16[16,512,256]{2,1,0:T(8,128)(2,1)} %bitcast.12), calls=%async_computation.1 | async-start | bytes 8388608 | tf_op jit(solution)/shard_map/all_to_all | solution.py:353
  158.6 1.4 collective-permute-start.9
  160.1 5.0 %collective-permute-start.10 = (f32[128,256]{1,0:T(8,128)S(1)}, f32[128,256]{1,0:T(8,128)S(1)}, u32[]{:S(2)}, u32[]{:S(2)}) collective-permute-start(f32[128,256]{1,0:T(8,128)S(1)} %bitcast_add_fusion), channel_id=1, source_target_pairs={{0,2},{2,0},{4,6},{6,4},{8,10},{10,8},{12,14},{14,12},{1,3},{3,1},... | collective-permute-start | bytes 393224 | tf_op jit(solution)/shard_map/ppermute | solution.py:325
  165.1 8.3 %collective-permute-start.11 = (f32[128,256]{1,0:T(8,128)S(1)}, f32[128,256]{1,0:T(8,128)S(1)}, u32[]{:S(2)}, u32[]{:S(2)}) collective-permute-start(f32[128,256]{1,0:T(8,128)S(1)} %add.96), channel_id=1, source_target_pairs={{0,4},{2,6},{4,0},{6,2},{8,12},{10,14},{12,8},{14,10},{1,5},{3,7},... | collective-permute-start | bytes 393224 | tf_op jit(solution)/shard_map/ppermute | solution.py:325
  173.4 9.8 %collective-permute-start.12 = (f32[128,256]{1,0:T(8,128)S(1)}, f32[128,256]{1,0:T(8,128)S(1)}, u32[]{:S(2)}, u32[]{:S(2)}) collective-permute-start(f32[128,256]{1,0:T(8,128)S(1)} %add.97), channel_id=1, source_target_pairs={{0,8},{2,10},{4,12},{6,14},{8,0},{10,2},{12,4},{14,6},{1,9},{3,11}... | collective-permute-start | bytes 393224 | tf_op jit(solution)/shard_map/ppermute | solution.py:325
  200.9 14.1 %collective-permute-start.13 = (f32[128,256]{1,0:T(8,128)S(1)}, f32[128,256]{1,0:T(8,128)S(1)}, u32[]{:S(2)}, u32[]{:S(2)}) collective-permute-start(f32[128,256]{1,0:T(8,128)S(1)} %in_order.3), channel_id=1, source_target_pairs={{0,16},{16,32},{32,48},{48,0},{1,17},{17,33},{33,49},{49,1},{2,18}... | collective-permute-start | bytes 393224 | tf_op jit(solution)/shard_map/ppermute | solution.py:308
  201.3 16.8 %collective-permute-start.14 = (f32[128,256]{1,0:T(8,128)S(1)}, f32[128,256]{1,0:T(8,128)S(1)}, u32[]{:S(2)}, u32[]{:S(2)}) collective-permute-start(f32[128,256]{1,0:T(8,128)S(1)} %in_order.3), channel_id=1, source_target_pairs={{0,32},{16,48},{32,0},{48,16},{1,33},{17,49},{33,1},{49,17},{2,34}... | collective-permute-start | bytes 393224 | tf_op jit(solution)/shard_map/ppermute | solution.py:308
  205.6 12.6 %collective-permute-start.15 = (f32[128,256]{1,0:T(8,128)S(1)}, f32[128,256]{1,0:T(8,128)S(1)}, u32[]{:S(2)}, u32[]{:S(2)}) collective-permute-start(f32[128,256]{1,0:T(8,128)S(1)} %in_order.3), channel_id=1, source_target_pairs={{0,48},{16,0},{32,16},{48,32},{1,49},{17,1},{33,17},{49,33},{2,50}... | collective-permute-start | bytes 393224 | tf_op jit(solution)/shard_map/ppermute | solution.py:308
  205.6 27.3 %collective-permute-start.2 = (bf16[512,256]{1,0:T(8,128)(2,1)S(1)}, bf16[512,256]{1,0:T(8,128)(2,1)S(1)}, u32[]{:S(2)}, u32[]{:S(2)}) collective-permute-start(bf16[512,256]{1,0:T(8,128)(2,1)S(1)} %get-tuple-element.12), channel_id=1, source_target_pairs={{0,8},{2,10},{4,12},{6,14},{8,0},{10,2},{12,4},{14,6},{1,9},{3,11}... | collective-permute-start | bytes 786440 | tf_op jit(solution)/shard_map/ppermute | solution.py:359
  210.5 31.0 %collective-permute-start.3 = (bf16[512,256]{1,0:T(8,128)(2,1)S(1)}, bf16[512,256]{1,0:T(8,128)(2,1)S(1)}, u32[]{:S(2)}, u32[]{:S(2)}) collective-permute-start(bf16[512,256]{1,0:T(8,128)(2,1)S(1)} %get-tuple-element.13), channel_id=1, source_target_pairs={{0,6},{2,8},{4,10},{6,12},{8,14},{10,0},{12,2},{14,4},{1,7},{3,9},... | collective-permute-start | bytes 786440 | tf_op jit(solution)/shard_map/ppermute | solution.py:359
  218.2 5.5 %collective-permute-start.16 = (f32[128,256]{1,0:T(8,128)S(1)}, f32[128,256]{1,0:T(8,128)S(1)}, u32[]{:S(2)}, u32[]{:S(2)}) collective-permute-start(f32[128,256]{1,0:T(8,128)S(1)} %select_add_fusion.1), channel_id=1, source_target_pairs={{0,64},{64,128},{128,192},{192,0},{1,65},{65,129},{129,193},{193,1... | collective-permute-start | bytes 393224 | tf_op jit(solution)/shard_map/ppermute | solution.py:308
  218.3 10.4 %collective-permute-start.17 = (f32[128,256]{1,0:T(8,128)S(1)}, f32[128,256]{1,0:T(8,128)S(1)}, u32[]{:S(2)}, u32[]{:S(2)}) collective-permute-start(f32[128,256]{1,0:T(8,128)S(1)} %select_add_fusion.1), channel_id=1, source_target_pairs={{0,128},{64,192},{128,0},{192,64},{1,129},{65,193},{129,1},{193,65... | collective-permute-start | bytes 393224 | tf_op jit(solution)/shard_map/ppermute | solution.py:308
  220.9 9.2 %collective-permute-start.18 = (f32[128,256]{1,0:T(8,128)S(1)}, f32[128,256]{1,0:T(8,128)S(1)}, u32[]{:S(2)}, u32[]{:S(2)}) collective-permute-start(f32[128,256]{1,0:T(8,128)S(1)} %select_add_fusion.1), channel_id=1, source_target_pairs={{0,192},{64,0},{128,64},{192,128},{1,193},{65,1},{129,65},{193,129... | collective-permute-start | bytes 393224 | tf_op jit(solution)/shard_map/ppermute | solution.py:308
  224.3 19.9 %collective-permute-start.4 = (bf16[512,256]{1,0:T(8,128)(2,1)}, bf16[512,256]{1,0:T(8,128)(2,1)S(1)}, u32[]{:S(2)}, u32[]{:S(2)}) collective-permute-start(bf16[512,256]{1,0:T(8,128)(2,1)} %get-tuple-element.14), channel_id=1, source_target_pairs={{0,10},{2,12},{4,14},{6,0},{8,2},{10,4},{12,6},{14,8},{1,11},{3,13... | collective-permute-start | bytes 786440 | tf_op jit(solution)/shard_map/ppermute | solution.py:359
  229.3 22.9 %collective-permute-start.5 = (bf16[512,256]{1,0:T(8,128)(2,1)}, bf16[512,256]{1,0:T(8,128)(2,1)S(1)}, u32[]{:S(2)}, u32[]{:S(2)}) collective-permute-start(bf16[512,256]{1,0:T(8,128)(2,1)} %get-tuple-element.15), channel_id=1, source_target_pairs={{0,4},{2,6},{4,8},{6,10},{8,12},{10,14},{12,0},{14,2},{1,5},{3,7},... | collective-permute-start | bytes 786440 | tf_op jit(solution)/shard_map/ppermute | solution.py:359
  230.1 23.6 %collective-permute-start.6 = (bf16[512,256]{1,0:T(8,128)(2,1)S(1)}, bf16[512,256]{1,0:T(8,128)(2,1)S(1)}, u32[]{:S(2)}, u32[]{:S(2)}) collective-permute-start(bf16[512,256]{1,0:T(8,128)(2,1)S(1)} %get-tuple-element.16), channel_id=1, source_target_pairs={{0,12},{2,14},{4,0},{6,2},{8,4},{10,6},{12,8},{14,10},{1,13},{3,15... | collective-permute-start | bytes 786440 | tf_op jit(solution)/shard_map/ppermute | solution.py:359
  232.9 20.9 %collective-permute-start.7 = (bf16[512,256]{1,0:T(8,128)(2,1)S(1)}, bf16[512,256]{1,0:T(8,128)(2,1)S(1)}, u32[]{:S(2)}, u32[]{:S(2)}) collective-permute-start(bf16[512,256]{1,0:T(8,128)(2,1)S(1)} %get-tuple-element.17), channel_id=1, source_target_pairs={{0,2},{2,4},{4,6},{6,8},{8,10},{10,12},{12,14},{14,0},{1,3},{3,5},... | collective-permute-start | bytes 786440 | tf_op jit(solution)/shard_map/ppermute | solution.py:359
  241.6 19.8 %collective-permute-start.8 = (bf16[512,256]{1,0:T(8,128)(2,1)S(1)}, bf16[512,256]{1,0:T(8,128)(2,1)S(1)}, u32[]{:S(2)}, u32[]{:S(2)}) collective-permute-start(bf16[512,256]{1,0:T(8,128)(2,1)S(1)} %get-tuple-element.18), channel_id=1, source_target_pairs={{0,14},{2,0},{4,2},{6,4},{8,6},{10,8},{12,10},{14,12},{1,15},{3,1}... | collective-permute-start | bytes 786440 | tf_op jit(solution)/shard_map/ppermute | solution.py:359
  244.2 18.3 %collective-permute-start.19 = (f32[128,256]{1,0:T(8,128)S(1)}, f32[128,256]{1,0:T(8,128)S(1)}, u32[]{:S(2)}, u32[]{:S(2)}) collective-permute-start(f32[128,256]{1,0:T(8,128)S(1)} %select_add_fusion), channel_id=1, source_target_pairs={{0,1},{1,0},{2,3},{3,2},{4,5},{5,4},{6,7},{7,6},{8,9},{9,8},{10,11... | collective-permute-start | bytes 393224 | tf_op jit(solution)/shard_map/ppermute | solution.py:303
  (22 other events, 411.0 us)
Sparse Core Ops, SparseCore 0:
  24.1 40.8 all-gather.5
  85.3 58.6 all-gather.3

commit v3 on v2

--- a/solution.py
+++ b/solution.py
@@ -57,14 +57,15 @@
 
 
 def cost(us):
-    return pl.CostEstimate(flops=us * 10**6, bytes_accessed=us * 10**4, transcendentals=0)
+    return pl.CostEstimate(flops=us * 10**8, bytes_accessed=us * 3 * 10**6, transcendentals=0)
 
 
 def rows_at(k):
     return pl.ds(pl.multiple_of(k * BLK, BLK), BLK)
 
 
-def hidden_kernel(first, where, meta, ids, cols, rows, count, sent, feats, tiles, *rest):
+def hidden_kernel(first, where, meta, ids, cols, rows, count, sent, tiles, *rest):
+    feats, rest = rest[:8], rest[8:]
     out, total = rest[-2:]
     c, z_me, r_me = where[0], where[1], where[2]
     half = 1 - c if first else c
@@ -79,22 +80,24 @@
         at = r * 4 + lax.rem(row, 4)
         total[at] = total[at] + jnp.dot(tile, block, preferred_element_type=jnp.float32)
 
-    def remote(i, carry):
-        r, z = lax.div(i, 8), lax.rem(i, 8)
-        row = meta[i] - 1
-
-        @pl.when((meta[i] > 0) & (lax.div(row, 4) == half))
-        def _():
-            add(sent[r, rows_at(z), :], feats[z, rows_at(ids[z * 16 + r]), :], r, row)
-
-        return carry
-
-    lax.fori_loop(0, 128, remote, 0)
+    for s in range(8):
+        z = jnp.bitwise_and(z_me - s + 8, 7)
+
+        def remote(r, carry, s=s, z=z):
+            mark = meta[r * 8 + z]
+
+            @pl.when((mark > 0) & (lax.div(mark - 1, 4) == half))
+            def _():
+                add(sent[r, rows_at(z), :], feats[s][rows_at(ids[s * 16 + r]), :], r, mark - 1)
+
+            return carry
+
+        lax.fori_loop(0, 16, remote, 0)
 
     def own(t, carry):
         @pl.when((cols[t] < 4) & (lax.div(rows[t], 4) == half))
         def _():
-            add(tiles[t], feats[z_me, rows_at(jnp.minimum(cols[t], 3)), :], r_me, rows[t])
+            add(tiles[t], feats[0][rows_at(jnp.minimum(cols[t], 3)), :], r_me, rows[t])
 
         return carry
 
@@ -107,20 +110,20 @@
     lax.fori_loop(0, total.shape[0], cast, 0)
 
 
-def hidden_parts(where, meta, ids, cols, rows, count, sent, feats, tiles, *arrived):
+def hidden_parts(where, meta, ids, cols, rows, count, sent, tiles, feats, *arrived):
     smem = pl.BlockSpec(memory_space=pltpu.SMEM)
     vmem = pl.BlockSpec(memory_space=pltpu.VMEM)
-    width = feats.shape[2]
+    width = feats[0].shape[1]
     return pl.pallas_call(
         functools.partial(hidden_kernel, not arrived),
         out_shape=jax.ShapeDtypeStruct((64, BLK, width), jnp.bfloat16),
-        in_specs=[smem] * 6 + [vmem] * (3 + len(arrived)),
+        in_specs=[smem] * 6 + [vmem] * (2 + len(feats) + len(arrived)),
         out_specs=vmem,
         scratch_shapes=[pltpu.VMEM((64, BLK, width), jnp.float32)],
         compiler_params=pltpu.CompilerParams(vmem_limit_bytes=28 * 2**20),
         cost_estimate=cost(10),
         name="hidden_sums" if arrived else "hidden_for_other_core",
-    )(where, meta, ids, cols, rows, count, sent, feats, tiles, *arrived)
+    )(where, meta, ids, cols, rows, count, sent, tiles, *feats, *arrived)
 
 
 def add_grads(half, where, meta, ids, cols, rows, count, sent, grads, tiles, total):
@@ -128,7 +131,8 @@
 
     def add(at, tile, r, row):
         term = lax.dot_general(
-            tile, grads[r * 4 + lax.rem(row, 4)], (((0,), (0,)), ((), ())), preferred_element_type=jnp.float32
+            tile, grads[r * 4 + lax.rem(row, 4)], (((0,), (0,)), ((), ())),
+            preferred_element_type=jnp.float32,
         )
         total[at] = total[at] + term
 
@@ -138,8 +142,8 @@
 
         @pl.when((meta[i] > 0) & (lax.div(row, 4) == half))
         def _():
-            step = jnp.bitwise_and(z - z_me + 8, 7)
-            add(step * 4 + ids[z * 16 + r], sent[r, rows_at(z), :], r, row)
+            step, back = jnp.bitwise_and(z - z_me + 8, 7), jnp.bitwise_and(z_me - z + 8, 7)
+            add(step * 4 + ids[back * 16 + r], sent[r, rows_at(z), :], r, row)
 
         return carry
 
@@ -211,7 +215,7 @@
         in_specs=[vmem] * 2,
         out_specs=vmem,
         compiler_params=pltpu.CompilerParams(vmem_limit_bytes=12 * 2**20),
-        cost_estimate=cost(8),
+        cost_estimate=cost(4),
         name="weight_term",
     )(parts, cots)
 
@@ -264,48 +268,59 @@
     )(own, *parts, weight)
 
 
-def later_kernel(array, after, out):
-    del after
-    out[...] = array[...]
-
-
-def later(array, after):
-    vmem = pl.BlockSpec(memory_space=pltpu.VMEM)
-    return pl.pallas_call(
-        later_kernel,
-        out_shape=jax.ShapeDtypeStruct(array.shape, array.dtype),
-        in_specs=[vmem, pl.BlockSpec(memory_space=pl.ANY)],
-        out_specs=vmem,
-        compiler_params=pltpu.CompilerParams(vmem_limit_bytes=4 * 2**20),
+def join_kernel(*refs):
+    out, at = refs[-1], 0
+    for ref in refs[:-2]:
+        out[pl.ds(at, ref.shape[0]), :] = ref[...]
+        at += ref.shape[0]
+
+
+def join_later(arrays, after):
+    vmem = pl.BlockSpec(memory_space=pltpu.VMEM)
+    length = sum(a.shape[0] for a in arrays)
+    return pl.pallas_call(
+        join_kernel,
+        out_shape=jax.ShapeDtypeStruct((length, arrays[0].shape[1]), arrays[0].dtype),
+        in_specs=[vmem] * len(arrays) + [pl.BlockSpec(memory_space=pl.ANY)],
+        out_specs=vmem,
+        compiler_params=pltpu.CompilerParams(vmem_limit_bytes=12 * 2**20),
         cost_estimate=cost(1),
         name="in_order",
-    )(array, after)
-
-
-def same_later_kernel(array, after, out):
-    del array, after, out
-
-
-def same_later(array, after):
+    )(*arrays, after)
+
+
+def same_later_kernel(*refs):
+    del refs
+
+
+def same_later(arrays, after):
     hbm = pl.BlockSpec(memory_space=pl.ANY)
     return pl.pallas_call(
         same_later_kernel,
-        out_shape=jax.ShapeDtypeStruct(array.shape, array.dtype),
-        in_specs=[hbm, hbm],
-        out_specs=hbm,
-        input_output_aliases={0: 0},
+        out_shape=[jax.ShapeDtypeStruct(a.shape, a.dtype) for a in arrays],
+        in_specs=[hbm] * (len(arrays) + 1),
+        out_specs=[hbm] * len(arrays),
+        input_output_aliases={i: i for i in range(len(arrays))},
         cost_estimate=cost(1),
         name="in_order_in_place",
-    )(array, after)
+    )(*arrays, after)
 
 
 def swap_cores(a):
     return lax.ppermute(a, "col", [(0, 1), (1, 0)])
 
 
+def steps_along(a, axis, size):
+    return [a] + [lax.ppermute(a, axis, [(i, (i + s) % size) for i in range(size)]) for s in range(1, size)]
+
+
+def mark(*arrays):
+    return jnp.concatenate([a.reshape(-1, a.shape[-1])[:META].astype(jnp.bfloat16) for a in arrays], axis=0)
+
+
 def sum_four(a, axis):
     me = lax.axis_index(axis)
-    from_step = [a] + [lax.ppermute(a, axis, [(i, (i + step) % 4) for i in range(4)]) for step in (1, 2, 3)]
+    from_step = steps_along(a, axis, 4)
     total = None
     for source in range(4):
         step = jnp.bitwise_and(me - source + 4, 3)
@@ -320,10 +335,10 @@
     halves = term.reshape(2, 128, term.shape[1])
     keep = lax.dynamic_index_in_dim(halves, c, 0, keepdims=False)
     give = lax.dynamic_index_in_dim(halves, 1 - c, 0, keepdims=False)
-    half = keep + swap_cores(give)
+    half = join_later([keep + swap_cores(give)], after)
+    half = sum_four(sum_four(half, "x"), "y")
     for step in (1, 2, 4):
         half = half + lax.ppermute(half, "z", [(i, i ^ step) for i in range(8)])
-    half = sum_four(sum_four(later(half, after), "x"), "y")
     other = swap_cores(half)
     first = jnp.where(c == 0, half, other)
     second = jnp.where(c == 0, other, half)
@@ -336,32 +351,34 @@
     c = lax.axis_index("col")
     z_me = lax.axis_index("z")
     r_me = lax.axis_index(PLANE)
-    where = jnp.stack([c, z_me, r_me]).astype(jnp.int32)
+    where = jnp.stack([c, z_me, r_me, lax.axis_index("y"), lax.axis_index("x")]).astype(jnp.int32)
 
     ids_row = jnp.pad(send_blocks.astype(jnp.bfloat16), ((0, META - 1), (0, width - send_blocks.shape[1])))
-    column = lax.all_gather(jnp.concatenate([features, ids_row], axis=0), "z", axis=0)
+    feats = steps_along(jnp.concatenate([features, ids_row], axis=0), "z", 8)
+    cot_mine = lax.all_gather(cotangent.reshape(4, BLK, width), PLANE, axis=0, tiled=True)
     packed = pack(tile_cols, tile_rows, tile_count, tile_values)
     sent = lax.all_to_all(packed, PLANE, 0, 0, tiled=True)
-    cot_mine = lax.all_gather(later(cotangent, sent).reshape(4, BLK, width), PLANE, axis=0, tiled=True)
 
     meta = sent[:, 8 * BLK, :8].astype(jnp.int32).reshape(128)
-    ids = column[:, 4 * BLK, :128].astype(jnp.int32).reshape(8, 16, 8)
+    ids = jnp.stack([f[4 * BLK, :128] for f in feats]).astype(jnp.int32).reshape(8, 16, 8)
     ids = lax.dynamic_index_in_dim(ids, z_me, 2, keepdims=False).reshape(128)
 
-    operands = (where, meta, ids, tile_cols, tile_rows, tile_count, sent, column, tile_values)
-    both = hidden_parts(*operands, swap_cores(hidden_parts(*operands)))
+    operands = (where, meta, ids, tile_cols, tile_rows, tile_count, sent)
+    for_peer = swap_cores(hidden_parts(*operands, tile_values, feats))
+    both = hidden_parts(*operands, tile_values, feats, for_peer)
     parts = lax.all_to_all(both.reshape(16, 4 * BLK, width), PLANE, 0, 0, tiled=True)
-    cot_mine = same_later(cot_mine, both)
-    own, *away = grad_parts(*operands[:7], cot_mine, swap_cores(cot_mine), tile_values)
+    [cot_mine] = same_later([cot_mine], mark(both))
+    own, *away = grad_parts(*operands, cot_mine, swap_cores(cot_mine), tile_values)
     by_partition = (16, 4 * BLK, width)
     term = weight_term(both.reshape(by_partition), cot_mine.reshape(by_partition), float(1.0 / node_total**0.5))
+    term = join_later([term], mark(own))
     arrived = [
         lax.ppermute(part, "z", [(z, (z + step) % 8) for z in range(8)])
         for step, part in sorted(enumerate(away, 1), key=lambda e: -min(e[0], 8 - e[0]))
     ]
     feature_grad = feature_from(own, arrived, weight)
-    weight_grad = sum_everywhere(term, c, own)
-    output_rows = output_from(parts, weight, feature_grad, weight_grad)
+    weight_grad = sum_everywhere(term, c, mark(*arrived[:5]))
+    output_rows = output_from(parts, weight)
     return (output_rows, feature_grad, weight_grad)
 
 

time: 275 us -> 255 us (0.927)
  waiting for transfers between devices: 134 us -> 115 us
  local copies, waits for them, and re-layouts: 17.8 us -> 12.9 us
  starting transfers between devices: 60.9 us -> 65.3 us
    all_to_all x1, waiting for transfers between devices: 62.1 us -> 3.71 us  [local(): sent = lax.all_to_all(packed, PLANE, 0, 0, tiled=True)]
    ppermute x6 -> x13, waiting for transfers between devices: 3.94 us -> 61 us  [steps_along(): lax.ppermute(a, axis, [(i, (i + s) % size) for i in range(size)])]
    all_gather x2 -> x1, waiting for transfers between devices: 28.1 us -> 0.01 us  [local(): lax.all_gather(cotangent.reshape(4, BLK, width), PLANE, axis=0, tiled=True)]
    ppermute x7, waiting for transfers between devices: 18.7 us -> 34.2 us  [local(): lax.ppermute(part, 'z', [(z, (z + step) % 8) for z in range(8)])]
    ppermute x6 -> x13, starting transfers between devices: 9.33 us -> 20.4 us  [steps_along(): lax.ppermute(a, axis, [(i, (i + s) % size) for i in range(size)])]
    ppermute x4, starting transfers between devices: 10.3 us -> 3.71 us  [swap_cores(): return lax.ppermute(a, 'col', [(0, 1), (1, 0)])]
    unnamed x44 -> x39, local copies, waits for them, and re-layouts: 17.2 us -> 11.1 us
    ppermute x3, waiting for transfers between devices: 12.9 us -> 8.73 us  [sum_everywhere(): half = half + lax.ppermute(half, 'z', [(i, i ^ step) for i in range(8)])]
  transfers between devices with their start and end apart: 24 -> 30, of which waited for: 13 -> 18; matrix products, arithmetic and copies ran while one was open for 2% -> 1% of each run, Pallas kernels for 14% -> 17%
where the time goes in v3:
time: 255 us; the launch traced here: 254 us
  waiting for transfers between devices  115 us (45%)
  starting transfers between devices  65.3 us (26%)
  Pallas kernels  43.4 us (17%)
  between operations  15 us (6%)
  local copies, waits for them, and re-layouts  12.9 us (5%)
    ppermute x13, waiting for transfers between devices, steps_along(): lax.ppermute(a, axis, [(i, (i + s) % size) for i in range(size)])  61 us
    ppermute x7, waiting for transfers between devices, local(): lax.ppermute(part, 'z', [(z, (z + step) % 8) for z in range(8)])  34.2 us
    ppermute x13, starting transfers between devices, steps_along(): lax.ppermute(a, axis, [(i, (i + s) % size) for i in range(size)])  20.4 us
    ppermute x7, starting transfers between devices, local(): lax.ppermute(part, 'z', [(z, (z + step) % 8) for z in range(8)])  18.9 us
    pallas_call x2, Pallas kernels, hidden_parts(): pl.pallas_call(functools.partial(hidden_kernel, not arrived), out_shape=j...  17.1 us
    pallas_call x1, Pallas kernels, grad_parts(): pl.pallas_call(grad_kernel, out_shape=[jax.ShapeDtypeStruct((4 * BLK, wid...  16 us
    unnamed x39, local copies, waits for them, and re-layouts  11.1 us
    ppermute x3, starting transfers between devices, sum_everywhere(): half = half + lax.ppermute(half, 'z', [(i, i ^ step) for i in range(8)])  9.51 us
  transfers between devices with their start and end apart: 30, of which 18 were waited for; matrix products, arithmetic and copies ran while one was open for 1% of the time, Pallas kernels for 17%

profile of v3, /device:TPU:1, one launch (start us, length us, event | category | flops | bytes accessed | tf_op | source)
XLA Modules:
  0.0 253.9 jit_solution(10619164736123921195)
XLA Ops:
  13.7 7.8 %all-to-all-start = ((bf16[16,1040,128]{2,1,0:T(8,128)(2,1)}), bf16[16,1040,128]{2,1,0:T(8,128)(2,1)}, u32[]{:S(2)}, u32[]{:S(2)}) async-start(bf16[16,1040,128]{2,1,0:T(8,128)(2,1)} %copy-done.6), calls=%async_computation | async-start | bytes 8519680 | tf_op jit(solution)/shard_map/all_to_all | solution.py:360
  22.3 5.6 %collective-permute-start.6 = (bf16[528,256]{1,0:T(8,128)(2,1)S(1)}, bf16[528,256]{1,0:T(8,128)(2,1)S(1)}, u32[]{:S(2)}, u32[]{:S(2)}) collective-permute-start(bf16[528,256]{1,0:T(8,128)(2,1)S(1)} %fusion.1.rest_0_), channel_id=1, source_target_pairs={{0,14},{2,0},{4,2},{6,4},{8,6},{10,8},{12,10},{14,12},{1,15},{3,1}... | collective-permute-start | bytes 811016 | tf_op jit(solution)/shard_map/ppermute | solution.py:314
  29.6 4.6 %collective-permute-start.3 = (bf16[528,256]{1,0:T(8,128)(2,1)S(1)}, bf16[528,256]{1,0:T(8,128)(2,1)S(1)}, u32[]{:S(2)}, u32[]{:S(2)}) collective-permute-start(bf16[528,256]{1,0:T(8,128)(2,1)S(1)} %fusion.1.rest_0_), channel_id=1, source_target_pairs={{0,8},{2,10},{4,12},{6,14},{8,0},{10,2},{12,4},{14,6},{1,9},{3,11}... | collective-permute-start | bytes 811016 | tf_op jit(solution)/shard_map/ppermute | solution.py:314
  36.5 12.6 %collective-permute-done.5.rest_6_ = bf16[528,256]{1,0:T(8,128)(2,1)S(1)} collective-permute-done((bf16[528,256]{1,0:T(8,128)(2,1)S(1)}, bf16[528,256]{1,0:T(8,128)(2,1)S(1)}, u32[]{:S(2)}, u32[]{:S(2)}) %collective-permute-start.5) | collective-permute-done | bytes 270368 | tf_op jit(solution)/shard_map/ppermute | solution.py:314
  49.0 24.2 %collective-permute-done.4.rest_5_ = bf16[528,256]{1,0:T(8,128)(2,1)S(1)} collective-permute-done((bf16[528,256]{1,0:T(8,128)(2,1)S(1)}, bf16[528,256]{1,0:T(8,128)(2,1)S(1)}, u32[]{:S(2)}, u32[]{:S(2)}) %collective-permute-start.4) | collective-permute-done | bytes 270368 | tf_op jit(solution)/shard_map/ppermute | solution.py:314
  73.9 8.0 %collective-permute-done.rest_1_ = bf16[528,256]{1,0:T(8,128)(2,1)S(1)} collective-permute-done((bf16[528,256]{1,0:T(8,128)(2,1)S(1)}, bf16[528,256]{1,0:T(8,128)(2,1)S(1)}, u32[]{:S(2)}, u32[]{:S(2)}) %collective-permute-start) | collective-permute-done | bytes 270368 | tf_op jit(solution)/shard_map/ppermute | solution.py:314
  82.5 3.7 %all-to-all-done.sent = bf16[16,1040,128]{2,1,0:T(8,128)(2,1)} async-done(((bf16[16,1040,128]{2,1,0:T(8,128)(2,1)}), bf16[16,1040,128]{2,1,0:T(8,128)(2,1)}, u32[]{:S(2)}, u32[]{:S(2)}) %all-to-all-start) | async-done | bytes 4259872 | tf_op jit(solution)/shard_map/all_to_all | solution.py:360
  87.1 9.2 %hidden_for_other_core.1 = bf16[64,128,256]{2,1,0:T(8,128)(2,1)S(1)} custom-call(s32[5]{0:T(128)S(1)} %stack.42.where, s32[128]{0:T(128)S(1)} %reshape.45.meta, s32[128]{0:T(128)S(1)} %reshape.39.ids, s32[40]{0:T(128)S(1)} %copy-done.9, s32[40]{0:T(128)S(1)} %copy-done.11, s32[1]{0:T(128)S(6)} %copy.24.count, bf16[16,1040,128]{2,1,0:T(8,128)(2,1)} %all-to-all-done.sent, ...), custom_call_target="tpu_custom_call" | custom-call | flops 1000000000 | bytes 30000000 | tf_op jit(solution)/shard_map/hidden_for_other_core/pallas_call | solution.py:117
  97.0 6.8 %collective-permute-done.7.rest_8_ = bf16[64,128,256]{2,1,0:T(8,128)(2,1)S(1)} collective-permute-done((bf16[64,128,256]{2,1,0:T(8,128)(2,1)S(1)}, bf16[64,128,256]{2,1,0:T(8,128)(2,1)S(1)}, u32[]{:S(2)}, u32[]{:S(2)}) %collective-permute-start.7) | collective-permute-done | bytes 4194336 | tf_op jit(solution)/shard_map/ppermute | solution.py:310
  103.7 7.9 %hidden_sums.1 = bf16[64,128,256]{2,1,0:T(8,128)(2,1)S(1)} custom-call(s32[5]{0:T(128)S(1)} %stack.42.where, s32[128]{0:T(128)S(1)} %reshape.45.meta, s32[128]{0:T(128)S(1)} %reshape.39.ids, s32[40]{0:T(128)S(1)} %copy-done.9, s32[40]{0:T(128)S(1)} %copy-done.11, s32[1]{0:T(128)S(6)} %copy.24.count, bf16[16,1040,128]{2,1,0:T(8,128)(2,1)} %all-to-all-done.sent, ...), custom_call_target="tpu_custom_call" | custom-call | flops 1000000000 | bytes 30000000 | tf_op jit(solution)/shard_map/hidden_sums/pallas_call | solution.py:117
  115.4 5.0 %all-to-all-start.1 = ((bf16[16,512,256]{2,1,0:T(8,128)(2,1)}), bf16[16,512,256]{2,1,0:T(8,128)(2,1)}, u32[]{:S(2)}, u32[]{:S(2)}) async-start(bf16[16,512,256]{2,1,0:T(8,128)(2,1)} %bitcast.15), calls=%async_computation.1 | async-start | bytes 8388608 | tf_op jit(solution)/shard_map/all_to_all | solution.py:369
  124.7 4.4 %weight_term.1.refs_0_ = f32[256,256]{1,0:T(8,128)S(1)} custom-call(bf16[16,512,256]{2,1,0:T(8,128)(2,1)S(1)} %bitcast.16, bf16[16,512,256]{2,1,0:T(8,128)(2,1)S(1)} %bitcast.17), custom_call_target="tpu_custom_call" | custom-call | flops 400000000 | bytes 12000000 | tf_op jit(solution)/shard_map/weight_term/pallas_call | solution.py:212
  129.2 16.0 %grad_sums.1 = (f32[512,256]{1,0:T(8,128)S(1)}, bf16[512,256]{1,0:T(8,128)(2,1)S(1)}, bf16[512,256]{1,0:T(8,128)(2,1)S(1)}, bf16[512,256]{1,0:T(8,128)(2,1)}, bf...) custom-call(s32[5]{0:T(128)S(1)} %stack.42.where, ...), custom_call_target="tpu_custom_call" | custom-call | flops 800000000 | bytes 24000000 | tf_op jit(solution)/shard_map/grad_sums/pallas_call | solution.py:183
  145.3 5.5 %collective-permute-start.9 = (bf16[512,256]{1,0:T(8,128)(2,1)}, bf16[512,256]{1,0:T(8,128)(2,1)S(1)}, u32[]{:S(2)}, u32[]{:S(2)}) collective-permute-start(bf16[512,256]{1,0:T(8,128)(2,1)} %get-tuple-element.12), channel_id=1, source_target_pairs={{0,8},{2,10},{4,12},{6,14},{8,0},{10,2},{12,4},{14,6},{1,9},{3,11}... | collective-permute-start | bytes 786440 | tf_op jit(solution)/shard_map/ppermute | solution.py:376
  150.9 4.6 %collective-permute-start.10 = (bf16[512,256]{1,0:T(8,128)(2,1)}, bf16[512,256]{1,0:T(8,128)(2,1)S(1)}, u32[]{:S(2)}, u32[]{:S(2)}) collective-permute-start(bf16[512,256]{1,0:T(8,128)(2,1)} %get-tuple-element.13), channel_id=1, source_target_pairs={{0,6},{2,8},{4,10},{6,12},{8,14},{10,0},{12,2},{14,4},{1,7},{3,9},... | collective-permute-start | bytes 786440 | tf_op jit(solution)/shard_map/ppermute | solution.py:376
  155.4 3.8 %collective-permute-start.12 = (bf16[512,256]{1,0:T(8,128)(2,1)S(1)}, bf16[512,256]{1,0:T(8,128)(2,1)S(1)}, u32[]{:S(2)}, u32[]{:S(2)}) collective-permute-start(bf16[512,256]{1,0:T(8,128)(2,1)S(1)} %get-tuple-element.15), channel_id=1, source_target_pairs={{0,4},{2,6},{4,8},{6,10},{8,12},{10,14},{12,0},{14,2},{1,5},{3,7},... | collective-permute-start | bytes 786440 | tf_op jit(solution)/shard_map/ppermute | solution.py:376
  159.3 25.9 %collective-permute-done.10.rest_1_ = bf16[512,256]{1,0:T(8,128)(2,1)S(1)} collective-permute-done((bf16[512,256]{1,0:T(8,128)(2,1)}, bf16[512,256]{1,0:T(8,128)(2,1)S(1)}, u32[]{:S(2)}, u32[]{:S(2)}) %collective-permute-start.10) | collective-permute-done | bytes 262176 | tf_op jit(solution)/shard_map/ppermute | solution.py:376
  186.5 7.0 %collective-permute-done.13.rest_4_ = bf16[512,256]{1,0:T(8,128)(2,1)S(1)} collective-permute-done((bf16[512,256]{1,0:T(8,128)(2,1)S(1)}, bf16[512,256]{1,0:T(8,128)(2,1)S(1)}, u32[]{:S(2)}, u32[]{:S(2)}) %collective-permute-start.13) | collective-permute-done | bytes 262176 | tf_op jit(solution)/shard_map/ppermute | solution.py:376
  197.2 4.6 %collective-permute-done.19 = f32[128,256]{1,0:T(8,128)S(1)} collective-permute-done((f32[128,256]{1,0:T(8,128)S(1)}, f32[128,256]{1,0:T(8,128)S(1)}, u32[]{:S(2)}, u32[]{:S(2)}) %collective-permute-start.19) | collective-permute-done | bytes 131104 | tf_op jit(solution)/shard_map/ppermute | solution.py:314
  212.9 3.4 %collective-permute-done.20 = f32[128,256]{1,0:T(8,128)S(1)} collective-permute-done((f32[128,256]{1,0:T(8,128)S(1)}, f32[128,256]{1,0:T(8,128)S(1)}, u32[]{:S(2)}, u32[]{:S(2)}) %collective-permute-start.20) | collective-permute-done | bytes 131104 | tf_op jit(solution)/shard_map/ppermute | solution.py:314
  222.6 3.6 %collective-permute-start.15 = (bf16[512,256]{1,0:T(8,128)(2,1)S(1)}, bf16[512,256]{1,0:T(8,128)(2,1)S(1)}, u32[]{:S(2)}, u32[]{:S(2)}) collective-permute-start(bf16[512,256]{1,0:T(8,128)(2,1)S(1)} %get-tuple-element.18), channel_id=1, source_target_pairs={{0,14},{2,0},{4,2},{6,4},{8,6},{10,8},{12,10},{14,12},{1,15},{3,1}... | collective-permute-start | bytes 786440 | tf_op jit(solution)/shard_map/ppermute | solution.py:376
  226.6 7.5 %collective-permute-start.25 = (f32[128,256]{1,0:T(8,128)S(1)}, f32[128,256]{1,0:T(8,128)S(1)}, u32[]{:S(2)}, u32[]{:S(2)}) collective-permute-start(f32[128,256]{1,0:T(8,128)S(1)} %add.109), channel_id=1, source_target_pairs={{0,8},{2,10},{4,12},{6,14},{8,0},{10,2},{12,4},{14,6},{1,9},{3,11}... | collective-permute-start | bytes 393224 | tf_op jit(solution)/shard_map/ppermute | solution.py:341
  234.2 5.5 %collective-permute-done.25 = f32[128,256]{1,0:T(8,128)S(1)} collective-permute-done((f32[128,256]{1,0:T(8,128)S(1)}, f32[128,256]{1,0:T(8,128)S(1)}, u32[]{:S(2)}, u32[]{:S(2)}) %collective-permute-start.25) | collective-permute-done | bytes 131104 | tf_op jit(solution)/shard_map/ppermute | solution.py:341
  241.6 3.6 %output_rows.1 = bf16[512,256]{1,0:T(8,128)(2,1)} custom-call(bf16[16,512,256]{2,1,0:T(8,128)(2,1)} %all-to-all-done.1.parts, bf16[256,256]{1,0:T(8,128)(2,1)S(1)} %copy-done.7), custom_call_target="tpu_custom_call" | custom-call | flops 400000000 | bytes 12000000 | tf_op jit(solution)/shard_map/output_rows/pallas_call | solution.py:234
  (122 shorter events, 48.1 us)
Async XLA Ops:
  13.7 72.5 %all-to-all-start = ((bf16[16,1040,128]{2,1,0:T(8,128)(2,1)}), bf16[16,1040,128]{2,1,0:T(8,128)(2,1)}, u32[]{:S(2)}, u32[]{:S(2)}) async-start(bf16[16,1040,128]{2,1,0:T(8,128)(2,1)} %copy-done.6), calls=%async_computation | async-start | bytes 8519680 | tf_op jit(solution)/shard_map/all_to_all | solution.py:360
  21.5 92.7 %all-gather.2.cloned.1.call-start = ((), (), s32[]{:S(2)}) async-start(), calls=%async_computation.2 | async-start | bytes 4456448 | tf_op jit(solution)/shard_map/all_gather | solution.py:358
  22.3 13.0 %collective-permute-start.6 = (bf16[528,256]{1,0:T(8,128)(2,1)S(1)}, bf16[528,256]{1,0:T(8,128)(2,1)S(1)}, u32[]{:S(2)}, u32[]{:S(2)}) collective-permute-start(bf16[528,256]{1,0:T(8,128)(2,1)S(1)} %fusion.1.rest_0_), channel_id=1, source_target_pairs={{0,14},{2,0},{4,2},{6,4},{8,6},{10,8},{12,10},{14,12},{1,15},{3,1}... | collective-permute-start | bytes 811016 | tf_op jit(solution)/shard_map/ppermute | solution.py:314
  27.8 21.2 %collective-permute-start.5 = (bf16[528,256]{1,0:T(8,128)(2,1)S(1)}, bf16[528,256]{1,0:T(8,128)(2,1)S(1)}, u32[]{:S(2)}, u32[]{:S(2)}) collective-permute-start(bf16[528,256]{1,0:T(8,128)(2,1)S(1)} %fusion.1.rest_0_), channel_id=1, source_target_pairs={{0,12},{2,14},{4,0},{6,2},{8,4},{10,6},{12,8},{14,10},{1,13},{3,15... | collective-permute-start | bytes 811016 | tf_op jit(solution)/shard_map/ppermute | solution.py:314
  29.2 44.1 %collective-permute-start.4 = (bf16[528,256]{1,0:T(8,128)(2,1)S(1)}, bf16[528,256]{1,0:T(8,128)(2,1)S(1)}, u32[]{:S(2)}, u32[]{:S(2)}) collective-permute-start(bf16[528,256]{1,0:T(8,128)(2,1)S(1)} %fusion.1.rest_0_), channel_id=1, source_target_pairs={{0,10},{2,12},{4,14},{6,0},{8,2},{10,4},{12,6},{14,8},{1,11},{3,13... | collective-permute-start | bytes 811016 | tf_op jit(solution)/shard_map/ppermute | solution.py:314
  29.6 43.7 %collective-permute-start.3 = (bf16[528,256]{1,0:T(8,128)(2,1)S(1)}, bf16[528,256]{1,0:T(8,128)(2,1)S(1)}, u32[]{:S(2)}, u32[]{:S(2)}) collective-permute-start(bf16[528,256]{1,0:T(8,128)(2,1)S(1)} %fusion.1.rest_0_), channel_id=1, source_target_pairs={{0,8},{2,10},{4,12},{6,14},{8,0},{10,2},{12,4},{14,6},{1,9},{3,11}... | collective-permute-start | bytes 811016 | tf_op jit(solution)/shard_map/ppermute | solution.py:314
  34.2 39.5 %collective-permute-start.2 = (bf16[528,256]{1,0:T(8,128)(2,1)S(1)}, bf16[528,256]{1,0:T(8,128)(2,1)S(1)}, u32[]{:S(2)}, u32[]{:S(2)}) collective-permute-start(bf16[528,256]{1,0:T(8,128)(2,1)S(1)} %fusion.1.rest_0_), channel_id=1, source_target_pairs={{0,6},{2,8},{4,10},{6,12},{8,14},{10,0},{12,2},{14,4},{1,7},{3,9},... | collective-permute-start | bytes 811016 | tf_op jit(solution)/shard_map/ppermute | solution.py:314
  35.2 38.6 %collective-permute-start.1 = (bf16[528,256]{1,0:T(8,128)(2,1)S(1)}, bf16[528,256]{1,0:T(8,128)(2,1)S(1)}, u32[]{:S(2)}, u32[]{:S(2)}) collective-permute-start(bf16[528,256]{1,0:T(8,128)(2,1)S(1)} %fusion.1.rest_0_), channel_id=1, source_target_pairs={{0,4},{2,6},{4,8},{6,10},{8,12},{10,14},{12,0},{14,2},{1,5},{3,7},... | collective-permute-start | bytes 811016 | tf_op jit(solution)/shard_map/ppermute | solution.py:314
  49.0 32.9 %collective-permute-start = (bf16[528,256]{1,0:T(8,128)(2,1)S(1)}, bf16[528,256]{1,0:T(8,128)(2,1)S(1)}, u32[]{:S(2)}, u32[]{:S(2)}) collective-permute-start(bf16[528,256]{1,0:T(8,128)(2,1)S(1)} %fusion.1.rest_0_), channel_id=1, source_target_pairs={{0,2},{2,4},{4,6},{6,8},{8,10},{10,12},{12,14},{14,0},{1,3},{3,5},... | collective-permute-start | bytes 811016 | tf_op jit(solution)/shard_map/ppermute | solution.py:314
  96.4 7.4 %collective-permute-start.7 = (bf16[64,128,256]{2,1,0:T(8,128)(2,1)S(1)}, bf16[64,128,256]{2,1,0:T(8,128)(2,1)S(1)}, u32[]{:S(2)}, u32[]{:S(2)}) collective-permute-start(bf16[64,128,256]{2,1,0:T(8,128)(2,1)S(1)} %hidden_for_other_core.1), channel_id=1, source_target_pairs={{0,1},{1,0},{2,3},{3,2},{4,5},{5,4},{6,7},{7,6},{8,9},{9,8},{10,11... | collective-permute-start | bytes 12582920 | tf_op jit(solution)/shard_map/ppermute | solution.py:310
  114.2 15.0 %collective-permute-start.8 = (bf16[64,128,256]{2,1,0:T(8,128)(2,1)}, bf16[64,128,256]{2,1,0:T(8,128)(2,1)}, u32[]{:S(2)}, u32[]{:S(2)}) collective-permute-start(bf16[64,128,256]{2,1,0:T(8,128)(2,1)} %in_order_in_place.1.mine), channel_id=1, source_target_pairs={{0,1},{1,0},{2,3},{3,2},{4,5},{5,4},{6,7},{7,6},{8,9},{9,8},{10,11... | collective-permute-start | bytes 12582920 | tf_op jit(solution)/shard_map/ppermute | solution.py:310
  115.4 126.2 %all-to-all-start.1 = ((bf16[16,512,256]{2,1,0:T(8,128)(2,1)}), bf16[16,512,256]{2,1,0:T(8,128)(2,1)}, u32[]{:S(2)}, u32[]{:S(2)}) async-start(bf16[16,512,256]{2,1,0:T(8,128)(2,1)} %bitcast.15), calls=%async_computation.1 | async-start | bytes 8388608 | tf_op jit(solution)/shard_map/all_to_all | solution.py:369
  145.2 14.0 %collective-permute-start.16 = (f32[128,256]{1,0:T(8,128)S(1)}, f32[128,256]{1,0:T(8,128)S(1)}, u32[]{:S(2)}, u32[]{:S(2)}) collective-permute-start(f32[128,256]{1,0:T(8,128)S(1)} %dynamic-slice_bitcast_fusion), channel_id=1, source_target_pairs={{0,1},{1,0},{2,3},{3,2},{4,5},{5,4},{6,7},{7,6},{8,9},{9,8},{10,11... | collective-permute-start | bytes 393224 | tf_op jit(solution)/shard_map/ppermute | solution.py:310
  145.3 13.9 %collective-permute-start.9 = (bf16[512,256]{1,0:T(8,128)(2,1)}, bf16[512,256]{1,0:T(8,128)(2,1)S(1)}, u32[]{:S(2)}, u32[]{:S(2)}) collective-permute-start(bf16[512,256]{1,0:T(8,128)(2,1)} %get-tuple-element.12), channel_id=1, source_target_pairs={{0,8},{2,10},{4,12},{6,14},{8,0},{10,2},{12,4},{14,6},{1,9},{3,11}... | collective-permute-start | bytes 786440 | tf_op jit(solution)/shard_map/ppermute | solution.py:376
  150.9 34.4 %collective-permute-start.10 = (bf16[512,256]{1,0:T(8,128)(2,1)}, bf16[512,256]{1,0:T(8,128)(2,1)S(1)}, u32[]{:S(2)}, u32[]{:S(2)}) collective-permute-start(bf16[512,256]{1,0:T(8,128)(2,1)} %get-tuple-element.13), channel_id=1, source_target_pairs={{0,6},{2,8},{4,10},{6,12},{8,14},{10,0},{12,2},{14,4},{1,7},{3,9},... | collective-permute-start | bytes 786440 | tf_op jit(solution)/shard_map/ppermute | solution.py:376
  155.4 29.8 %collective-permute-start.11 = (bf16[512,256]{1,0:T(8,128)(2,1)}, bf16[512,256]{1,0:T(8,128)(2,1)S(1)}, u32[]{:S(2)}, u32[]{:S(2)}) collective-permute-start(bf16[512,256]{1,0:T(8,128)(2,1)} %get-tuple-element.14), channel_id=1, source_target_pairs={{0,10},{2,12},{4,14},{6,0},{8,2},{10,4},{12,6},{14,8},{1,11},{3,13... | collective-permute-start | bytes 786440 | tf_op jit(solution)/shard_map/ppermute | solution.py:376
  155.4 31.1 %collective-permute-start.12 = (bf16[512,256]{1,0:T(8,128)(2,1)S(1)}, bf16[512,256]{1,0:T(8,128)(2,1)S(1)}, u32[]{:S(2)}, u32[]{:S(2)}) collective-permute-start(bf16[512,256]{1,0:T(8,128)(2,1)S(1)} %get-tuple-element.15), channel_id=1, source_target_pairs={{0,4},{2,6},{4,8},{6,10},{8,12},{10,14},{12,0},{14,2},{1,5},{3,7},... | collective-permute-start | bytes 786440 | tf_op jit(solution)/shard_map/ppermute | solution.py:376
  159.2 34.3 %collective-permute-start.13 = (bf16[512,256]{1,0:T(8,128)(2,1)S(1)}, bf16[512,256]{1,0:T(8,128)(2,1)S(1)}, u32[]{:S(2)}, u32[]{:S(2)}) collective-permute-start(bf16[512,256]{1,0:T(8,128)(2,1)S(1)} %get-tuple-element.16), channel_id=1, source_target_pairs={{0,12},{2,14},{4,0},{6,2},{8,4},{10,6},{12,8},{14,10},{1,13},{3,15... | collective-permute-start | bytes 786440 | tf_op jit(solution)/shard_map/ppermute | solution.py:376
  193.5 8.3 %collective-permute-start.19 = (f32[128,256]{1,0:T(8,128)S(1)}, f32[128,256]{1,0:T(8,128)S(1)}, u32[]{:S(2)}, u32[]{:S(2)}) collective-permute-start(f32[128,256]{1,0:T(8,128)S(1)} %in_order.3), channel_id=1, source_target_pairs={{0,48},{16,0},{32,16},{48,32},{1,49},{17,1},{33,17},{49,33},{2,50}... | collective-permute-start | bytes 393224 | tf_op jit(solution)/shard_map/ppermute | solution.py:314
  196.6 9.1 %collective-permute-start.17 = (f32[128,256]{1,0:T(8,128)S(1)}, f32[128,256]{1,0:T(8,128)S(1)}, u32[]{:S(2)}, u32[]{:S(2)}) collective-permute-start(f32[128,256]{1,0:T(8,128)S(1)} %in_order.3), channel_id=1, source_target_pairs={{0,16},{16,32},{32,48},{48,0},{1,17},{17,33},{33,49},{49,1},{2,18}... | collective-permute-start | bytes 393224 | tf_op jit(solution)/shard_map/ppermute | solution.py:314
  209.3 7.0 %collective-permute-start.20 = (f32[128,256]{1,0:T(8,128)S(1)}, f32[128,256]{1,0:T(8,128)S(1)}, u32[]{:S(2)}, u32[]{:S(2)}) collective-permute-start(f32[128,256]{1,0:T(8,128)S(1)} %select_add_fusion.1), channel_id=1, source_target_pairs={{0,64},{64,128},{128,192},{192,0},{1,65},{65,129},{129,193},{193,1... | collective-permute-start | bytes 393224 | tf_op jit(solution)/shard_map/ppermute | solution.py:314
  221.2 24.0 %collective-permute-start.14 = (bf16[512,256]{1,0:T(8,128)(2,1)S(1)}, bf16[512,256]{1,0:T(8,128)(2,1)S(1)}, u32[]{:S(2)}, u32[]{:S(2)}) collective-permute-start(bf16[512,256]{1,0:T(8,128)(2,1)S(1)} %get-tuple-element.17), channel_id=1, source_target_pairs={{0,2},{2,4},{4,6},{6,8},{8,10},{10,12},{12,14},{14,0},{1,3},{3,5},... | collective-permute-start | bytes 786440 | tf_op jit(solution)/shard_map/ppermute | solution.py:376
  222.6 22.5 %collective-permute-start.15 = (bf16[512,256]{1,0:T(8,128)(2,1)S(1)}, bf16[512,256]{1,0:T(8,128)(2,1)S(1)}, u32[]{:S(2)}, u32[]{:S(2)}) collective-permute-start(bf16[512,256]{1,0:T(8,128)(2,1)S(1)} %get-tuple-element.18), channel_id=1, source_target_pairs={{0,14},{2,0},{4,2},{6,4},{8,6},{10,8},{12,10},{14,12},{1,15},{3,1}... | collective-permute-start | bytes 786440 | tf_op jit(solution)/shard_map/ppermute | solution.py:376
  226.6 13.1 %collective-permute-start.25 = (f32[128,256]{1,0:T(8,128)S(1)}, f32[128,256]{1,0:T(8,128)S(1)}, u32[]{:S(2)}, u32[]{:S(2)}) collective-permute-start(f32[128,256]{1,0:T(8,128)S(1)} %add.109), channel_id=1, source_target_pairs={{0,8},{2,10},{4,12},{6,14},{8,0},{10,2},{12,4},{14,6},{1,9},{3,11}... | collective-permute-start | bytes 393224 | tf_op jit(solution)/shard_map/ppermute | solution.py:341
  (20 other events, 382.2 us)
Sparse Core Ops, SparseCore 0:
  24.7 88.8 all-gather.1

commit v4 on v3

--- a/solution.py
+++ b/solution.py
@@ -126,31 +126,38 @@
     )(where, meta, ids, cols, rows, count, sent, tiles, *feats, *arrived)
 
 
-def add_grads(half, where, meta, ids, cols, rows, count, sent, grads, tiles, total):
-    z_me, r_me = where[1], where[2]
+def add_grads(where, meta, ids, cols, rows, count, sent, mine, peer, tiles, total):
+    c, z_me, r_me = where[0], where[1], where[2]
 
     def add(at, tile, r, row):
-        term = lax.dot_general(
-            tile, grads[r * 4 + lax.rem(row, 4)], (((0,), (0,)), ((), ())),
-            preferred_element_type=jnp.float32,
-        )
-        total[at] = total[at] + term
+        def go(cots):
+            term = lax.dot_general(
+                tile, cots[r * 4 + lax.rem(row, 4)], (((0,), (0,)), ((), ())), preferred_element_type=jnp.float32
+            )
+            total[at] = total[at] + term
+
+        @pl.when(lax.div(row, 4) == c)
+        def _():
+            go(mine)
+
+        @pl.when(lax.div(row, 4) != c)
+        def _():
+            go(peer)
 
     def remote(i, carry):
         r, z = lax.div(i, 8), lax.rem(i, 8)
-        row = meta[i] - 1
-
-        @pl.when((meta[i] > 0) & (lax.div(row, 4) == half))
+
+        @pl.when(meta[i] > 0)
         def _():
             step, back = jnp.bitwise_and(z - z_me + 8, 7), jnp.bitwise_and(z_me - z + 8, 7)
-            add(step * 4 + ids[back * 16 + r], sent[r, rows_at(z), :], r, row)
+            add(step * 4 + ids[back * 16 + r], sent[r, rows_at(z), :], r, meta[i] - 1)
 
         return carry
 
     lax.fori_loop(0, 128, remote, 0)
 
     def own(t, carry):
-        @pl.when((cols[t] < 4) & (lax.div(rows[t], 4) == half))
+        @pl.when(cols[t] < 4)
         def _():
             add(jnp.minimum(cols[t], 3), tiles[t], r_me, rows[t])
 
@@ -167,8 +174,7 @@
         return carry
 
     lax.fori_loop(0, total.shape[0], begin, 0)
-    add_grads(where[0], where, meta, ids, cols, rows, count, sent, mine, tiles, total)
-    add_grads(1 - where[0], where, meta, ids, cols, rows, count, sent, peer, tiles, total)
+    add_grads(where, meta, ids, cols, rows, count, sent, mine, peer, tiles, total)
     for k in range(4):
         outs[0][rows_at(k), :] = total[k]
     for step in range(1, 8):
@@ -193,7 +199,8 @@
     )(where, meta, ids, cols, rows, count, sent, mine, peer, tiles)
 
 
-def term_kernel(scale, parts, cots, term):
+def term_kernel(scale, parts, cots, after, term):
+    del after
     term[...] = jnp.zeros(term.shape, term.dtype)
 
     def product(i, carry):
@@ -206,18 +213,18 @@
     term[...] = term[...] * scale
 
 
-def weight_term(parts, cots, scale):
+def weight_term(parts, cots, after, scale):
     vmem = pl.BlockSpec(memory_space=pltpu.VMEM)
     width = parts.shape[2]
     return pl.pallas_call(
         functools.partial(term_kernel, scale),
         out_shape=jax.ShapeDtypeStruct((width, width), jnp.float32),
-        in_specs=[vmem] * 2,
+        in_specs=[vmem] * 2 + [pl.BlockSpec(memory_space=pl.ANY)],
         out_specs=vmem,
         compiler_params=pltpu.CompilerParams(vmem_limit_bytes=12 * 2**20),
         cost_estimate=cost(4),
         name="weight_term",
-    )(parts, cots)
+    )(parts, cots, after)
 
 
 def output_kernel(parts, weight, *rest):
@@ -315,30 +322,20 @@
 
 
 def mark(*arrays):
-    return jnp.concatenate([a.reshape(-1, a.shape[-1])[:META].astype(jnp.bfloat16) for a in arrays], axis=0)
-
-
-def sum_four(a, axis):
-    me = lax.axis_index(axis)
-    from_step = steps_along(a, axis, 4)
-    total = None
-    for source in range(4):
-        step = jnp.bitwise_and(me - source + 4, 3)
-        low = jnp.where(step == 0, from_step[0], from_step[1])
-        high = jnp.where(step == 2, from_step[2], from_step[3])
-        part = jnp.where(step < 2, low, high)
-        total = part if total is None else total + part
-    return total
-
-
-def sum_everywhere(term, c, after):
-    halves = term.reshape(2, 128, term.shape[1])
+    return jnp.concatenate([a.reshape(-1, a.shape[-1])[:8].astype(jnp.bfloat16) for a in arrays], axis=0)
+
+
+def sum_everywhere(term, c, after, before_last):
+    n = term.shape[1]
+    halves = term.reshape(2, 128, n)
     keep = lax.dynamic_index_in_dim(halves, c, 0, keepdims=False)
     give = lax.dynamic_index_in_dim(halves, 1 - c, 0, keepdims=False)
     half = join_later([keep + swap_cores(give)], after)
-    half = sum_four(sum_four(half, "x"), "y")
+    rows = jnp.sum(lax.all_to_all(half.reshape(16, 8, n), PLANE, 0, 0, tiled=True), axis=0)
     for step in (1, 2, 4):
-        half = half + lax.ppermute(half, "z", [(i, i ^ step) for i in range(8)])
+        rows = rows + lax.ppermute(rows, "z", [(i, i ^ step) for i in range(8)])
+    rows = join_later([rows], before_last)
+    half = lax.all_to_all(jnp.broadcast_to(rows[None], (16, 8, n)), PLANE, 0, 0, tiled=True).reshape(128, n)
     other = swap_cores(half)
     first = jnp.where(c == 0, half, other)
     second = jnp.where(c == 0, other, half)
@@ -370,15 +367,16 @@
     [cot_mine] = same_later([cot_mine], mark(both))
     own, *away = grad_parts(*operands, cot_mine, swap_cores(cot_mine), tile_values)
     by_partition = (16, 4 * BLK, width)
-    term = weight_term(both.reshape(by_partition), cot_mine.reshape(by_partition), float(1.0 / node_total**0.5))
-    term = join_later([term], mark(own))
+    scale = float(1.0 / node_total**0.5)
+    term = weight_term(both.reshape(by_partition), cot_mine.reshape(by_partition), mark(own), scale)
     arrived = [
         lax.ppermute(part, "z", [(z, (z + step) % 8) for z in range(8)])
         for step, part in sorted(enumerate(away, 1), key=lambda e: -min(e[0], 8 - e[0]))
     ]
     feature_grad = feature_from(own, arrived, weight)
-    weight_grad = sum_everywhere(term, c, mark(*arrived[:5]))
     output_rows = output_from(parts, weight)
+    gate = join_later([mark(*arrived[:5])], parts)
+    weight_grad = sum_everywhere(term, c, gate, mark(output_rows))
     return (output_rows, feature_grad, weight_grad)
 
 

time: 255 us -> 242 us (0.949)
  waiting for transfers between devices: 115 us -> 84.3 us
  blocking collectives: 0 us -> 22.8 us
  Pallas kernels: 43.4 us -> 35.9 us
  starting transfers between devices: 65.3 us -> 69.8 us
    ppermute x13 -> x7, waiting for transfers between devices: 61 us -> 34.3 us  [steps_along(): lax.ppermute(a, axis, [(i, (i + s) % size) for i in range(size)])]
    all_to_all x0 -> x2, blocking collectives: none -> 22.8 us  [the longest x1 12.8 us: sum_everywhere(): lax.all_to_all(half.reshape(16, 8, n), PLANE, 0, 0, tiled=True)]
    ppermute x3, waiting for transfers between devices: 8.73 us -> 2.84 us  [sum_everywhere(): rows = rows + lax.ppermute(rows, 'z', [(i, i ^ step) for i in range(8)])]
    pallas_call x1, Pallas kernels: 16 us -> 10.4 us  [grad_parts(): pl.pallas_call(grad_kernel, out_shape=[jax.ShapeDtypeStruct((4 * BLK, wid...]
    ppermute x4, starting transfers between devices: 3.71 us -> 9.05 us  [swap_cores(): return lax.ppermute(a, 'col', [(0, 1), (1, 0)])]
    ppermute x3, starting transfers between devices: 9.51 us -> 4.45 us  [sum_everywhere(): rows = rows + lax.ppermute(rows, 'z', [(i, i ^ step) for i in range(8)])]
    ppermute x7, waiting for transfers between devices: 34.2 us -> 30.2 us  [local(): lax.ppermute(part, 'z', [(z, (z + step) % 8) for z in range(8)])]
    ppermute x7, starting transfers between devices: 18.9 us -> 22.4 us  [local(): lax.ppermute(part, 'z', [(z, (z + step) % 8) for z in range(8)])]
  transfers between devices with their start and end apart: 30 -> 24, of which waited for: 18 -> 13; matrix products, arithmetic and copies ran while one was open for 1% -> 2% of each run, Pallas kernels for 17% -> 14%
where the time goes in v4:
time: 242 us; the launch traced here: 241 us
  waiting for transfers between devices  84.3 us (35%)
  starting transfers between devices  69.8 us (29%)
  Pallas kernels  35.9 us (15%)
  blocking collectives  22.8 us (9%)
  between operations  15 us (6%)
  local copies, waits for them, and re-layouts  11.3 us (5%)
    ppermute x7, waiting for transfers between devices, steps_along(): lax.ppermute(a, axis, [(i, (i + s) % size) for i in range(size)])  34.3 us
    ppermute x7, waiting for transfers between devices, local(): lax.ppermute(part, 'z', [(z, (z + step) % 8) for z in range(8)])  30.2 us
    ppermute x7, starting transfers between devices, local(): lax.ppermute(part, 'z', [(z, (z + step) % 8) for z in range(8)])  22.4 us
    ppermute x7, starting transfers between devices, steps_along(): lax.ppermute(a, axis, [(i, (i + s) % size) for i in range(size)])  21.5 us
    pallas_call x2, Pallas kernels, hidden_parts(): pl.pallas_call(functools.partial(hidden_kernel, not arrived), out_shape=j...  15.1 us
    all_to_all x1, blocking collectives, sum_everywhere(): lax.all_to_all(half.reshape(16, 8, n), PLANE, 0, 0, tiled=True)  12.8 us
    pallas_call x1, Pallas kernels, grad_parts(): pl.pallas_call(grad_kernel, out_shape=[jax.ShapeDtypeStruct((4 * BLK, wid...  10.4 us
    all_to_all x1, blocking collectives, sum_everywhere(): lax.all_to_all(jnp.broadcast_to(rows[None], (16, 8, n)), PLANE, 0, 0, til...  9.93 us
  transfers between devices with their start and end apart: 24, of which 13 were waited for; matrix products, arithmetic and copies ran while one was open for 2% of the time, Pallas kernels for 14%

profile of v4, /device:TPU:1, one launch (start us, length us, event | category | flops | bytes accessed | tf_op | source)
XLA Modules:
  0.0 241.0 jit_solution(10492280936771559898)
XLA Ops:
  13.7 7.8 %all-to-all-start = ((bf16[16,1040,128]{2,1,0:T(8,128)(2,1)}), bf16[16,1040,128]{2,1,0:T(8,128)(2,1)}, u32[]{:S(2)}, u32[]{:S(2)}) async-start(bf16[16,1040,128]{2,1,0:T(8,128)(2,1)} %copy-done.5), calls=%async_computation | async-start | bytes 8519680 | tf_op jit(solution)/shard_map/all_to_all | solution.py:357
  26.9 3.7 %collective-permute-start.2 = (bf16[528,256]{1,0:T(8,128)(2,1)S(1)}, bf16[528,256]{1,0:T(8,128)(2,1)S(1)}, u32[]{:S(2)}, u32[]{:S(2)}) collective-permute-start(bf16[528,256]{1,0:T(8,128)(2,1)S(1)} %fusion.1.rest_0_), channel_id=1, source_target_pairs={{0,6},{2,8},{4,10},{6,12},{8,14},{10,0},{12,2},{14,4},{1,7},{3,9},... | collective-permute-start | bytes 811016 | tf_op jit(solution)/shard_map/ppermute | solution.py:321
  31.1 4.5 %collective-permute-start.4 = (bf16[528,256]{1,0:T(8,128)(2,1)S(1)}, bf16[528,256]{1,0:T(8,128)(2,1)S(1)}, u32[]{:S(2)}, u32[]{:S(2)}) collective-permute-start(bf16[528,256]{1,0:T(8,128)(2,1)S(1)} %fusion.1.rest_0_), channel_id=1, source_target_pairs={{0,10},{2,12},{4,14},{6,0},{8,2},{10,4},{12,6},{14,8},{1,11},{3,13... | collective-permute-start | bytes 811016 | tf_op jit(solution)/shard_map/ppermute | solution.py:321
  41.6 5.8 %collective-permute-start.6 = (bf16[528,256]{1,0:T(8,128)(2,1)S(1)}, bf16[528,256]{1,0:T(8,128)(2,1)S(1)}, u32[]{:S(2)}, u32[]{:S(2)}) collective-permute-start(bf16[528,256]{1,0:T(8,128)(2,1)S(1)} %fusion.1.rest_0_), channel_id=1, source_target_pairs={{0,14},{2,0},{4,2},{6,4},{8,6},{10,8},{12,10},{14,12},{1,15},{3,1}... | collective-permute-start | bytes 811016 | tf_op jit(solution)/shard_map/ppermute | solution.py:321
  47.5 12.6 %collective-permute-done.2.rest_3_ = bf16[528,256]{1,0:T(8,128)(2,1)S(1)} collective-permute-done((bf16[528,256]{1,0:T(8,128)(2,1)S(1)}, bf16[528,256]{1,0:T(8,128)(2,1)S(1)}, u32[]{:S(2)}, u32[]{:S(2)}) %collective-permute-start.2) | collective-permute-done | bytes 270368 | tf_op jit(solution)/shard_map/ppermute | solution.py:321
  60.2 8.0 %collective-permute-done.3.rest_4_ = bf16[528,256]{1,0:T(8,128)(2,1)S(1)} collective-permute-done((bf16[528,256]{1,0:T(8,128)(2,1)S(1)}, bf16[528,256]{1,0:T(8,128)(2,1)S(1)}, u32[]{:S(2)}, u32[]{:S(2)}) %collective-permute-start.3) | collective-permute-done | bytes 270368 | tf_op jit(solution)/shard_map/ppermute | solution.py:321
  68.7 7.5 %collective-permute-done.5.rest_6_ = bf16[528,256]{1,0:T(8,128)(2,1)S(1)} collective-permute-done((bf16[528,256]{1,0:T(8,128)(2,1)S(1)}, bf16[528,256]{1,0:T(8,128)(2,1)S(1)}, u32[]{:S(2)}, u32[]{:S(2)}) %collective-permute-start.5) | collective-permute-done | bytes 270368 | tf_op jit(solution)/shard_map/ppermute | solution.py:321
  79.6 6.5 %all-to-all-done.sent = bf16[16,1040,128]{2,1,0:T(8,128)(2,1)} async-done(((bf16[16,1040,128]{2,1,0:T(8,128)(2,1)}), bf16[16,1040,128]{2,1,0:T(8,128)(2,1)}, u32[]{:S(2)}, u32[]{:S(2)}) %all-to-all-start) | async-done | bytes 4259872 | tf_op jit(solution)/shard_map/all_to_all | solution.py:357
  87.0 7.1 %hidden_for_other_core.1 = bf16[64,128,256]{2,1,0:T(8,128)(2,1)S(1)} custom-call(s32[5]{0:T(128)S(1)} %stack.42.where, s32[128]{0:T(128)S(1)} %reshape.54.meta, s32[128]{0:T(128)S(1)} %reshape.46.ids, s32[40]{0:T(128)S(1)} %copy-done.8, s32[40]{0:T(128)S(1)} %copy-done.10, s32[1]{0:T(128)S(6)} %copy.24.count, bf16[16,1040,128]{2,1,0:T(8,128)(2,1)} %all-to-all-done.sent, ...), custom_call_target="tpu_custom_call" | custom-call | flops 1000000000 | bytes 30000000 | tf_op jit(solution)/shard_map/hidden_for_other_core/pallas_call | solution.py:117
  97.0 6.8 %collective-permute-done.7.rest_8_ = bf16[64,128,256]{2,1,0:T(8,128)(2,1)S(1)} collective-permute-done((bf16[64,128,256]{2,1,0:T(8,128)(2,1)S(1)}, bf16[64,128,256]{2,1,0:T(8,128)(2,1)S(1)}, u32[]{:S(2)}, u32[]{:S(2)}) %collective-permute-start.7) | collective-permute-done | bytes 4194336 | tf_op jit(solution)/shard_map/ppermute | solution.py:317
  103.8 8.0 %hidden_sums.1 = bf16[64,128,256]{2,1,0:T(8,128)(2,1)S(1)} custom-call(s32[5]{0:T(128)S(1)} %stack.42.where, s32[128]{0:T(128)S(1)} %reshape.54.meta, s32[128]{0:T(128)S(1)} %reshape.46.ids, s32[40]{0:T(128)S(1)} %copy-done.8, s32[40]{0:T(128)S(1)} %copy-done.10, s32[1]{0:T(128)S(6)} %copy.24.count, bf16[16,1040,128]{2,1,0:T(8,128)(2,1)} %all-to-all-done.sent, ...), custom_call_target="tpu_custom_call" | custom-call | flops 1000000000 | bytes 30000000 | tf_op jit(solution)/shard_map/hidden_sums/pallas_call | solution.py:117
  114.4 4.6 %all-to-all-start.1 = ((bf16[16,512,256]{2,1,0:T(8,128)(2,1)}), bf16[16,512,256]{2,1,0:T(8,128)(2,1)}, u32[]{:S(2)}, u32[]{:S(2)}) async-start(bf16[16,512,256]{2,1,0:T(8,128)(2,1)} %bitcast.19), calls=%async_computation.1 | async-start | bytes 8388608 | tf_op jit(solution)/shard_map/all_to_all | solution.py:366
  124.1 10.4 %grad_sums.1 = (f32[512,256]{1,0:T(8,128)S(1)}, bf16[512,256]{1,0:T(8,128)(2,1)S(1)}, bf16[512,256]{1,0:T(8,128)(2,1)}, bf16[512,256]{1,0:T(8,128)(2,1)}, bf16[5...) custom-call(s32[5]{0:T(128)S(1)} %stack.42.where, ...), custom_call_target="tpu_custom_call" | custom-call | flops 800000000 | bytes 24000000 | tf_op jit(solution)/shard_map/grad_sums/pallas_call | solution.py:189
  134.5 4.4 %weight_term.1 = f32[256,256]{1,0:T(8,128)S(1)} custom-call(bf16[16,512,256]{2,1,0:T(8,128)(2,1)S(1)} %bitcast.20, bf16[16,512,256]{2,1,0:T(8,128)(2,1)S(1)} %bitcast.21, bf16[8,256]{1,0:T(8,128)(2,1)S(1)} %slice.98.after), custom_call_target="tpu_custom_call" | custom-call | flops 400000000 | bytes 12000000 | tf_op jit(solution)/shard_map/weight_term/pallas_call | solution.py:219
  139.9 11.5 %collective-permute-start.9 = (bf16[512,256]{1,0:T(8,128)(2,1)}, bf16[512,256]{1,0:T(8,128)(2,1)S(1)}, u32[]{:S(2)}, u32[]{:S(2)}) collective-permute-start(bf16[512,256]{1,0:T(8,128)(2,1)} %get-tuple-element.12), channel_id=1, source_target_pairs={{0,8},{2,10},{4,12},{6,14},{8,0},{10,2},{12,4},{14,6},{1,9},{3,11}... | collective-permute-start | bytes 786440 | tf_op jit(solution)/shard_map/ppermute | solution.py:373
  152.0 3.8 %collective-permute-start.11 = (bf16[512,256]{1,0:T(8,128)(2,1)}, bf16[512,256]{1,0:T(8,128)(2,1)S(1)}, u32[]{:S(2)}, u32[]{:S(2)}) collective-permute-start(bf16[512,256]{1,0:T(8,128)(2,1)} %get-tuple-element.14), channel_id=1, source_target_pairs={{0,10},{2,12},{4,14},{6,0},{8,2},{10,4},{12,6},{14,8},{1,11},{3,13... | collective-permute-start | bytes 786440 | tf_op jit(solution)/shard_map/ppermute | solution.py:373
  155.8 3.6 %collective-permute-start.13 = (bf16[512,256]{1,0:T(8,128)(2,1)S(1)}, bf16[512,256]{1,0:T(8,128)(2,1)S(1)}, u32[]{:S(2)}, u32[]{:S(2)}) collective-permute-start(bf16[512,256]{1,0:T(8,128)(2,1)S(1)} %get-tuple-element.16), channel_id=1, source_target_pairs={{0,12},{2,14},{4,0},{6,2},{8,4},{10,6},{12,8},{14,10},{1,13},{3,15... | collective-permute-start | bytes 786440 | tf_op jit(solution)/shard_map/ppermute | solution.py:373
  160.6 23.3 %collective-permute-done.10.rest_1_ = bf16[512,256]{1,0:T(8,128)(2,1)S(1)} collective-permute-done((bf16[512,256]{1,0:T(8,128)(2,1)}, bf16[512,256]{1,0:T(8,128)(2,1)S(1)}, u32[]{:S(2)}, u32[]{:S(2)}) %collective-permute-start.10) | collective-permute-done | bytes 262176 | tf_op jit(solution)/shard_map/ppermute | solution.py:373
  184.0 5.7 %collective-permute-done.13.rest_4_ = bf16[512,256]{1,0:T(8,128)(2,1)S(1)} collective-permute-done((bf16[512,256]{1,0:T(8,128)(2,1)S(1)}, bf16[512,256]{1,0:T(8,128)(2,1)S(1)}, u32[]{:S(2)}, u32[]{:S(2)}) %collective-permute-start.13) | collective-permute-done | bytes 262176 | tf_op jit(solution)/shard_map/ppermute | solution.py:373
  189.7 12.8 %all_to_all.20 = f32[16,8,256]{2,1,0:T(8,128)S(1)} all-to-all(f32[16,8,256]{2,1,0:T(8,128)S(1)} %bitcast.24), channel_id=1, replica_groups=mesh['y'=4,'x'=4,'z'=8,'col'=2] {'y','x'}, dimensions={0} | all-to-all | bytes 262144 | tf_op jit(solution)/shard_map/all_to_all | solution.py:334
  208.6 4.2 %collective-permute-start.19 = (f32[8,256]{1,0:T(8,128)S(1)}, f32[8,256]{1,0:T(8,128)S(1)}, u32[]{:S(2)}, u32[]{:S(2)}) collective-permute-start(f32[8,256]{1,0:T(8,128)S(1)} %add.35), channel_id=1, source_target_pairs={{0,8},{2,10},{4,12},{6,14},{8,0},{10,2},{12,4},{14,6},{1,9},{3,11}... | collective-permute-start | bytes 24584 | tf_op jit(solution)/shard_map/ppermute | solution.py:336
  212.7 3.6 %output_rows.1 = bf16[512,256]{1,0:T(8,128)(2,1)} custom-call(bf16[16,512,256]{2,1,0:T(8,128)(2,1)} %all-to-all-done.1.parts.refs_1_, bf16[256,256]{1,0:T(8,128)(2,1)S(1)} %copy-done.6), custom_call_target="tpu_custom_call" | custom-call | flops 400000000 | bytes 12000000 | tf_op jit(solution)/shard_map/output_rows/pallas_call | solution.py:241
  217.0 9.9 %all_to_all.21 = f32[16,8,256]{2,1,0:T(8,128)S(1)} all-to-all(f32[16,8,256]{2,1,0:T(8,128)S(1)} %broadcast_in_dim.2), channel_id=1, replica_groups=mesh['y'=4,'x'=4,'z'=8,'col'=2] {'y','x'}, dimensions={0} | all-to-all | bytes 262144 | tf_op jit(solution)/shard_map/all_to_all | solution.py:338
  226.9 5.3 %collective-permute-start.20 = (f32[128,256]{1,0:T(8,128)S(1)}, f32[128,256]{1,0:T(8,128)S(1)}, u32[]{:S(2)}, u32[]{:S(2)}) collective-permute-start(f32[128,256]{1,0:T(8,128)S(1)} %bitcast.25), channel_id=1, source_target_pairs={{0,1},{1,0},{2,3},{3,2},{4,5},{5,4},{6,7},{7,6},{8,9},{9,8},{10,11... | collective-permute-start | bytes 393224 | tf_op jit(solution)/shard_map/ppermute | solution.py:317
  (112 shorter events, 44.5 us)
Async XLA Ops:
  13.7 72.5 %all-to-all-start = ((bf16[16,1040,128]{2,1,0:T(8,128)(2,1)}), bf16[16,1040,128]{2,1,0:T(8,128)(2,1)}, u32[]{:S(2)}, u32[]{:S(2)}) async-start(bf16[16,1040,128]{2,1,0:T(8,128)(2,1)} %copy-done.5), calls=%async_computation | async-start | bytes 8519680 | tf_op jit(solution)/shard_map/all_to_all | solution.py:357
  21.5 92.9 %all-gather.2.cloned.1.call-start = ((), (), s32[]{:S(2)}) async-start(), calls=%async_computation.4 | async-start | bytes 4456448 | tf_op jit(solution)/shard_map/all_gather | solution.py:355
  22.3 13.5 %collective-permute-start = (bf16[528,256]{1,0:T(8,128)(2,1)S(1)}, bf16[528,256]{1,0:T(8,128)(2,1)S(1)}, u32[]{:S(2)}, u32[]{:S(2)}) collective-permute-start(bf16[528,256]{1,0:T(8,128)(2,1)S(1)} %fusion.1.rest_0_), channel_id=1, source_target_pairs={{0,2},{2,4},{4,6},{6,8},{8,10},{10,12},{12,14},{14,0},{1,3},{3,5},... | collective-permute-start | bytes 811016 | tf_op jit(solution)/shard_map/ppermute | solution.py:321
  24.0 17.6 %collective-permute-start.1 = (bf16[528,256]{1,0:T(8,128)(2,1)S(1)}, bf16[528,256]{1,0:T(8,128)(2,1)S(1)}, u32[]{:S(2)}, u32[]{:S(2)}) collective-permute-start(bf16[528,256]{1,0:T(8,128)(2,1)S(1)} %fusion.1.rest_0_), channel_id=1, source_target_pairs={{0,4},{2,6},{4,8},{6,10},{8,12},{10,14},{12,0},{14,2},{1,5},{3,7},... | collective-permute-start | bytes 811016 | tf_op jit(solution)/shard_map/ppermute | solution.py:321
  26.9 33.2 %collective-permute-start.2 = (bf16[528,256]{1,0:T(8,128)(2,1)S(1)}, bf16[528,256]{1,0:T(8,128)(2,1)S(1)}, u32[]{:S(2)}, u32[]{:S(2)}) collective-permute-start(bf16[528,256]{1,0:T(8,128)(2,1)S(1)} %fusion.1.rest_0_), channel_id=1, source_target_pairs={{0,6},{2,8},{4,10},{6,12},{8,14},{10,0},{12,2},{14,4},{1,7},{3,9},... | collective-permute-start | bytes 811016 | tf_op jit(solution)/shard_map/ppermute | solution.py:321
  30.6 37.6 %collective-permute-start.3 = (bf16[528,256]{1,0:T(8,128)(2,1)S(1)}, bf16[528,256]{1,0:T(8,128)(2,1)S(1)}, u32[]{:S(2)}, u32[]{:S(2)}) collective-permute-start(bf16[528,256]{1,0:T(8,128)(2,1)S(1)} %fusion.1.rest_0_), channel_id=1, source_target_pairs={{0,8},{2,10},{4,12},{6,14},{8,0},{10,2},{12,4},{14,6},{1,9},{3,11}... | collective-permute-start | bytes 811016 | tf_op jit(solution)/shard_map/ppermute | solution.py:321
  31.1 37.5 %collective-permute-start.4 = (bf16[528,256]{1,0:T(8,128)(2,1)S(1)}, bf16[528,256]{1,0:T(8,128)(2,1)S(1)}, u32[]{:S(2)}, u32[]{:S(2)}) collective-permute-start(bf16[528,256]{1,0:T(8,128)(2,1)S(1)} %fusion.1.rest_0_), channel_id=1, source_target_pairs={{0,10},{2,12},{4,14},{6,0},{8,2},{10,4},{12,6},{14,8},{1,11},{3,13... | collective-permute-start | bytes 811016 | tf_op jit(solution)/shard_map/ppermute | solution.py:321
  35.8 40.4 %collective-permute-start.5 = (bf16[528,256]{1,0:T(8,128)(2,1)S(1)}, bf16[528,256]{1,0:T(8,128)(2,1)S(1)}, u32[]{:S(2)}, u32[]{:S(2)}) collective-permute-start(bf16[528,256]{1,0:T(8,128)(2,1)S(1)} %fusion.1.rest_0_), channel_id=1, source_target_pairs={{0,12},{2,14},{4,0},{6,2},{8,4},{10,6},{12,8},{14,10},{1,13},{3,15... | collective-permute-start | bytes 811016 | tf_op jit(solution)/shard_map/ppermute | solution.py:321
  41.6 37.4 %collective-permute-start.6 = (bf16[528,256]{1,0:T(8,128)(2,1)S(1)}, bf16[528,256]{1,0:T(8,128)(2,1)S(1)}, u32[]{:S(2)}, u32[]{:S(2)}) collective-permute-start(bf16[528,256]{1,0:T(8,128)(2,1)S(1)} %fusion.1.rest_0_), channel_id=1, source_target_pairs={{0,14},{2,0},{4,2},{6,4},{8,6},{10,8},{12,10},{14,12},{1,15},{3,1}... | collective-permute-start | bytes 811016 | tf_op jit(solution)/shard_map/ppermute | solution.py:321
  94.2 9.7 %collective-permute-start.7 = (bf16[64,128,256]{2,1,0:T(8,128)(2,1)S(1)}, bf16[64,128,256]{2,1,0:T(8,128)(2,1)S(1)}, u32[]{:S(2)}, u32[]{:S(2)}) collective-permute-start(bf16[64,128,256]{2,1,0:T(8,128)(2,1)S(1)} %hidden_for_other_core.1), channel_id=1, source_target_pairs={{0,1},{1,0},{2,3},{3,2},{4,5},{5,4},{6,7},{7,6},{8,9},{9,8},{10,11... | collective-permute-start | bytes 12582920 | tf_op jit(solution)/shard_map/ppermute | solution.py:317
  114.4 7.5 %collective-permute-start.8 = (bf16[64,128,256]{2,1,0:T(8,128)(2,1)}, bf16[64,128,256]{2,1,0:T(8,128)(2,1)}, u32[]{:S(2)}, u32[]{:S(2)}) collective-permute-start(bf16[64,128,256]{2,1,0:T(8,128)(2,1)} %in_order_in_place.1.mine), channel_id=1, source_target_pairs={{0,1},{1,0},{2,3},{3,2},{4,5},{5,4},{6,7},{7,6},{8,9},{9,8},{10,11... | collective-permute-start | bytes 12582920 | tf_op jit(solution)/shard_map/ppermute | solution.py:317
  114.4 75.3 %all-to-all-start.1 = ((bf16[16,512,256]{2,1,0:T(8,128)(2,1)}), bf16[16,512,256]{2,1,0:T(8,128)(2,1)}, u32[]{:S(2)}, u32[]{:S(2)}) async-start(bf16[16,512,256]{2,1,0:T(8,128)(2,1)} %bitcast.19), calls=%async_computation.1 | async-start | bytes 8388608 | tf_op jit(solution)/shard_map/all_to_all | solution.py:366
  139.0 16.8 %collective-permute-start.16 = (f32[128,256]{1,0:T(8,128)S(1)}, f32[128,256]{1,0:T(8,128)S(1)}, u32[]{:S(2)}, u32[]{:S(2)}) collective-permute-start(f32[128,256]{1,0:T(8,128)S(1)} %dynamic-slice_bitcast_fusion), channel_id=1, source_target_pairs={{0,1},{1,0},{2,3},{3,2},{4,5},{5,4},{6,7},{7,6},{8,9},{9,8},{10,11... | collective-permute-start | bytes 393224 | tf_op jit(solution)/shard_map/ppermute | solution.py:317
  139.9 20.7 %collective-permute-start.9 = (bf16[512,256]{1,0:T(8,128)(2,1)}, bf16[512,256]{1,0:T(8,128)(2,1)S(1)}, u32[]{:S(2)}, u32[]{:S(2)}) collective-permute-start(bf16[512,256]{1,0:T(8,128)(2,1)} %get-tuple-element.12), channel_id=1, source_target_pairs={{0,8},{2,10},{4,12},{6,14},{8,0},{10,2},{12,4},{14,6},{1,9},{3,11}... | collective-permute-start | bytes 786440 | tf_op jit(solution)/shard_map/ppermute | solution.py:373
  151.4 32.6 %collective-permute-start.10 = (bf16[512,256]{1,0:T(8,128)(2,1)}, bf16[512,256]{1,0:T(8,128)(2,1)S(1)}, u32[]{:S(2)}, u32[]{:S(2)}) collective-permute-start(bf16[512,256]{1,0:T(8,128)(2,1)} %get-tuple-element.13), channel_id=1, source_target_pairs={{0,6},{2,8},{4,10},{6,12},{8,14},{10,0},{12,2},{14,4},{1,7},{3,9},... | collective-permute-start | bytes 786440 | tf_op jit(solution)/shard_map/ppermute | solution.py:373
  152.0 31.9 %collective-permute-start.11 = (bf16[512,256]{1,0:T(8,128)(2,1)}, bf16[512,256]{1,0:T(8,128)(2,1)S(1)}, u32[]{:S(2)}, u32[]{:S(2)}) collective-permute-start(bf16[512,256]{1,0:T(8,128)(2,1)} %get-tuple-element.14), channel_id=1, source_target_pairs={{0,10},{2,12},{4,14},{6,0},{8,2},{10,4},{12,6},{14,8},{1,11},{3,13... | collective-permute-start | bytes 786440 | tf_op jit(solution)/shard_map/ppermute | solution.py:373
  155.8 28.1 %collective-permute-start.12 = (bf16[512,256]{1,0:T(8,128)(2,1)}, bf16[512,256]{1,0:T(8,128)(2,1)S(1)}, u32[]{:S(2)}, u32[]{:S(2)}) collective-permute-start(bf16[512,256]{1,0:T(8,128)(2,1)} %get-tuple-element.15), channel_id=1, source_target_pairs={{0,4},{2,6},{4,8},{6,10},{8,12},{10,14},{12,0},{14,2},{1,5},{3,7},... | collective-permute-start | bytes 786440 | tf_op jit(solution)/shard_map/ppermute | solution.py:373
  155.8 33.8 %collective-permute-start.13 = (bf16[512,256]{1,0:T(8,128)(2,1)S(1)}, bf16[512,256]{1,0:T(8,128)(2,1)S(1)}, u32[]{:S(2)}, u32[]{:S(2)}) collective-permute-start(bf16[512,256]{1,0:T(8,128)(2,1)S(1)} %get-tuple-element.16), channel_id=1, source_target_pairs={{0,12},{2,14},{4,0},{6,2},{8,4},{10,6},{12,8},{14,10},{1,13},{3,15... | collective-permute-start | bytes 786440 | tf_op jit(solution)/shard_map/ppermute | solution.py:373
  202.6 2.6 %collective-permute-start.17 = (f32[8,256]{1,0:T(8,128)S(1)}, f32[8,256]{1,0:T(8,128)S(1)}, u32[]{:S(2)}, u32[]{:S(2)}) collective-permute-start(f32[8,256]{1,0:T(8,128)S(1)} %reduce_sum.9), channel_id=1, source_target_pairs={{0,2},{2,0},{4,6},{6,4},{8,10},{10,8},{12,14},{14,12},{1,3},{3,1},... | collective-permute-start | bytes 24584 | tf_op jit(solution)/shard_map/ppermute | solution.py:336
  205.1 3.4 %collective-permute-start.18 = (f32[8,256]{1,0:T(8,128)S(1)}, f32[8,256]{1,0:T(8,128)S(1)}, u32[]{:S(2)}, u32[]{:S(2)}) collective-permute-start(f32[8,256]{1,0:T(8,128)S(1)} %add.34), channel_id=1, source_target_pairs={{0,4},{2,6},{4,0},{6,2},{8,12},{10,14},{12,8},{14,10},{1,5},{3,7},... | collective-permute-start | bytes 24584 | tf_op jit(solution)/shard_map/ppermute | solution.py:336
  205.3 26.9 %collective-permute-start.14 = (bf16[512,256]{1,0:T(8,128)(2,1)S(1)}, bf16[512,256]{1,0:T(8,128)(2,1)S(1)}, u32[]{:S(2)}, u32[]{:S(2)}) collective-permute-start(bf16[512,256]{1,0:T(8,128)(2,1)S(1)} %get-tuple-element.17), channel_id=1, source_target_pairs={{0,2},{2,4},{4,6},{6,8},{8,10},{10,12},{12,14},{14,0},{1,3},{3,5},... | collective-permute-start | bytes 786440 | tf_op jit(solution)/shard_map/ppermute | solution.py:373
  206.3 26.0 %collective-permute-start.15 = (bf16[512,256]{1,0:T(8,128)(2,1)S(1)}, bf16[512,256]{1,0:T(8,128)(2,1)S(1)}, u32[]{:S(2)}, u32[]{:S(2)}) collective-permute-start(bf16[512,256]{1,0:T(8,128)(2,1)S(1)} %get-tuple-element.18), channel_id=1, source_target_pairs={{0,14},{2,0},{4,2},{6,4},{8,6},{10,8},{12,10},{14,12},{1,15},{3,1}... | collective-permute-start | bytes 786440 | tf_op jit(solution)/shard_map/ppermute | solution.py:373
  208.6 8.4 %collective-permute-start.19 = (f32[8,256]{1,0:T(8,128)S(1)}, f32[8,256]{1,0:T(8,128)S(1)}, u32[]{:S(2)}, u32[]{:S(2)}) collective-permute-start(f32[8,256]{1,0:T(8,128)S(1)} %add.35), channel_id=1, source_target_pairs={{0,8},{2,10},{4,12},{6,14},{8,0},{10,2},{12,4},{14,6},{1,9},{3,11}... | collective-permute-start | bytes 24584 | tf_op jit(solution)/shard_map/ppermute | solution.py:336
  226.9 6.5 %collective-permute-start.20 = (f32[128,256]{1,0:T(8,128)S(1)}, f32[128,256]{1,0:T(8,128)S(1)}, u32[]{:S(2)}, u32[]{:S(2)}) collective-permute-start(f32[128,256]{1,0:T(8,128)S(1)} %bitcast.25), channel_id=1, source_target_pairs={{0,1},{1,0},{2,3},{3,2},{4,5},{5,4},{6,7},{7,6},{8,9},{9,8},{10,11... | collective-permute-start | bytes 393224 | tf_op jit(solution)/shard_map/ppermute | solution.py:317
  (13 other events, 335.4 us)
Sparse Core Ops, SparseCore 0:
  24.7 87.8 all-gather.1

commit v5 on v4

--- a/solution.py
+++ b/solution.py
@@ -92,7 +92,7 @@
 
             return carry
 
-        lax.fori_loop(0, 16, remote, 0)
+        lax.fori_loop(0, 16, remote, 0, unroll=2)
 
     def own(t, carry):
         @pl.when((cols[t] < 4) & (lax.div(rows[t], 4) == half))
@@ -154,7 +154,7 @@
 
         return carry
 
-    lax.fori_loop(0, 128, remote, 0)
+    lax.fori_loop(0, 128, remote, 0, unroll=4)
 
     def own(t, carry):
         @pl.when(cols[t] < 4)
@@ -325,6 +325,18 @@
     return jnp.concatenate([a.reshape(-1, a.shape[-1])[:8].astype(jnp.bfloat16) for a in arrays], axis=0)
 
 
+def sum_of_eight(rows):
+    rows = rows + lax.ppermute(rows, "z", [(i, i ^ 1) for i in range(8)])
+    found = [rows] + [lax.ppermute(rows, "z", [(i, i ^ k) for i in range(8)]) for k in (2, 4, 6)]
+    me = lax.div(lax.axis_index("z"), 2)
+    total = None
+    for pair in range(4):
+        k = jnp.bitwise_xor(me, pair)
+        part = jnp.where(k < 2, jnp.where(k == 0, found[0], found[1]), jnp.where(k == 2, found[2], found[3]))
+        total = part if total is None else total + part
+    return total
+
+
 def sum_everywhere(term, c, after, before_last):
     n = term.shape[1]
     halves = term.reshape(2, 128, n)
@@ -332,8 +344,7 @@
     give = lax.dynamic_index_in_dim(halves, 1 - c, 0, keepdims=False)
     half = join_later([keep + swap_cores(give)], after)
     rows = jnp.sum(lax.all_to_all(half.reshape(16, 8, n), PLANE, 0, 0, tiled=True), axis=0)
-    for step in (1, 2, 4):
-        rows = rows + lax.ppermute(rows, "z", [(i, i ^ step) for i in range(8)])
+    rows = sum_of_eight(rows)
     rows = join_later([rows], before_last)
     half = lax.all_to_all(jnp.broadcast_to(rows[None], (16, 8, n)), PLANE, 0, 0, tiled=True).reshape(128, n)
     other = swap_cores(half)
@@ -368,11 +379,11 @@
     own, *away = grad_parts(*operands, cot_mine, swap_cores(cot_mine), tile_values)
     by_partition = (16, 4 * BLK, width)
     scale = float(1.0 / node_total**0.5)
-    term = weight_term(both.reshape(by_partition), cot_mine.reshape(by_partition), mark(own), scale)
     arrived = [
         lax.ppermute(part, "z", [(z, (z + step) % 8) for z in range(8)])
         for step, part in sorted(enumerate(away, 1), key=lambda e: -min(e[0], 8 - e[0]))
     ]
+    term = weight_term(both.reshape(by_partition), cot_mine.reshape(by_partition), mark(arrived[0]), scale)
     feature_grad = feature_from(own, arrived, weight)
     output_rows = output_from(parts, weight)
     gate = join_later([mark(*arrived[:5])], parts)

time: 242 us -> 240 us (level)
  waiting for transfers between devices: 84.3 us -> 68 us
  starting transfers between devices: 69.8 us -> 80.7 us
  local copies, waits for them, and re-layouts: 11.3 us -> 16.4 us
    ppermute x7, waiting for transfers between devices: 30.2 us -> 13.9 us  [local(): lax.ppermute(part, 'z', [(z, (z + step) % 8) for z in range(8)])]
    ppermute x4, starting transfers between devices: 9.05 us -> 18.6 us  [swap_cores(): return lax.ppermute(a, 'col', [(0, 1), (1, 0)])]
    unnamed x37 -> x39, local copies, waits for them, and re-layouts: 8.87 us -> 13.2 us
    ppermute x3 -> x4, starting transfers between devices: 4.45 us -> 8.33 us  [the longest x3 8.24 us: sum_of_eight(): lax.ppermute(rows, 'z', [(i, i ^ k) for i in range(8)])]
    ppermute x7, starting transfers between devices: 22.4 us -> 19.6 us  [local(): lax.ppermute(part, 'z', [(z, (z + step) % 8) for z in range(8)])]
  transfers between devices with their start and end apart: 24 -> 25, of which waited for: 13 -> 12; matrix products, arithmetic and copies ran while one was open for 2% -> 2% of each run, Pallas kernels for 14% -> 15%
where the time goes in v5:
time: 240 us; the launch traced here: 239 us
  starting transfers between devices  80.7 us (34%)
  waiting for transfers between devices  68 us (28%)
  Pallas kernels  36.3 us (15%)
  blocking collectives  20.9 us (9%)
  local copies, waits for them, and re-layouts  16.4 us (7%)
  between operations  15 us (6%)
    ppermute x7, waiting for transfers between devices, steps_along(): lax.ppermute(a, axis, [(i, (i + s) % size) for i in range(size)])  34.1 us
    ppermute x7, starting transfers between devices, steps_along(): lax.ppermute(a, axis, [(i, (i + s) % size) for i in range(size)])  21.6 us
    ppermute x7, starting transfers between devices, local(): lax.ppermute(part, 'z', [(z, (z + step) % 8) for z in range(8)])  19.6 us
    ppermute x4, starting transfers between devices, swap_cores(): return lax.ppermute(a, 'col', [(0, 1), (1, 0)])  18.6 us
    pallas_call x2, Pallas kernels, hidden_parts(): pl.pallas_call(functools.partial(hidden_kernel, not arrived), out_shape=j...  15.1 us
    ppermute x7, waiting for transfers between devices, local(): lax.ppermute(part, 'z', [(z, (z + step) % 8) for z in range(8)])  13.9 us
    unnamed x39, local copies, waits for them, and re-layouts  13.2 us
    pallas_call x1, Pallas kernels, grad_parts(): pl.pallas_call(grad_kernel, out_shape=[jax.ShapeDtypeStruct((4 * BLK, wid...  11 us
  transfers between devices with their start and end apart: 25, of which 12 were waited for; matrix products, arithmetic and copies ran while one was open for 2% of the time, Pallas kernels for 15%

profile of v5, /device:TPU:1, one launch (start us, length us, event | category | flops | bytes accessed | tf_op | source)
XLA Modules:
  0.0 239.1 jit_solution(3606290440783967837)
XLA Ops:
  13.5 8.0 %all-to-all-start = ((bf16[16,1040,128]{2,1,0:T(8,128)(2,1)}), bf16[16,1040,128]{2,1,0:T(8,128)(2,1)}, u32[]{:S(2)}, u32[]{:S(2)}) async-start(bf16[16,1040,128]{2,1,0:T(8,128)(2,1)} %copy-done.6), calls=%async_computation | async-start | bytes 8519680 | tf_op jit(solution)/shard_map/all_to_all | solution.py:368
  26.8 3.9 %collective-permute-start.2 = (bf16[528,256]{1,0:T(8,128)(2,1)S(1)}, bf16[528,256]{1,0:T(8,128)(2,1)S(1)}, u32[]{:S(2)}, u32[]{:S(2)}) collective-permute-start(bf16[528,256]{1,0:T(8,128)(2,1)S(1)} %fusion.1.rest_0_), channel_id=1, source_target_pairs={{0,6},{2,8},{4,10},{6,12},{8,14},{10,0},{12,2},{14,4},{1,7},{3,9},... | collective-permute-start | bytes 811016 | tf_op jit(solution)/shard_map/ppermute | solution.py:321
  31.4 4.5 %collective-permute-start.4 = (bf16[528,256]{1,0:T(8,128)(2,1)S(1)}, bf16[528,256]{1,0:T(8,128)(2,1)S(1)}, u32[]{:S(2)}, u32[]{:S(2)}) collective-permute-start(bf16[528,256]{1,0:T(8,128)(2,1)S(1)} %fusion.1.rest_0_), channel_id=1, source_target_pairs={{0,10},{2,12},{4,14},{6,0},{8,2},{10,4},{12,6},{14,8},{1,11},{3,13... | collective-permute-start | bytes 811016 | tf_op jit(solution)/shard_map/ppermute | solution.py:321
  38.1 4.0 %collective-permute-done.1.rest_2_ = bf16[528,256]{1,0:T(8,128)(2,1)S(1)} collective-permute-done((bf16[528,256]{1,0:T(8,128)(2,1)S(1)}, bf16[528,256]{1,0:T(8,128)(2,1)S(1)}, u32[]{:S(2)}, u32[]{:S(2)}) %collective-permute-start.1) | collective-permute-done | bytes 270368 | tf_op jit(solution)/shard_map/ppermute | solution.py:321
  42.1 6.1 %collective-permute-start.6 = (bf16[528,256]{1,0:T(8,128)(2,1)S(1)}, bf16[528,256]{1,0:T(8,128)(2,1)S(1)}, u32[]{:S(2)}, u32[]{:S(2)}) collective-permute-start(bf16[528,256]{1,0:T(8,128)(2,1)S(1)} %fusion.1.rest_0_), channel_id=1, source_target_pairs={{0,14},{2,0},{4,2},{6,4},{8,6},{10,8},{12,10},{14,12},{1,15},{3,1}... | collective-permute-start | bytes 811016 | tf_op jit(solution)/shard_map/ppermute | solution.py:321
  48.2 14.8 %collective-permute-done.2.rest_3_ = bf16[528,256]{1,0:T(8,128)(2,1)S(1)} collective-permute-done((bf16[528,256]{1,0:T(8,128)(2,1)S(1)}, bf16[528,256]{1,0:T(8,128)(2,1)S(1)}, u32[]{:S(2)}, u32[]{:S(2)}) %collective-permute-start.2) | collective-permute-done | bytes 270368 | tf_op jit(solution)/shard_map/ppermute | solution.py:321
  63.1 4.9 %collective-permute-done.3.rest_4_ = bf16[528,256]{1,0:T(8,128)(2,1)S(1)} collective-permute-done((bf16[528,256]{1,0:T(8,128)(2,1)S(1)}, bf16[528,256]{1,0:T(8,128)(2,1)S(1)}, u32[]{:S(2)}, u32[]{:S(2)}) %collective-permute-start.3) | collective-permute-done | bytes 270368 | tf_op jit(solution)/shard_map/ppermute | solution.py:321
  68.5 7.8 %collective-permute-done.5.rest_6_ = bf16[528,256]{1,0:T(8,128)(2,1)S(1)} collective-permute-done((bf16[528,256]{1,0:T(8,128)(2,1)S(1)}, bf16[528,256]{1,0:T(8,128)(2,1)S(1)}, u32[]{:S(2)}, u32[]{:S(2)}) %collective-permute-start.5) | collective-permute-done | bytes 270368 | tf_op jit(solution)/shard_map/ppermute | solution.py:321
  79.6 7.4 %all-to-all-done.sent = bf16[16,1040,128]{2,1,0:T(8,128)(2,1)} async-done(((bf16[16,1040,128]{2,1,0:T(8,128)(2,1)}), bf16[16,1040,128]{2,1,0:T(8,128)(2,1)}, u32[]{:S(2)}, u32[]{:S(2)}) %all-to-all-start) | async-done | bytes 4259872 | tf_op jit(solution)/shard_map/all_to_all | solution.py:368
  87.9 7.7 %hidden_for_other_core.1 = bf16[64,128,256]{2,1,0:T(8,128)(2,1)S(1)} custom-call(s32[5]{0:T(128)S(1)} %stack.42.where, s32[128]{0:T(128)S(1)} %reshape.54.meta, s32[128]{0:T(128)S(1)} %reshape.46.ids, s32[40]{0:T(128)S(1)} %copy-done.9, s32[40]{0:T(128)S(1)} %copy-done.11, s32[1]{0:T(128)S(6)} %copy.24.count, bf16[16,1040,128]{2,1,0:T(8,128)(2,1)} %all-to-all-done.sent, ...), custom_call_target="tpu_custom_call" | custom-call | flops 1000000000 | bytes 30000000 | tf_op jit(solution)/shard_map/hidden_for_other_core/pallas_call | solution.py:117
  97.4 6.8 %collective-permute-done.7.rest_8_ = bf16[64,128,256]{2,1,0:T(8,128)(2,1)S(1)} collective-permute-done((bf16[64,128,256]{2,1,0:T(8,128)(2,1)S(1)}, bf16[64,128,256]{2,1,0:T(8,128)(2,1)S(1)}, u32[]{:S(2)}, u32[]{:S(2)}) %collective-permute-start.7) | collective-permute-done | bytes 4194336 | tf_op jit(solution)/shard_map/ppermute | solution.py:317
  104.2 7.4 %hidden_sums.1 = bf16[64,128,256]{2,1,0:T(8,128)(2,1)S(1)} custom-call(s32[5]{0:T(128)S(1)} %stack.42.where, s32[128]{0:T(128)S(1)} %reshape.54.meta, s32[128]{0:T(128)S(1)} %reshape.46.ids, s32[40]{0:T(128)S(1)} %copy-done.9, s32[40]{0:T(128)S(1)} %copy-done.11, s32[1]{0:T(128)S(6)} %copy.24.count, bf16[16,1040,128]{2,1,0:T(8,128)(2,1)} %all-to-all-done.sent, ...), custom_call_target="tpu_custom_call" | custom-call | flops 1000000000 | bytes 30000000 | tf_op jit(solution)/shard_map/hidden_sums/pallas_call | solution.py:117
  114.9 4.5 %all-to-all-start.1 = ((bf16[16,512,256]{2,1,0:T(8,128)(2,1)}), bf16[16,512,256]{2,1,0:T(8,128)(2,1)}, u32[]{:S(2)}, u32[]{:S(2)}) async-start(bf16[16,512,256]{2,1,0:T(8,128)(2,1)} %bitcast.19), calls=%async_computation.1 | async-start | bytes 8388608 | tf_op jit(solution)/shard_map/all_to_all | solution.py:377
  124.3 11.0 %grad_sums.1 = (f32[512,256]{1,0:T(8,128)S(1)}, bf16[512,256]{1,0:T(8,128)(2,1)S(1)}, bf16[512,256]{1,0:T(8,128)(2,1)S(1)}, bf16[512,256]{1,0:T(8,128)(2,1)}, bf...) custom-call(s32[5]{0:T(128)S(1)} %stack.42.where, ...), custom_call_target="tpu_custom_call" | custom-call | flops 800000000 | bytes 24000000 | tf_op jit(solution)/shard_map/grad_sums/pallas_call | solution.py:189
  135.2 8.1 %collective-permute-start.9 = (bf16[512,256]{1,0:T(8,128)(2,1)}, bf16[512,256]{1,0:T(8,128)(2,1)S(1)}, u32[]{:S(2)}, u32[]{:S(2)}) collective-permute-start(bf16[512,256]{1,0:T(8,128)(2,1)} %get-tuple-element.12), channel_id=1, source_target_pairs={{0,8},{2,10},{4,12},{6,14},{8,0},{10,2},{12,4},{14,6},{1,9},{3,11}... | collective-permute-start | bytes 786440 | tf_op jit(solution)/shard_map/ppermute | solution.py:383
  155.8 4.4 %weight_term.1 = f32[256,256]{1,0:T(8,128)S(1)} custom-call(bf16[16,512,256]{2,1,0:T(8,128)(2,1)S(1)} %bitcast.20, bf16[16,512,256]{2,1,0:T(8,128)(2,1)S(1)} %bitcast.21, bf16[8,256]{1,0:T(8,128)(2,1)S(1)} %get-tuple-element.22.after), custom_call_target="tpu_custom_call" | custom-call | flops 400000000 | bytes 12000000 | tf_op jit(solution)/shard_map/weight_term/pallas_call | solution.py:219
  160.9 10.4 %collective-permute-start.16 = (f32[128,256]{1,0:T(8,128)}, f32[128,256]{1,0:T(8,128)S(1)}, u32[]{:S(2)}, u32[]{:S(2)}) collective-permute-start(f32[128,256]{1,0:T(8,128)} %dynamic-slice_bitcast_fusion), channel_id=1, source_target_pairs={{0,1},{1,0},{2,3},{3,2},{4,5},{5,4},{6,7},{7,6},{8,9},{9,8},{10,11... | collective-permute-start | bytes 393224 | tf_op jit(solution)/shard_map/ppermute | solution.py:317
  171.2 6.4 %collective-permute-done.10.rest_1_ = bf16[512,256]{1,0:T(8,128)(2,1)S(1)} collective-permute-done((bf16[512,256]{1,0:T(8,128)(2,1)}, bf16[512,256]{1,0:T(8,128)(2,1)S(1)}, u32[]{:S(2)}, u32[]{:S(2)}) %collective-permute-start.10) | collective-permute-done | bytes 262176 | tf_op jit(solution)/shard_map/ppermute | solution.py:383
  179.8 5.4 %collective-permute-done.13.rest_4_ = bf16[512,256]{1,0:T(8,128)(2,1)S(1)} collective-permute-done((bf16[512,256]{1,0:T(8,128)(2,1)S(1)}, bf16[512,256]{1,0:T(8,128)(2,1)S(1)}, u32[]{:S(2)}, u32[]{:S(2)}) %collective-permute-start.13) | collective-permute-done | bytes 262176 | tf_op jit(solution)/shard_map/ppermute | solution.py:383
  185.2 11.0 %all_to_all.20 = f32[16,8,256]{2,1,0:T(8,128)S(1)} all-to-all(f32[16,8,256]{2,1,0:T(8,128)S(1)} %bitcast.24), channel_id=1, replica_groups=mesh['y'=4,'x'=4,'z'=8,'col'=2] {'y','x'}, dimensions={0} | all-to-all | bytes 262144 | tf_op jit(solution)/shard_map/all_to_all | solution.py:346
  201.0 6.0 %collective-permute-start.19 = (f32[8,256]{1,0:T(8,128)S(1)}, f32[8,256]{1,0:T(8,128)S(1)}, u32[]{:S(2)}, u32[]{:S(2)}) collective-permute-start(f32[8,256]{1,0:T(8,128)S(1)} %add.37), channel_id=1, source_target_pairs={{0,8},{2,10},{4,12},{6,14},{8,0},{10,2},{12,4},{14,6},{1,9},{3,11}... | collective-permute-start | bytes 24584 | tf_op jit(solution)/shard_map/ppermute | solution.py:330
  207.1 3.6 %output_rows.1 = bf16[512,256]{1,0:T(8,128)(2,1)} custom-call(bf16[16,512,256]{2,1,0:T(8,128)(2,1)} %all-to-all-done.1.parts.refs_1_, bf16[256,256]{1,0:T(8,128)(2,1)S(1)} %copy-done.7), custom_call_target="tpu_custom_call" | custom-call | flops 400000000 | bytes 12000000 | tf_op jit(solution)/shard_map/output_rows/pallas_call | solution.py:241
  214.8 9.9 %all_to_all.21 = f32[16,8,256]{2,1,0:T(8,128)S(1)} all-to-all(f32[16,8,256]{2,1,0:T(8,128)S(1)} %broadcast_in_dim.2), channel_id=1, replica_groups=mesh['y'=4,'x'=4,'z'=8,'col'=2] {'y','x'}, dimensions={0} | all-to-all | bytes 262144 | tf_op jit(solution)/shard_map/all_to_all | solution.py:349
  224.7 5.6 %collective-permute-start.21 = (f32[128,256]{1,0:T(8,128)S(1)}, f32[128,256]{1,0:T(8,128)S(1)}, u32[]{:S(2)}, u32[]{:S(2)}) collective-permute-start(f32[128,256]{1,0:T(8,128)S(1)} %bitcast.25), channel_id=1, source_target_pairs={{0,1},{1,0},{2,3},{3,2},{4,5},{5,4},{6,7},{7,6},{8,9},{9,8},{10,11... | collective-permute-start | bytes 393224 | tf_op jit(solution)/shard_map/ppermute | solution.py:317
  (114 shorter events, 54.5 us)
Async XLA Ops:
  13.5 73.5 %all-to-all-start = ((bf16[16,1040,128]{2,1,0:T(8,128)(2,1)}), bf16[16,1040,128]{2,1,0:T(8,128)(2,1)}, u32[]{:S(2)}, u32[]{:S(2)}) async-start(bf16[16,1040,128]{2,1,0:T(8,128)(2,1)} %copy-done.6), calls=%async_computation | async-start | bytes 8519680 | tf_op jit(solution)/shard_map/all_to_all | solution.py:368
  21.5 92.7 %all-gather.2.cloned.1.call-start = ((), (), s32[]{:S(2)}) async-start(), calls=%async_computation.4 | async-start | bytes 4456448 | tf_op jit(solution)/shard_map/all_gather | solution.py:366
  22.3 13.7 %collective-permute-start = (bf16[528,256]{1,0:T(8,128)(2,1)S(1)}, bf16[528,256]{1,0:T(8,128)(2,1)S(1)}, u32[]{:S(2)}, u32[]{:S(2)}) collective-permute-start(bf16[528,256]{1,0:T(8,128)(2,1)S(1)} %fusion.1.rest_0_), channel_id=1, source_target_pairs={{0,2},{2,4},{4,6},{6,8},{8,10},{10,12},{12,14},{14,0},{1,3},{3,5},... | collective-permute-start | bytes 811016 | tf_op jit(solution)/shard_map/ppermute | solution.py:321
  24.2 17.9 %collective-permute-start.1 = (bf16[528,256]{1,0:T(8,128)(2,1)S(1)}, bf16[528,256]{1,0:T(8,128)(2,1)S(1)}, u32[]{:S(2)}, u32[]{:S(2)}) collective-permute-start(bf16[528,256]{1,0:T(8,128)(2,1)S(1)} %fusion.1.rest_0_), channel_id=1, source_target_pairs={{0,4},{2,6},{4,8},{6,10},{8,12},{10,14},{12,0},{14,2},{1,5},{3,7},... | collective-permute-start | bytes 811016 | tf_op jit(solution)/shard_map/ppermute | solution.py:321
  26.8 36.2 %collective-permute-start.2 = (bf16[528,256]{1,0:T(8,128)(2,1)S(1)}, bf16[528,256]{1,0:T(8,128)(2,1)S(1)}, u32[]{:S(2)}, u32[]{:S(2)}) collective-permute-start(bf16[528,256]{1,0:T(8,128)(2,1)S(1)} %fusion.1.rest_0_), channel_id=1, source_target_pairs={{0,6},{2,8},{4,10},{6,12},{8,14},{10,0},{12,2},{14,4},{1,7},{3,9},... | collective-permute-start | bytes 811016 | tf_op jit(solution)/shard_map/ppermute | solution.py:321
  30.8 37.2 %collective-permute-start.3 = (bf16[528,256]{1,0:T(8,128)(2,1)S(1)}, bf16[528,256]{1,0:T(8,128)(2,1)S(1)}, u32[]{:S(2)}, u32[]{:S(2)}) collective-permute-start(bf16[528,256]{1,0:T(8,128)(2,1)S(1)} %fusion.1.rest_0_), channel_id=1, source_target_pairs={{0,8},{2,10},{4,12},{6,14},{8,0},{10,2},{12,4},{14,6},{1,9},{3,11}... | collective-permute-start | bytes 811016 | tf_op jit(solution)/shard_map/ppermute | solution.py:321
  31.4 37.0 %collective-permute-start.4 = (bf16[528,256]{1,0:T(8,128)(2,1)S(1)}, bf16[528,256]{1,0:T(8,128)(2,1)S(1)}, u32[]{:S(2)}, u32[]{:S(2)}) collective-permute-start(bf16[528,256]{1,0:T(8,128)(2,1)S(1)} %fusion.1.rest_0_), channel_id=1, source_target_pairs={{0,10},{2,12},{4,14},{6,0},{8,2},{10,4},{12,6},{14,8},{1,11},{3,13... | collective-permute-start | bytes 811016 | tf_op jit(solution)/shard_map/ppermute | solution.py:321
  36.1 40.2 %collective-permute-start.5 = (bf16[528,256]{1,0:T(8,128)(2,1)S(1)}, bf16[528,256]{1,0:T(8,128)(2,1)S(1)}, u32[]{:S(2)}, u32[]{:S(2)}) collective-permute-start(bf16[528,256]{1,0:T(8,128)(2,1)S(1)} %fusion.1.rest_0_), channel_id=1, source_target_pairs={{0,12},{2,14},{4,0},{6,2},{8,4},{10,6},{12,8},{14,10},{1,13},{3,15... | collective-permute-start | bytes 811016 | tf_op jit(solution)/shard_map/ppermute | solution.py:321
  42.1 36.9 %collective-permute-start.6 = (bf16[528,256]{1,0:T(8,128)(2,1)S(1)}, bf16[528,256]{1,0:T(8,128)(2,1)S(1)}, u32[]{:S(2)}, u32[]{:S(2)}) collective-permute-start(bf16[528,256]{1,0:T(8,128)(2,1)S(1)} %fusion.1.rest_0_), channel_id=1, source_target_pairs={{0,14},{2,0},{4,2},{6,4},{8,6},{10,8},{12,10},{14,12},{1,15},{3,1}... | collective-permute-start | bytes 811016 | tf_op jit(solution)/shard_map/ppermute | solution.py:321
  95.6 8.6 %collective-permute-start.7 = (bf16[64,128,256]{2,1,0:T(8,128)(2,1)S(1)}, bf16[64,128,256]{2,1,0:T(8,128)(2,1)S(1)}, u32[]{:S(2)}, u32[]{:S(2)}) collective-permute-start(bf16[64,128,256]{2,1,0:T(8,128)(2,1)S(1)} %hidden_for_other_core.1), channel_id=1, source_target_pairs={{0,1},{1,0},{2,3},{3,2},{4,5},{5,4},{6,7},{7,6},{8,9},{9,8},{10,11... | collective-permute-start | bytes 12582920 | tf_op jit(solution)/shard_map/ppermute | solution.py:317
  114.2 7.9 %collective-permute-start.8 = (bf16[64,128,256]{2,1,0:T(8,128)(2,1)}, bf16[64,128,256]{2,1,0:T(8,128)(2,1)}, u32[]{:S(2)}, u32[]{:S(2)}) collective-permute-start(bf16[64,128,256]{2,1,0:T(8,128)(2,1)} %in_order_in_place.1.mine), channel_id=1, source_target_pairs={{0,1},{1,0},{2,3},{3,2},{4,5},{5,4},{6,7},{7,6},{8,9},{9,8},{10,11... | collective-permute-start | bytes 12582920 | tf_op jit(solution)/shard_map/ppermute | solution.py:317
  114.9 70.2 %all-to-all-start.1 = ((bf16[16,512,256]{2,1,0:T(8,128)(2,1)}), bf16[16,512,256]{2,1,0:T(8,128)(2,1)}, u32[]{:S(2)}, u32[]{:S(2)}) async-start(bf16[16,512,256]{2,1,0:T(8,128)(2,1)} %bitcast.19), calls=%async_computation.1 | async-start | bytes 8388608 | tf_op jit(solution)/shard_map/all_to_all | solution.py:377
  135.2 16.2 %collective-permute-start.9 = (bf16[512,256]{1,0:T(8,128)(2,1)}, bf16[512,256]{1,0:T(8,128)(2,1)S(1)}, u32[]{:S(2)}, u32[]{:S(2)}) collective-permute-start(bf16[512,256]{1,0:T(8,128)(2,1)} %get-tuple-element.12), channel_id=1, source_target_pairs={{0,8},{2,10},{4,12},{6,14},{8,0},{10,2},{12,4},{14,6},{1,9},{3,11}... | collective-permute-start | bytes 786440 | tf_op jit(solution)/shard_map/ppermute | solution.py:383
  143.3 34.3 %collective-permute-start.10 = (bf16[512,256]{1,0:T(8,128)(2,1)}, bf16[512,256]{1,0:T(8,128)(2,1)S(1)}, u32[]{:S(2)}, u32[]{:S(2)}) collective-permute-start(bf16[512,256]{1,0:T(8,128)(2,1)} %get-tuple-element.13), channel_id=1, source_target_pairs={{0,6},{2,8},{4,10},{6,12},{8,14},{10,0},{12,2},{14,4},{1,7},{3,9},... | collective-permute-start | bytes 786440 | tf_op jit(solution)/shard_map/ppermute | solution.py:383
  145.6 32.0 %collective-permute-start.11 = (bf16[512,256]{1,0:T(8,128)(2,1)}, bf16[512,256]{1,0:T(8,128)(2,1)S(1)}, u32[]{:S(2)}, u32[]{:S(2)}) collective-permute-start(bf16[512,256]{1,0:T(8,128)(2,1)} %get-tuple-element.14), channel_id=1, source_target_pairs={{0,10},{2,12},{4,14},{6,0},{8,2},{10,4},{12,6},{14,8},{1,11},{3,13... | collective-permute-start | bytes 786440 | tf_op jit(solution)/shard_map/ppermute | solution.py:383
  147.8 31.9 %collective-permute-start.12 = (bf16[512,256]{1,0:T(8,128)(2,1)S(1)}, bf16[512,256]{1,0:T(8,128)(2,1)S(1)}, u32[]{:S(2)}, u32[]{:S(2)}) collective-permute-start(bf16[512,256]{1,0:T(8,128)(2,1)S(1)} %get-tuple-element.15), channel_id=1, source_target_pairs={{0,4},{2,6},{4,8},{6,10},{8,12},{10,14},{12,0},{14,2},{1,5},{3,7},... | collective-permute-start | bytes 786440 | tf_op jit(solution)/shard_map/ppermute | solution.py:383
  150.6 34.6 %collective-permute-start.13 = (bf16[512,256]{1,0:T(8,128)(2,1)S(1)}, bf16[512,256]{1,0:T(8,128)(2,1)S(1)}, u32[]{:S(2)}, u32[]{:S(2)}) collective-permute-start(bf16[512,256]{1,0:T(8,128)(2,1)S(1)} %get-tuple-element.16), channel_id=1, source_target_pairs={{0,12},{2,14},{4,0},{6,2},{8,4},{10,6},{12,8},{14,10},{1,13},{3,15... | collective-permute-start | bytes 786440 | tf_op jit(solution)/shard_map/ppermute | solution.py:383
  160.9 24.3 %collective-permute-start.16 = (f32[128,256]{1,0:T(8,128)}, f32[128,256]{1,0:T(8,128)S(1)}, u32[]{:S(2)}, u32[]{:S(2)}) collective-permute-start(f32[128,256]{1,0:T(8,128)} %dynamic-slice_bitcast_fusion), channel_id=1, source_target_pairs={{0,1},{1,0},{2,3},{3,2},{4,5},{5,4},{6,7},{7,6},{8,9},{9,8},{10,11... | collective-permute-start | bytes 393224 | tf_op jit(solution)/shard_map/ppermute | solution.py:317
  198.8 16.0 %collective-permute-start.18 = (f32[8,256]{1,0:T(8,128)S(1)}, f32[8,256]{1,0:T(8,128)S(1)}, u32[]{:S(2)}, u32[]{:S(2)}) collective-permute-start(f32[8,256]{1,0:T(8,128)S(1)} %add.37), channel_id=1, source_target_pairs={{0,4},{2,6},{4,0},{6,2},{8,12},{10,14},{12,8},{14,10},{1,5},{3,7},... | collective-permute-start | bytes 24584 | tf_op jit(solution)/shard_map/ppermute | solution.py:330
  201.0 13.8 %collective-permute-start.19 = (f32[8,256]{1,0:T(8,128)S(1)}, f32[8,256]{1,0:T(8,128)S(1)}, u32[]{:S(2)}, u32[]{:S(2)}) collective-permute-start(f32[8,256]{1,0:T(8,128)S(1)} %add.37), channel_id=1, source_target_pairs={{0,8},{2,10},{4,12},{6,14},{8,0},{10,2},{12,4},{14,6},{1,9},{3,11}... | collective-permute-start | bytes 24584 | tf_op jit(solution)/shard_map/ppermute | solution.py:330
  207.0 7.7 %collective-permute-start.20 = (f32[8,256]{1,0:T(8,128)S(1)}, f32[8,256]{1,0:T(8,128)S(1)}, u32[]{:S(2)}, u32[]{:S(2)}) collective-permute-start(f32[8,256]{1,0:T(8,128)S(1)} %add.37), channel_id=1, source_target_pairs={{0,12},{2,14},{4,8},{6,10},{8,4},{10,6},{12,0},{14,2},{1,13},{3,15... | collective-permute-start | bytes 24584 | tf_op jit(solution)/shard_map/ppermute | solution.py:330
  211.3 19.0 %collective-permute-start.14 = (bf16[512,256]{1,0:T(8,128)(2,1)S(1)}, bf16[512,256]{1,0:T(8,128)(2,1)S(1)}, u32[]{:S(2)}, u32[]{:S(2)}) collective-permute-start(bf16[512,256]{1,0:T(8,128)(2,1)S(1)} %get-tuple-element.17), channel_id=1, source_target_pairs={{0,2},{2,4},{4,6},{6,8},{8,10},{10,12},{12,14},{14,0},{1,3},{3,5},... | collective-permute-start | bytes 786440 | tf_op jit(solution)/shard_map/ppermute | solution.py:383
  212.4 18.0 %collective-permute-start.15 = (bf16[512,256]{1,0:T(8,128)(2,1)S(1)}, bf16[512,256]{1,0:T(8,128)(2,1)S(1)}, u32[]{:S(2)}, u32[]{:S(2)}) collective-permute-start(bf16[512,256]{1,0:T(8,128)(2,1)S(1)} %get-tuple-element.18), channel_id=1, source_target_pairs={{0,14},{2,0},{4,2},{6,4},{8,6},{10,8},{12,10},{14,12},{1,15},{3,1}... | collective-permute-start | bytes 786440 | tf_op jit(solution)/shard_map/ppermute | solution.py:383
  224.7 6.8 %collective-permute-start.21 = (f32[128,256]{1,0:T(8,128)S(1)}, f32[128,256]{1,0:T(8,128)S(1)}, u32[]{:S(2)}, u32[]{:S(2)}) collective-permute-start(f32[128,256]{1,0:T(8,128)S(1)} %bitcast.25), channel_id=1, source_target_pairs={{0,1},{1,0},{2,3},{3,2},{4,5},{5,4},{6,7},{7,6},{8,9},{9,8},{10,11... | collective-permute-start | bytes 393224 | tf_op jit(solution)/shard_map/ppermute | solution.py:317
  (15 other events, 303.3 us)
Sparse Core Ops, SparseCore 0:
  24.8 88.3 all-gather.1

commit v6 on v5

--- a/solution.py
+++ b/solution.py
@@ -66,12 +66,12 @@
 
 def hidden_kernel(first, where, meta, ids, cols, rows, count, sent, tiles, *rest):
     feats, rest = rest[:8], rest[8:]
-    out, total = rest[-2:]
+    out, total = rest[0], rest[-1]
     c, z_me, r_me = where[0], where[1], where[2]
     half = 1 - c if first else c
 
     def begin(i, carry):
-        total[i] = jnp.zeros(total.shape[1:], total.dtype) if first else rest[0][i].astype(total.dtype)
+        total[i] = jnp.zeros(total.shape[1:], total.dtype)
         return carry
 
     lax.fori_loop(0, total.shape[0], begin, 0)
@@ -107,23 +107,45 @@
         out[i] = total[i].astype(out.dtype)
         return carry
 
-    lax.fori_loop(0, total.shape[0], cast, 0)
-
-
-def hidden_parts(where, meta, ids, cols, rows, count, sent, tiles, feats, *arrived):
+    if first:
+        lax.fori_loop(0, total.shape[0], cast, 0)
+
+
+def add_kernel(mine, arrived, out):
+    def one(i, carry):
+        out[i] = (mine[i] + arrived[i].astype(mine.dtype)).astype(out.dtype)
+        return carry
+
+    lax.fori_loop(0, mine.shape[0], one, 0)
+
+
+def add_halves(mine, arrived):
+    vmem = pl.BlockSpec(memory_space=pltpu.VMEM)
+    return pl.pallas_call(
+        add_kernel,
+        out_shape=jax.ShapeDtypeStruct(arrived.shape, arrived.dtype),
+        in_specs=[vmem] * 2,
+        out_specs=vmem,
+        compiler_params=pltpu.CompilerParams(vmem_limit_bytes=20 * 2**20),
+        cost_estimate=cost(4),
+        name="add_halves",
+    )(mine, arrived)
+
+
+def hidden_parts(first, where, meta, ids, cols, rows, count, sent, tiles, feats):
     smem = pl.BlockSpec(memory_space=pltpu.SMEM)
     vmem = pl.BlockSpec(memory_space=pltpu.VMEM)
     width = feats[0].shape[1]
     return pl.pallas_call(
-        functools.partial(hidden_kernel, not arrived),
-        out_shape=jax.ShapeDtypeStruct((64, BLK, width), jnp.bfloat16),
-        in_specs=[smem] * 6 + [vmem] * (2 + len(feats) + len(arrived)),
-        out_specs=vmem,
-        scratch_shapes=[pltpu.VMEM((64, BLK, width), jnp.float32)],
+        functools.partial(hidden_kernel, first),
+        out_shape=jax.ShapeDtypeStruct((64, BLK, width), jnp.bfloat16 if first else jnp.float32),
+        in_specs=[smem] * 6 + [vmem] * (2 + len(feats)),
+        out_specs=vmem,
+        scratch_shapes=[pltpu.VMEM((64, BLK, width), jnp.float32)] if first else [],
         compiler_params=pltpu.CompilerParams(vmem_limit_bytes=28 * 2**20),
         cost_estimate=cost(10),
-        name="hidden_sums" if arrived else "hidden_for_other_core",
-    )(where, meta, ids, cols, rows, count, sent, tiles, *feats, *arrived)
+        name="hidden_for_other_core" if first else "hidden_sums",
+    )(where, meta, ids, cols, rows, count, sent, tiles, *feats)
 
 
 def add_grads(where, meta, ids, cols, rows, count, sent, mine, peer, tiles, total):
@@ -372,8 +394,8 @@
     ids = lax.dynamic_index_in_dim(ids, z_me, 2, keepdims=False).reshape(128)
 
     operands = (where, meta, ids, tile_cols, tile_rows, tile_count, sent)
-    for_peer = swap_cores(hidden_parts(*operands, tile_values, feats))
-    both = hidden_parts(*operands, tile_values, feats, for_peer)
+    for_peer = hidden_parts(True, *operands, tile_values, feats)
+    both = add_halves(hidden_parts(False, *operands, tile_values, feats), swap_cores(for_peer))
     parts = lax.all_to_all(both.reshape(16, 4 * BLK, width), PLANE, 0, 0, tiled=True)
     [cot_mine] = same_later([cot_mine], mark(both))
     own, *away = grad_parts(*operands, cot_mine, swap_cores(cot_mine), tile_values)

time: 240 us -> 234 us (0.975)
  starting transfers between devices: 80.7 us -> 75.2 us
    ppermute x4, waiting for transfers between devices: 9.37 us -> 2.34 us  [swap_cores(): return lax.ppermute(a, 'col', [(0, 1), (1, 0)])]
    all_gather x1, waiting for transfers between devices: 0.01 us -> 5.85 us  [local(): lax.all_gather(cotangent.reshape(4, BLK, width), PLANE, axis=0, tiled=True)]
    ppermute x7, waiting for transfers between devices: 13.9 us -> 18 us  [local(): lax.ppermute(part, 'z', [(z, (z + step) % 8) for z in range(8)])]
    ppermute x4, starting transfers between devices: 18.6 us -> 14.6 us  [swap_cores(): return lax.ppermute(a, 'col', [(0, 1), (1, 0)])]
    pallas_call x2 -> x3, Pallas kernels: 15.1 us -> 15.1 us  [the longest x2 14.1 us: hidden_parts(): pl.pallas_call(functools.partial(hidden_kernel, first), out_shape=jax.Sha...]
  transfers between devices with their start and end apart: 25 -> 25, of which waited for: 12 -> 14; matrix products, arithmetic and copies ran while one was open for 2% -> 2% of each run, Pallas kernels for 15% -> 15%
where the time goes in v6:
time: 234 us
  starting transfers between devices  75.2 us (32%)
  waiting for transfers between devices  68.8 us (29%)
  Pallas kernels  35.9 us (15%)
  blocking collectives  21.2 us (9%)
  local copies, waits for them, and re-layouts  16.4 us (7%)
  between operations  15 us (6%)
    ppermute x7, waiting for transfers between devices, steps_along(): lax.ppermute(a, axis, [(i, (i + s) % size) for i in range(size)])  33 us
    ppermute x7, starting transfers between devices, steps_along(): lax.ppermute(a, axis, [(i, (i + s) % size) for i in range(size)])  22.8 us
    ppermute x7, waiting for transfers between devices, local(): lax.ppermute(part, 'z', [(z, (z + step) % 8) for z in range(8)])  18 us
    ppermute x7, starting transfers between devices, local(): lax.ppermute(part, 'z', [(z, (z + step) % 8) for z in range(8)])  17.5 us
    ppermute x4, starting transfers between devices, swap_cores(): return lax.ppermute(a, 'col', [(0, 1), (1, 0)])  14.6 us
    pallas_call x2, Pallas kernels, hidden_parts(): pl.pallas_call(functools.partial(hidden_kernel, first), out_shape=jax.Sha...  14.1 us
    unnamed x39, local copies, waits for them, and re-layouts  13.2 us
    all_to_all x1, blocking collectives, sum_everywhere(): lax.all_to_all(half.reshape(16, 8, n), PLANE, 0, 0, tiled=True)  11.3 us
  transfers between devices with their start and end apart: 25, of which 14 were waited for; matrix products, arithmetic and copies ran while one was open for 2% of the time, Pallas kernels for 15%

profile of v6, /device:TPU:1, one launch (start us, length us, event | category | flops | bytes accessed | tf_op | source)
XLA Modules:
  0.0 234.3 jit_solution(84139491469067120)
XLA Ops:
  13.5 7.9 %all-to-all-start = ((bf16[16,1040,128]{2,1,0:T(8,128)(2,1)}), bf16[16,1040,128]{2,1,0:T(8,128)(2,1)}, u32[]{:S(2)}, u32[]{:S(2)}) async-start(bf16[16,1040,128]{2,1,0:T(8,128)(2,1)} %copy-done.6), calls=%async_computation | async-start | bytes 8519680 | tf_op jit(solution)/shard_map/all_to_all | solution.py:390
  26.8 3.9 %collective-permute-start.2 = (bf16[528,256]{1,0:T(8,128)(2,1)S(1)}, bf16[528,256]{1,0:T(8,128)(2,1)S(1)}, u32[]{:S(2)}, u32[]{:S(2)}) collective-permute-start(bf16[528,256]{1,0:T(8,128)(2,1)S(1)} %fusion.1.rest_0_), channel_id=1, source_target_pairs={{0,6},{2,8},{4,10},{6,12},{8,14},{10,0},{12,2},{14,4},{1,7},{3,9},... | collective-permute-start | bytes 811016 | tf_op jit(solution)/shard_map/ppermute | solution.py:343
  31.0 4.5 %collective-permute-start.4 = (bf16[528,256]{1,0:T(8,128)(2,1)S(1)}, bf16[528,256]{1,0:T(8,128)(2,1)S(1)}, u32[]{:S(2)}, u32[]{:S(2)}) collective-permute-start(bf16[528,256]{1,0:T(8,128)(2,1)S(1)} %fusion.1.rest_0_), channel_id=1, source_target_pairs={{0,10},{2,12},{4,14},{6,0},{8,2},{10,4},{12,6},{14,8},{1,11},{3,13... | collective-permute-start | bytes 811016 | tf_op jit(solution)/shard_map/ppermute | solution.py:343
  41.0 7.1 %collective-permute-start.6 = (bf16[528,256]{1,0:T(8,128)(2,1)S(1)}, bf16[528,256]{1,0:T(8,128)(2,1)S(1)}, u32[]{:S(2)}, u32[]{:S(2)}) collective-permute-start(bf16[528,256]{1,0:T(8,128)(2,1)S(1)} %fusion.1.rest_0_), channel_id=1, source_target_pairs={{0,14},{2,0},{4,2},{6,4},{8,6},{10,8},{12,10},{14,12},{1,15},{3,1}... | collective-permute-start | bytes 811016 | tf_op jit(solution)/shard_map/ppermute | solution.py:343
  48.1 13.9 %collective-permute-done.2.rest_3_ = bf16[528,256]{1,0:T(8,128)(2,1)S(1)} collective-permute-done((bf16[528,256]{1,0:T(8,128)(2,1)S(1)}, bf16[528,256]{1,0:T(8,128)(2,1)S(1)}, u32[]{:S(2)}, u32[]{:S(2)}) %collective-permute-start.2) | collective-permute-done | bytes 270368 | tf_op jit(solution)/shard_map/ppermute | solution.py:343
  62.0 6.4 %collective-permute-done.3.rest_4_ = bf16[528,256]{1,0:T(8,128)(2,1)S(1)} collective-permute-done((bf16[528,256]{1,0:T(8,128)(2,1)S(1)}, bf16[528,256]{1,0:T(8,128)(2,1)S(1)}, u32[]{:S(2)}, u32[]{:S(2)}) %collective-permute-start.3) | collective-permute-done | bytes 270368 | tf_op jit(solution)/shard_map/ppermute | solution.py:343
  68.9 7.0 %collective-permute-done.5.rest_6_ = bf16[528,256]{1,0:T(8,128)(2,1)S(1)} collective-permute-done((bf16[528,256]{1,0:T(8,128)(2,1)S(1)}, bf16[528,256]{1,0:T(8,128)(2,1)S(1)}, u32[]{:S(2)}, u32[]{:S(2)}) %collective-permute-start.5) | collective-permute-done | bytes 270368 | tf_op jit(solution)/shard_map/ppermute | solution.py:343
  79.6 6.7 %all-to-all-done.sent = bf16[16,1040,128]{2,1,0:T(8,128)(2,1)} async-done(((bf16[16,1040,128]{2,1,0:T(8,128)(2,1)}), bf16[16,1040,128]{2,1,0:T(8,128)(2,1)}, u32[]{:S(2)}, u32[]{:S(2)}) %all-to-all-start) | async-done | bytes 4259872 | tf_op jit(solution)/shard_map/all_to_all | solution.py:390
  87.2 7.5 %hidden_for_other_core.1 = bf16[64,128,256]{2,1,0:T(8,128)(2,1)S(1)} custom-call(s32[5]{0:T(128)S(1)} %stack.42.where, s32[128]{0:T(128)S(1)} %reshape.54.meta, s32[128]{0:T(128)S(1)} %reshape.46.ids, s32[40]{0:T(128)S(1)} %copy-done.9, s32[40]{0:T(128)S(1)} %copy-done.11, s32[1]{0:T(128)S(6)} %copy.24.count, bf16[16,1040,128]{2,1,0:T(8,128)(2,1)} %all-to-all-done.sent, ...), custom_call_target="tpu_custom_call" | custom-call | flops 1000000000 | bytes 30000000 | tf_op jit(solution)/shard_map/hidden_for_other_core/pallas_call | solution.py:139
  97.2 6.6 %hidden_sums.1.mine = f32[64,128,256]{2,1,0:T(8,128)S(1)} custom-call(s32[5]{0:T(128)S(1)} %stack.42.where, s32[128]{0:T(128)S(1)} %reshape.54.meta, s32[128]{0:T(128)S(1)} %reshape.46.ids, s32[40]{0:T(128)S(1)} %copy-done.9, s32[40]{0:T(128)S(1)} %copy-done.11, s32[1]{0:T(128)S(6)} %copy.24.count, bf16[16,1040,128]{2,1,0:T(8,128)(2,1)} %all-to-all-done.sent, ...), custom_call_target="tpu_custom_call" | custom-call | flops 1000000000 | bytes 30000000 | tf_op jit(solution)/shard_map/hidden_sums/pallas_call | solution.py:139
  107.6 5.9 %all-gather.2.cloned.1.call-done.refs_0_ = bf16[64,128,256]{2,1,0:T(8,128)(2,1)} async-done(((bf16[4,128,256]{2,1,0:T(8,128)(2,1)}), bf16[64,128,256]{2,1,0:T(8,128)(2,1)}) %all-gather.2.cloned.1.call-update) | async-done | bytes 4194320 | tf_op jit(solution)/shard_map/all_gather | solution.py:388
  114.2 5.0 %all-to-all-start.1 = ((bf16[16,512,256]{2,1,0:T(8,128)(2,1)}), bf16[16,512,256]{2,1,0:T(8,128)(2,1)}, u32[]{:S(2)}, u32[]{:S(2)}) async-start(bf16[16,512,256]{2,1,0:T(8,128)(2,1)} %bitcast.19), calls=%async_computation.1 | async-start | bytes 8388608 | tf_op jit(solution)/shard_map/all_to_all | solution.py:399
  123.5 10.6 %grad_sums.1 = (f32[512,256]{1,0:T(8,128)S(1)}, bf16[512,256]{1,0:T(8,128)(2,1)S(1)}, bf16[512,256]{1,0:T(8,128)(2,1)S(1)}, bf16[512,256]{1,0:T(8,128)(2,1)}, bf...) custom-call(s32[5]{0:T(128)S(1)} %stack.42.where, ...), custom_call_target="tpu_custom_call" | custom-call | flops 800000000 | bytes 24000000 | tf_op jit(solution)/shard_map/grad_sums/pallas_call | solution.py:211
  134.0 6.8 %collective-permute-start.9 = (bf16[512,256]{1,0:T(8,128)(2,1)}, bf16[512,256]{1,0:T(8,128)(2,1)S(1)}, u32[]{:S(2)}, u32[]{:S(2)}) collective-permute-start(bf16[512,256]{1,0:T(8,128)(2,1)} %get-tuple-element.12), channel_id=1, source_target_pairs={{0,8},{2,10},{4,12},{6,14},{8,0},{10,2},{12,4},{14,6},{1,9},{3,11}... | collective-permute-start | bytes 786440 | tf_op jit(solution)/shard_map/ppermute | solution.py:405
  140.9 4.4 %collective-permute-start.11 = (bf16[512,256]{1,0:T(8,128)(2,1)}, bf16[512,256]{1,0:T(8,128)(2,1)S(1)}, u32[]{:S(2)}, u32[]{:S(2)}) collective-permute-start(bf16[512,256]{1,0:T(8,128)(2,1)} %get-tuple-element.14), channel_id=1, source_target_pairs={{0,10},{2,12},{4,14},{6,0},{8,2},{10,4},{12,6},{14,8},{1,11},{3,13... | collective-permute-start | bytes 786440 | tf_op jit(solution)/shard_map/ppermute | solution.py:405
  155.1 4.4 %weight_term.1 = f32[256,256]{1,0:T(8,128)S(1)} custom-call(bf16[16,512,256]{2,1,0:T(8,128)(2,1)S(1)} %bitcast.20, bf16[16,512,256]{2,1,0:T(8,128)(2,1)S(1)} %bitcast.21, bf16[8,256]{1,0:T(8,128)(2,1)S(1)} %get-tuple-element.22.after), custom_call_target="tpu_custom_call" | custom-call | flops 400000000 | bytes 12000000 | tf_op jit(solution)/shard_map/weight_term/pallas_call | solution.py:241
  160.2 5.3 %collective-permute-start.16 = (f32[128,256]{1,0:T(8,128)}, f32[128,256]{1,0:T(8,128)S(1)}, u32[]{:S(2)}, u32[]{:S(2)}) collective-permute-start(f32[128,256]{1,0:T(8,128)} %dynamic-slice_bitcast_fusion), channel_id=1, source_target_pairs={{0,1},{1,0},{2,3},{3,2},{4,5},{5,4},{6,7},{7,6},{8,9},{9,8},{10,11... | collective-permute-start | bytes 393224 | tf_op jit(solution)/shard_map/ppermute | solution.py:339
  165.5 9.4 %collective-permute-done.10.rest_1_ = bf16[512,256]{1,0:T(8,128)(2,1)S(1)} collective-permute-done((bf16[512,256]{1,0:T(8,128)(2,1)}, bf16[512,256]{1,0:T(8,128)(2,1)S(1)}, u32[]{:S(2)}, u32[]{:S(2)}) %collective-permute-start.10) | collective-permute-done | bytes 262176 | tf_op jit(solution)/shard_map/ppermute | solution.py:405
  174.9 6.8 %collective-permute-done.13.rest_4_ = bf16[512,256]{1,0:T(8,128)(2,1)S(1)} collective-permute-done((bf16[512,256]{1,0:T(8,128)(2,1)S(1)}, bf16[512,256]{1,0:T(8,128)(2,1)S(1)}, u32[]{:S(2)}, u32[]{:S(2)}) %collective-permute-start.13) | collective-permute-done | bytes 262176 | tf_op jit(solution)/shard_map/ppermute | solution.py:405
  182.8 11.3 %all_to_all.20 = f32[16,8,256]{2,1,0:T(8,128)S(1)} all-to-all(f32[16,8,256]{2,1,0:T(8,128)S(1)} %bitcast.24), channel_id=1, replica_groups=mesh['y'=4,'x'=4,'z'=8,'col'=2] {'y','x'}, dimensions={0} | all-to-all | bytes 262144 | tf_op jit(solution)/shard_map/all_to_all | solution.py:368
  198.9 3.8 %collective-permute-start.19 = (f32[8,256]{1,0:T(8,128)S(1)}, f32[8,256]{1,0:T(8,128)S(1)}, u32[]{:S(2)}, u32[]{:S(2)}) collective-permute-start(f32[8,256]{1,0:T(8,128)S(1)} %add.37), channel_id=1, source_target_pairs={{0,8},{2,10},{4,12},{6,14},{8,0},{10,2},{12,4},{14,6},{1,9},{3,11}... | collective-permute-start | bytes 24584 | tf_op jit(solution)/shard_map/ppermute | solution.py:352
  202.8 3.6 %output_rows.1 = bf16[512,256]{1,0:T(8,128)(2,1)} custom-call(bf16[16,512,256]{2,1,0:T(8,128)(2,1)} %all-to-all-done.1.parts.refs_1_, bf16[256,256]{1,0:T(8,128)(2,1)S(1)} %copy-done.7), custom_call_target="tpu_custom_call" | custom-call | flops 400000000 | bytes 12000000 | tf_op jit(solution)/shard_map/output_rows/pallas_call | solution.py:263
  209.8 9.9 %all_to_all.21 = f32[16,8,256]{2,1,0:T(8,128)S(1)} all-to-all(f32[16,8,256]{2,1,0:T(8,128)S(1)} %broadcast_in_dim.2), channel_id=1, replica_groups=mesh['y'=4,'x'=4,'z'=8,'col'=2] {'y','x'}, dimensions={0} | all-to-all | bytes 262144 | tf_op jit(solution)/shard_map/all_to_all | solution.py:371
  219.6 5.9 %collective-permute-start.21 = (f32[128,256]{1,0:T(8,128)S(1)}, f32[128,256]{1,0:T(8,128)S(1)}, u32[]{:S(2)}, u32[]{:S(2)}) collective-permute-start(f32[128,256]{1,0:T(8,128)S(1)} %bitcast.25), channel_id=1, source_target_pairs={{0,1},{1,0},{2,3},{3,2},{4,5},{5,4},{6,7},{7,6},{8,9},{9,8},{10,11... | collective-permute-start | bytes 393224 | tf_op jit(solution)/shard_map/ppermute | solution.py:339
  (115 shorter events, 54.9 us)
Async XLA Ops:
  13.5 72.7 %all-to-all-start = ((bf16[16,1040,128]{2,1,0:T(8,128)(2,1)}), bf16[16,1040,128]{2,1,0:T(8,128)(2,1)}, u32[]{:S(2)}, u32[]{:S(2)}) async-start(bf16[16,1040,128]{2,1,0:T(8,128)(2,1)} %copy-done.6), calls=%async_computation | async-start | bytes 8519680 | tf_op jit(solution)/shard_map/all_to_all | solution.py:390
  21.4 92.0 %all-gather.2.cloned.1.call-start = ((), (), s32[]{:S(2)}) async-start(), calls=%async_computation.4 | async-start | bytes 4456448 | tf_op jit(solution)/shard_map/all_gather | solution.py:388
  22.2 13.5 %collective-permute-start = (bf16[528,256]{1,0:T(8,128)(2,1)S(1)}, bf16[528,256]{1,0:T(8,128)(2,1)S(1)}, u32[]{:S(2)}, u32[]{:S(2)}) collective-permute-start(bf16[528,256]{1,0:T(8,128)(2,1)S(1)} %fusion.1.rest_0_), channel_id=1, source_target_pairs={{0,2},{2,4},{4,6},{6,8},{8,10},{10,12},{12,14},{14,0},{1,3},{3,5},... | collective-permute-start | bytes 811016 | tf_op jit(solution)/shard_map/ppermute | solution.py:343
  24.2 16.8 %collective-permute-start.1 = (bf16[528,256]{1,0:T(8,128)(2,1)S(1)}, bf16[528,256]{1,0:T(8,128)(2,1)S(1)}, u32[]{:S(2)}, u32[]{:S(2)}) collective-permute-start(bf16[528,256]{1,0:T(8,128)(2,1)S(1)} %fusion.1.rest_0_), channel_id=1, source_target_pairs={{0,4},{2,6},{4,8},{6,10},{8,12},{10,14},{12,0},{14,2},{1,5},{3,7},... | collective-permute-start | bytes 811016 | tf_op jit(solution)/shard_map/ppermute | solution.py:343
  26.8 35.2 %collective-permute-start.2 = (bf16[528,256]{1,0:T(8,128)(2,1)S(1)}, bf16[528,256]{1,0:T(8,128)(2,1)S(1)}, u32[]{:S(2)}, u32[]{:S(2)}) collective-permute-start(bf16[528,256]{1,0:T(8,128)(2,1)S(1)} %fusion.1.rest_0_), channel_id=1, source_target_pairs={{0,6},{2,8},{4,10},{6,12},{8,14},{10,0},{12,2},{14,4},{1,7},{3,9},... | collective-permute-start | bytes 811016 | tf_op jit(solution)/shard_map/ppermute | solution.py:343
  30.7 37.7 %collective-permute-start.3 = (bf16[528,256]{1,0:T(8,128)(2,1)S(1)}, bf16[528,256]{1,0:T(8,128)(2,1)S(1)}, u32[]{:S(2)}, u32[]{:S(2)}) collective-permute-start(bf16[528,256]{1,0:T(8,128)(2,1)S(1)} %fusion.1.rest_0_), channel_id=1, source_target_pairs={{0,8},{2,10},{4,12},{6,14},{8,0},{10,2},{12,4},{14,6},{1,9},{3,11}... | collective-permute-start | bytes 811016 | tf_op jit(solution)/shard_map/ppermute | solution.py:343
  31.0 37.8 %collective-permute-start.4 = (bf16[528,256]{1,0:T(8,128)(2,1)S(1)}, bf16[528,256]{1,0:T(8,128)(2,1)S(1)}, u32[]{:S(2)}, u32[]{:S(2)}) collective-permute-start(bf16[528,256]{1,0:T(8,128)(2,1)S(1)} %fusion.1.rest_0_), channel_id=1, source_target_pairs={{0,10},{2,12},{4,14},{6,0},{8,2},{10,4},{12,6},{14,8},{1,11},{3,13... | collective-permute-start | bytes 811016 | tf_op jit(solution)/shard_map/ppermute | solution.py:343
  35.7 40.3 %collective-permute-start.5 = (bf16[528,256]{1,0:T(8,128)(2,1)S(1)}, bf16[528,256]{1,0:T(8,128)(2,1)S(1)}, u32[]{:S(2)}, u32[]{:S(2)}) collective-permute-start(bf16[528,256]{1,0:T(8,128)(2,1)S(1)} %fusion.1.rest_0_), channel_id=1, source_target_pairs={{0,12},{2,14},{4,0},{6,2},{8,4},{10,6},{12,8},{14,10},{1,13},{3,15... | collective-permute-start | bytes 811016 | tf_op jit(solution)/shard_map/ppermute | solution.py:343
  41.0 38.0 %collective-permute-start.6 = (bf16[528,256]{1,0:T(8,128)(2,1)S(1)}, bf16[528,256]{1,0:T(8,128)(2,1)S(1)}, u32[]{:S(2)}, u32[]{:S(2)}) collective-permute-start(bf16[528,256]{1,0:T(8,128)(2,1)S(1)} %fusion.1.rest_0_), channel_id=1, source_target_pairs={{0,14},{2,0},{4,2},{6,4},{8,6},{10,8},{12,10},{14,12},{1,15},{3,1}... | collective-permute-start | bytes 811016 | tf_op jit(solution)/shard_map/ppermute | solution.py:343
  94.7 9.3 %collective-permute-start.7 = (bf16[64,128,256]{2,1,0:T(8,128)(2,1)S(1)}, bf16[64,128,256]{2,1,0:T(8,128)(2,1)S(1)}, u32[]{:S(2)}, u32[]{:S(2)}) collective-permute-start(bf16[64,128,256]{2,1,0:T(8,128)(2,1)S(1)} %hidden_for_other_core.1), channel_id=1, source_target_pairs={{0,1},{1,0},{2,3},{3,2},{4,5},{5,4},{6,7},{7,6},{8,9},{9,8},{10,11... | collective-permute-start | bytes 12582920 | tf_op jit(solution)/shard_map/ppermute | solution.py:339
  113.4 7.9 %collective-permute-start.8 = (bf16[64,128,256]{2,1,0:T(8,128)(2,1)}, bf16[64,128,256]{2,1,0:T(8,128)(2,1)}, u32[]{:S(2)}, u32[]{:S(2)}) collective-permute-start(bf16[64,128,256]{2,1,0:T(8,128)(2,1)} %in_order_in_place.1.mine), channel_id=1, source_target_pairs={{0,1},{1,0},{2,3},{3,2},{4,5},{5,4},{6,7},{7,6},{8,9},{9,8},{10,11... | collective-permute-start | bytes 12582920 | tf_op jit(solution)/shard_map/ppermute | solution.py:339
  114.2 68.6 %all-to-all-start.1 = ((bf16[16,512,256]{2,1,0:T(8,128)(2,1)}), bf16[16,512,256]{2,1,0:T(8,128)(2,1)}, u32[]{:S(2)}, u32[]{:S(2)}) async-start(bf16[16,512,256]{2,1,0:T(8,128)(2,1)} %bitcast.19), calls=%async_computation.1 | async-start | bytes 8388608 | tf_op jit(solution)/shard_map/all_to_all | solution.py:399
  134.0 16.6 %collective-permute-start.9 = (bf16[512,256]{1,0:T(8,128)(2,1)}, bf16[512,256]{1,0:T(8,128)(2,1)S(1)}, u32[]{:S(2)}, u32[]{:S(2)}) collective-permute-start(bf16[512,256]{1,0:T(8,128)(2,1)} %get-tuple-element.12), channel_id=1, source_target_pairs={{0,8},{2,10},{4,12},{6,14},{8,0},{10,2},{12,4},{14,6},{1,9},{3,11}... | collective-permute-start | bytes 786440 | tf_op jit(solution)/shard_map/ppermute | solution.py:405
  140.8 34.1 %collective-permute-start.10 = (bf16[512,256]{1,0:T(8,128)(2,1)}, bf16[512,256]{1,0:T(8,128)(2,1)S(1)}, u32[]{:S(2)}, u32[]{:S(2)}) collective-permute-start(bf16[512,256]{1,0:T(8,128)(2,1)} %get-tuple-element.13), channel_id=1, source_target_pairs={{0,6},{2,8},{4,10},{6,12},{8,14},{10,0},{12,2},{14,4},{1,7},{3,9},... | collective-permute-start | bytes 786440 | tf_op jit(solution)/shard_map/ppermute | solution.py:405
  140.9 34.0 %collective-permute-start.11 = (bf16[512,256]{1,0:T(8,128)(2,1)}, bf16[512,256]{1,0:T(8,128)(2,1)S(1)}, u32[]{:S(2)}, u32[]{:S(2)}) collective-permute-start(bf16[512,256]{1,0:T(8,128)(2,1)} %get-tuple-element.14), channel_id=1, source_target_pairs={{0,10},{2,12},{4,14},{6,0},{8,2},{10,4},{12,6},{14,8},{1,11},{3,13... | collective-permute-start | bytes 786440 | tf_op jit(solution)/shard_map/ppermute | solution.py:405
  145.3 29.6 %collective-permute-start.12 = (bf16[512,256]{1,0:T(8,128)(2,1)S(1)}, bf16[512,256]{1,0:T(8,128)(2,1)S(1)}, u32[]{:S(2)}, u32[]{:S(2)}) collective-permute-start(bf16[512,256]{1,0:T(8,128)(2,1)S(1)} %get-tuple-element.15), channel_id=1, source_target_pairs={{0,4},{2,6},{4,8},{6,10},{8,12},{10,14},{12,0},{14,2},{1,5},{3,7},... | collective-permute-start | bytes 786440 | tf_op jit(solution)/shard_map/ppermute | solution.py:405
  145.3 36.4 %collective-permute-start.13 = (bf16[512,256]{1,0:T(8,128)(2,1)S(1)}, bf16[512,256]{1,0:T(8,128)(2,1)S(1)}, u32[]{:S(2)}, u32[]{:S(2)}) collective-permute-start(bf16[512,256]{1,0:T(8,128)(2,1)S(1)} %get-tuple-element.16), channel_id=1, source_target_pairs={{0,12},{2,14},{4,0},{6,2},{8,4},{10,6},{12,8},{14,10},{1,13},{3,15... | collective-permute-start | bytes 786440 | tf_op jit(solution)/shard_map/ppermute | solution.py:405
  160.2 22.6 %collective-permute-start.16 = (f32[128,256]{1,0:T(8,128)}, f32[128,256]{1,0:T(8,128)S(1)}, u32[]{:S(2)}, u32[]{:S(2)}) collective-permute-start(f32[128,256]{1,0:T(8,128)} %dynamic-slice_bitcast_fusion), channel_id=1, source_target_pairs={{0,1},{1,0},{2,3},{3,2},{4,5},{5,4},{6,7},{7,6},{8,9},{9,8},{10,11... | collective-permute-start | bytes 393224 | tf_op jit(solution)/shard_map/ppermute | solution.py:339
  196.7 13.0 %collective-permute-start.18 = (f32[8,256]{1,0:T(8,128)S(1)}, f32[8,256]{1,0:T(8,128)S(1)}, u32[]{:S(2)}, u32[]{:S(2)}) collective-permute-start(f32[8,256]{1,0:T(8,128)S(1)} %add.37), channel_id=1, source_target_pairs={{0,4},{2,6},{4,0},{6,2},{8,12},{10,14},{12,8},{14,10},{1,5},{3,7},... | collective-permute-start | bytes 24584 | tf_op jit(solution)/shard_map/ppermute | solution.py:352
  198.9 10.8 %collective-permute-start.19 = (f32[8,256]{1,0:T(8,128)S(1)}, f32[8,256]{1,0:T(8,128)S(1)}, u32[]{:S(2)}, u32[]{:S(2)}) collective-permute-start(f32[8,256]{1,0:T(8,128)S(1)} %add.37), channel_id=1, source_target_pairs={{0,8},{2,10},{4,12},{6,14},{8,0},{10,2},{12,4},{14,6},{1,9},{3,11}... | collective-permute-start | bytes 24584 | tf_op jit(solution)/shard_map/ppermute | solution.py:352
  202.8 7.0 %collective-permute-start.20 = (f32[8,256]{1,0:T(8,128)S(1)}, f32[8,256]{1,0:T(8,128)S(1)}, u32[]{:S(2)}, u32[]{:S(2)}) collective-permute-start(f32[8,256]{1,0:T(8,128)S(1)} %add.37), channel_id=1, source_target_pairs={{0,12},{2,14},{4,8},{6,10},{8,4},{10,6},{12,0},{14,2},{1,13},{3,15... | collective-permute-start | bytes 24584 | tf_op jit(solution)/shard_map/ppermute | solution.py:352
  207.0 18.5 %collective-permute-start.14 = (bf16[512,256]{1,0:T(8,128)(2,1)S(1)}, bf16[512,256]{1,0:T(8,128)(2,1)S(1)}, u32[]{:S(2)}, u32[]{:S(2)}) collective-permute-start(bf16[512,256]{1,0:T(8,128)(2,1)S(1)} %get-tuple-element.17), channel_id=1, source_target_pairs={{0,2},{2,4},{4,6},{6,8},{8,10},{10,12},{12,14},{14,0},{1,3},{3,5},... | collective-permute-start | bytes 786440 | tf_op jit(solution)/shard_map/ppermute | solution.py:405
  207.9 17.6 %collective-permute-start.15 = (bf16[512,256]{1,0:T(8,128)(2,1)S(1)}, bf16[512,256]{1,0:T(8,128)(2,1)S(1)}, u32[]{:S(2)}, u32[]{:S(2)}) collective-permute-start(bf16[512,256]{1,0:T(8,128)(2,1)S(1)} %get-tuple-element.18), channel_id=1, source_target_pairs={{0,14},{2,0},{4,2},{6,4},{8,6},{10,8},{12,10},{14,12},{1,15},{3,1}... | collective-permute-start | bytes 786440 | tf_op jit(solution)/shard_map/ppermute | solution.py:405
  219.6 7.1 %collective-permute-start.21 = (f32[128,256]{1,0:T(8,128)S(1)}, f32[128,256]{1,0:T(8,128)S(1)}, u32[]{:S(2)}, u32[]{:S(2)}) collective-permute-start(f32[128,256]{1,0:T(8,128)S(1)} %bitcast.25), channel_id=1, source_target_pairs={{0,1},{1,0},{2,3},{3,2},{4,5},{5,4},{6,7},{7,6},{8,9},{9,8},{10,11... | collective-permute-start | bytes 393224 | tf_op jit(solution)/shard_map/ppermute | solution.py:339
  (15 other events, 297.3 us)
Sparse Core Ops, SparseCore 0:
  24.7 88.6 all-gather.1

commit v7 on v6

--- a/solution.py
+++ b/solution.py
@@ -74,7 +74,7 @@
         total[i] = jnp.zeros(total.shape[1:], total.dtype)
         return carry
 
-    lax.fori_loop(0, total.shape[0], begin, 0)
+    lax.fori_loop(0, total.shape[0], begin, 0, unroll=4)
 
     def add(tile, block, r, row):
         at = r * 4 + lax.rem(row, 4)
@@ -108,7 +108,7 @@
         return carry
 
     if first:
-        lax.fori_loop(0, total.shape[0], cast, 0)
+        lax.fori_loop(0, total.shape[0], cast, 0, unroll=4)
 
 
 def add_kernel(mine, arrived, out):
@@ -116,7 +116,7 @@
         out[i] = (mine[i] + arrived[i].astype(mine.dtype)).astype(out.dtype)
         return carry
 
-    lax.fori_loop(0, mine.shape[0], one, 0)
+    lax.fori_loop(0, mine.shape[0], one, 0, unroll=4)
 
 
 def add_halves(mine, arrived):
@@ -195,7 +195,7 @@
         total[i] = jnp.zeros(total.shape[1:], total.dtype)
         return carry
 
-    lax.fori_loop(0, total.shape[0], begin, 0)
+    lax.fori_loop(0, total.shape[0], begin, 0, unroll=4)
     add_grads(where, meta, ids, cols, rows, count, sent, mine, peer, tiles, total)
     for k in range(4):
         outs[0][rows_at(k), :] = total[k]
@@ -397,7 +397,7 @@
     for_peer = hidden_parts(True, *operands, tile_values, feats)
     both = add_halves(hidden_parts(False, *operands, tile_values, feats), swap_cores(for_peer))
     parts = lax.all_to_all(both.reshape(16, 4 * BLK, width), PLANE, 0, 0, tiled=True)
-    [cot_mine] = same_later([cot_mine], mark(both))
+    [cot_mine] = same_later([cot_mine], both)
     own, *away = grad_parts(*operands, cot_mine, swap_cores(cot_mine), tile_values)
     by_partition = (16, 4 * BLK, width)
     scale = float(1.0 / node_total**0.5)

time: 234 us -> 235 us (level)
  starting transfers between devices: 75.2 us -> 65.8 us
  waiting for transfers between devices: 68.8 us -> 75.2 us
  Pallas kernels: 35.9 us -> 39.1 us
    ppermute x4, starting transfers between devices: 14.6 us -> 9.56 us  [swap_cores(): return lax.ppermute(a, 'col', [(0, 1), (1, 0)])]
    ppermute x7, waiting for transfers between devices: 18 us -> 22 us  [local(): lax.ppermute(part, 'z', [(z, (z + step) % 8) for z in range(8)])]
  transfers between devices with their start and end apart: 25 -> 25, of which waited for: 14 -> 14; matrix products, arithmetic and copies ran while one was open for 2% -> 2% of each run, Pallas kernels for 15% -> 16%
where the time goes in v7:
time: 235 us; the launch traced here: 234 us
  waiting for transfers between devices  75.2 us (32%)
  starting transfers between devices  65.8 us (28%)
  Pallas kernels  39.1 us (17%)
  blocking collectives  21.2 us (9%)
  local copies, waits for them, and re-layouts  15.8 us (7%)
  between operations  15 us (6%)
    ppermute x7, waiting for transfers between devices, steps_along(): lax.ppermute(a, axis, [(i, (i + s) % size) for i in range(size)])  35.2 us
    ppermute x7, waiting for transfers between devices, local(): lax.ppermute(part, 'z', [(z, (z + step) % 8) for z in range(8)])  22 us
    ppermute x7, starting transfers between devices, steps_along(): lax.ppermute(a, axis, [(i, (i + s) % size) for i in range(size)])  20.9 us
    pallas_call x2, Pallas kernels, hidden_parts(): pl.pallas_call(functools.partial(hidden_kernel, first), out_shape=jax.Sha...  15.4 us
    ppermute x7, starting transfers between devices, local(): lax.ppermute(part, 'z', [(z, (z + step) % 8) for z in range(8)])  15.3 us
    unnamed x39, local copies, waits for them, and re-layouts  13.2 us
    pallas_call x1, Pallas kernels, grad_parts(): pl.pallas_call(grad_kernel, out_shape=[jax.ShapeDtypeStruct((4 * BLK, wid...  12.6 us
    all_to_all x1, blocking collectives, sum_everywhere(): lax.all_to_all(half.reshape(16, 8, n), PLANE, 0, 0, tiled=True)  11.3 us
  transfers between devices with their start and end apart: 25, of which 14 were waited for; matrix products, arithmetic and copies ran while one was open for 2% of the time, Pallas kernels for 16%

profile of v7, /device:TPU:1, one launch (start us, length us, event | category | flops | bytes accessed | tf_op | source)
XLA Modules:
  0.0 234.0 jit_solution(10369075987047417998)
XLA Ops:
  13.7 7.7 %all-to-all-start = ((bf16[16,1040,128]{2,1,0:T(8,128)(2,1)}), bf16[16,1040,128]{2,1,0:T(8,128)(2,1)}, u32[]{:S(2)}, u32[]{:S(2)}) async-start(bf16[16,1040,128]{2,1,0:T(8,128)(2,1)} %copy-done.6), calls=%async_computation | async-start | bytes 8519680 | tf_op jit(solution)/shard_map/all_to_all | solution.py:390
  27.0 3.5 %collective-permute-start.2 = (bf16[528,256]{1,0:T(8,128)(2,1)S(1)}, bf16[528,256]{1,0:T(8,128)(2,1)S(1)}, u32[]{:S(2)}, u32[]{:S(2)}) collective-permute-start(bf16[528,256]{1,0:T(8,128)(2,1)S(1)} %fusion.1.rest_0_), channel_id=1, source_target_pairs={{0,6},{2,8},{4,10},{6,12},{8,14},{10,0},{12,2},{14,4},{1,7},{3,9},... | collective-permute-start | bytes 811016 | tf_op jit(solution)/shard_map/ppermute | solution.py:343
  31.3 4.5 %collective-permute-start.4 = (bf16[528,256]{1,0:T(8,128)(2,1)S(1)}, bf16[528,256]{1,0:T(8,128)(2,1)S(1)}, u32[]{:S(2)}, u32[]{:S(2)}) collective-permute-start(bf16[528,256]{1,0:T(8,128)(2,1)S(1)} %fusion.1.rest_0_), channel_id=1, source_target_pairs={{0,10},{2,12},{4,14},{6,0},{8,2},{10,4},{12,6},{14,8},{1,11},{3,13... | collective-permute-start | bytes 811016 | tf_op jit(solution)/shard_map/ppermute | solution.py:343
  38.3 4.1 %collective-permute-done.1.rest_2_ = bf16[528,256]{1,0:T(8,128)(2,1)S(1)} collective-permute-done((bf16[528,256]{1,0:T(8,128)(2,1)S(1)}, bf16[528,256]{1,0:T(8,128)(2,1)S(1)}, u32[]{:S(2)}, u32[]{:S(2)}) %collective-permute-start.1) | collective-permute-done | bytes 270368 | tf_op jit(solution)/shard_map/ppermute | solution.py:343
  42.4 5.0 %collective-permute-start.6 = (bf16[528,256]{1,0:T(8,128)(2,1)S(1)}, bf16[528,256]{1,0:T(8,128)(2,1)S(1)}, u32[]{:S(2)}, u32[]{:S(2)}) collective-permute-start(bf16[528,256]{1,0:T(8,128)(2,1)S(1)} %fusion.1.rest_0_), channel_id=1, source_target_pairs={{0,14},{2,0},{4,2},{6,4},{8,6},{10,8},{12,10},{14,12},{1,15},{3,1}... | collective-permute-start | bytes 811016 | tf_op jit(solution)/shard_map/ppermute | solution.py:343
  47.5 13.4 %collective-permute-done.2.rest_3_ = bf16[528,256]{1,0:T(8,128)(2,1)S(1)} collective-permute-done((bf16[528,256]{1,0:T(8,128)(2,1)S(1)}, bf16[528,256]{1,0:T(8,128)(2,1)S(1)}, u32[]{:S(2)}, u32[]{:S(2)}) %collective-permute-start.2) | collective-permute-done | bytes 270368 | tf_op jit(solution)/shard_map/ppermute | solution.py:343
  60.8 7.4 %collective-permute-done.3.rest_4_ = bf16[528,256]{1,0:T(8,128)(2,1)S(1)} collective-permute-done((bf16[528,256]{1,0:T(8,128)(2,1)S(1)}, bf16[528,256]{1,0:T(8,128)(2,1)S(1)}, u32[]{:S(2)}, u32[]{:S(2)}) %collective-permute-start.3) | collective-permute-done | bytes 270368 | tf_op jit(solution)/shard_map/ppermute | solution.py:343
  68.8 7.6 %collective-permute-done.5.rest_6_ = bf16[528,256]{1,0:T(8,128)(2,1)S(1)} collective-permute-done((bf16[528,256]{1,0:T(8,128)(2,1)S(1)}, bf16[528,256]{1,0:T(8,128)(2,1)S(1)}, u32[]{:S(2)}, u32[]{:S(2)}) %collective-permute-start.5) | collective-permute-done | bytes 270368 | tf_op jit(solution)/shard_map/ppermute | solution.py:343
  79.8 5.6 %all-to-all-done.sent = bf16[16,1040,128]{2,1,0:T(8,128)(2,1)} async-done(((bf16[16,1040,128]{2,1,0:T(8,128)(2,1)}), bf16[16,1040,128]{2,1,0:T(8,128)(2,1)}, u32[]{:S(2)}, u32[]{:S(2)}) %all-to-all-start) | async-done | bytes 4259872 | tf_op jit(solution)/shard_map/all_to_all | solution.py:390
  86.3 8.1 %hidden_for_other_core.1 = bf16[64,128,256]{2,1,0:T(8,128)(2,1)S(1)} custom-call(s32[5]{0:T(128)S(1)} %stack.42.where, s32[128]{0:T(128)S(1)} %reshape.50.meta, s32[128]{0:T(128)S(1)} %reshape.43.ids, s32[40]{0:T(128)S(1)} %copy-done.9, s32[40]{0:T(128)S(1)} %copy-done.11, s32[1]{0:T(128)S(6)} %copy.24.count, bf16[16,1040,128]{2,1,0:T(8,128)(2,1)} %all-to-all-done.sent, ...), custom_call_target="tpu_custom_call" | custom-call | flops 1000000000 | bytes 30000000 | tf_op jit(solution)/shard_map/hidden_for_other_core/pallas_call | solution.py:139
  96.4 7.3 %hidden_sums.1.mine = f32[64,128,256]{2,1,0:T(8,128)S(1)} custom-call(s32[5]{0:T(128)S(1)} %stack.42.where, s32[128]{0:T(128)S(1)} %reshape.50.meta, s32[128]{0:T(128)S(1)} %reshape.43.ids, s32[40]{0:T(128)S(1)} %copy-done.9, s32[40]{0:T(128)S(1)} %copy-done.11, s32[1]{0:T(128)S(6)} %copy.24.count, bf16[16,1040,128]{2,1,0:T(8,128)(2,1)} %all-to-all-done.sent, ...), custom_call_target="tpu_custom_call" | custom-call | flops 1000000000 | bytes 30000000 | tf_op jit(solution)/shard_map/hidden_sums/pallas_call | solution.py:139
  106.4 6.6 %all-gather.2.cloned.1.call-done.refs_0_ = bf16[64,128,256]{2,1,0:T(8,128)(2,1)} async-done(((bf16[4,128,256]{2,1,0:T(8,128)(2,1)}), bf16[64,128,256]{2,1,0:T(8,128)(2,1)}) %all-gather.2.cloned.1.call-update) | async-done | bytes 4194320 | tf_op jit(solution)/shard_map/all_gather | solution.py:388
  113.7 5.0 %all-to-all-start.1 = ((bf16[16,512,256]{2,1,0:T(8,128)(2,1)}), bf16[16,512,256]{2,1,0:T(8,128)(2,1)}, u32[]{:S(2)}, u32[]{:S(2)}) async-start(bf16[16,512,256]{2,1,0:T(8,128)(2,1)} %bitcast.17), calls=%async_computation.1 | async-start | bytes 8388608 | tf_op jit(solution)/shard_map/all_to_all | solution.py:399
  123.0 12.6 %grad_sums.1 = (f32[512,256]{1,0:T(8,128)S(1)}, bf16[512,256]{1,0:T(8,128)(2,1)S(1)}, bf16[512,256]{1,0:T(8,128)(2,1)S(1)}, bf16[512,256]{1,0:T(8,128)(2,1)}, bf...) custom-call(s32[5]{0:T(128)S(1)} %stack.42.where, ...), custom_call_target="tpu_custom_call" | custom-call | flops 800000000 | bytes 24000000 | tf_op jit(solution)/shard_map/grad_sums/pallas_call | solution.py:211
  135.7 4.4 %collective-permute-start.9 = (bf16[512,256]{1,0:T(8,128)(2,1)}, bf16[512,256]{1,0:T(8,128)(2,1)S(1)}, u32[]{:S(2)}, u32[]{:S(2)}) collective-permute-start(bf16[512,256]{1,0:T(8,128)(2,1)} %get-tuple-element.12), channel_id=1, source_target_pairs={{0,8},{2,10},{4,12},{6,14},{8,0},{10,2},{12,4},{14,6},{1,9},{3,11}... | collective-permute-start | bytes 786440 | tf_op jit(solution)/shard_map/ppermute | solution.py:405
  140.1 4.5 %collective-permute-start.11 = (bf16[512,256]{1,0:T(8,128)(2,1)}, bf16[512,256]{1,0:T(8,128)(2,1)S(1)}, u32[]{:S(2)}, u32[]{:S(2)}) collective-permute-start(bf16[512,256]{1,0:T(8,128)(2,1)} %get-tuple-element.14), channel_id=1, source_target_pairs={{0,10},{2,12},{4,14},{6,0},{8,2},{10,4},{12,6},{14,8},{1,11},{3,13... | collective-permute-start | bytes 786440 | tf_op jit(solution)/shard_map/ppermute | solution.py:405
  154.2 4.4 %weight_term.1 = f32[256,256]{1,0:T(8,128)S(1)} custom-call(bf16[16,512,256]{2,1,0:T(8,128)(2,1)S(1)} %bitcast.18, bf16[16,512,256]{2,1,0:T(8,128)(2,1)S(1)} %bitcast.19, bf16[8,256]{1,0:T(8,128)(2,1)S(1)} %get-tuple-element.22.after), custom_call_target="tpu_custom_call" | custom-call | flops 400000000 | bytes 12000000 | tf_op jit(solution)/shard_map/weight_term/pallas_call | solution.py:241
  160.4 12.0 %collective-permute-done.10.rest_1_ = bf16[512,256]{1,0:T(8,128)(2,1)S(1)} collective-permute-done((bf16[512,256]{1,0:T(8,128)(2,1)}, bf16[512,256]{1,0:T(8,128)(2,1)S(1)}, u32[]{:S(2)}, u32[]{:S(2)}) %collective-permute-start.10) | collective-permute-done | bytes 262176 | tf_op jit(solution)/shard_map/ppermute | solution.py:405
  175.6 5.1 %collective-permute-done.13.rest_4_ = bf16[512,256]{1,0:T(8,128)(2,1)S(1)} collective-permute-done((bf16[512,256]{1,0:T(8,128)(2,1)S(1)}, bf16[512,256]{1,0:T(8,128)(2,1)S(1)}, u32[]{:S(2)}, u32[]{:S(2)}) %collective-permute-start.13) | collective-permute-done | bytes 262176 | tf_op jit(solution)/shard_map/ppermute | solution.py:405
  182.4 11.3 %all_to_all.20 = f32[16,8,256]{2,1,0:T(8,128)S(1)} all-to-all(f32[16,8,256]{2,1,0:T(8,128)S(1)} %bitcast.22), channel_id=1, replica_groups=mesh['y'=4,'x'=4,'z'=8,'col'=2] {'y','x'}, dimensions={0} | all-to-all | bytes 262144 | tf_op jit(solution)/shard_map/all_to_all | solution.py:368
  198.7 3.6 %collective-permute-start.19 = (f32[8,256]{1,0:T(8,128)S(1)}, f32[8,256]{1,0:T(8,128)S(1)}, u32[]{:S(2)}, u32[]{:S(2)}) collective-permute-start(f32[8,256]{1,0:T(8,128)S(1)} %add.37), channel_id=1, source_target_pairs={{0,8},{2,10},{4,12},{6,14},{8,0},{10,2},{12,4},{14,6},{1,9},{3,11}... | collective-permute-start | bytes 24584 | tf_op jit(solution)/shard_map/ppermute | solution.py:352
  202.3 3.6 %output_rows.1 = bf16[512,256]{1,0:T(8,128)(2,1)} custom-call(bf16[16,512,256]{2,1,0:T(8,128)(2,1)} %all-to-all-done.1.parts.refs_1_, bf16[256,256]{1,0:T(8,128)(2,1)S(1)} %copy-done.7), custom_call_target="tpu_custom_call" | custom-call | flops 400000000 | bytes 12000000 | tf_op jit(solution)/shard_map/output_rows/pallas_call | solution.py:263
  209.4 9.9 %all_to_all.21 = f32[16,8,256]{2,1,0:T(8,128)S(1)} all-to-all(f32[16,8,256]{2,1,0:T(8,128)S(1)} %broadcast_in_dim.2), channel_id=1, replica_groups=mesh['y'=4,'x'=4,'z'=8,'col'=2] {'y','x'}, dimensions={0} | all-to-all | bytes 262144 | tf_op jit(solution)/shard_map/all_to_all | solution.py:371
  219.3 5.9 %collective-permute-start.21 = (f32[128,256]{1,0:T(8,128)S(1)}, f32[128,256]{1,0:T(8,128)S(1)}, u32[]{:S(2)}, u32[]{:S(2)}) collective-permute-start(f32[128,256]{1,0:T(8,128)S(1)} %bitcast.23), channel_id=1, source_target_pairs={{0,1},{1,0},{2,3},{3,2},{4,5},{5,4},{6,7},{7,6},{8,9},{9,8},{10,11... | collective-permute-start | bytes 393224 | tf_op jit(solution)/shard_map/ppermute | solution.py:339
  (114 shorter events, 55.7 us)
Async XLA Ops:
  13.7 71.7 %all-to-all-start = ((bf16[16,1040,128]{2,1,0:T(8,128)(2,1)}), bf16[16,1040,128]{2,1,0:T(8,128)(2,1)}, u32[]{:S(2)}, u32[]{:S(2)}) async-start(bf16[16,1040,128]{2,1,0:T(8,128)(2,1)} %copy-done.6), calls=%async_computation | async-start | bytes 8519680 | tf_op jit(solution)/shard_map/all_to_all | solution.py:390
  21.3 91.7 %all-gather.2.cloned.1.call-start = ((), (), s32[]{:S(2)}) async-start(), calls=%async_computation.4 | async-start | bytes 4456448 | tf_op jit(solution)/shard_map/all_gather | solution.py:388
  22.1 13.9 %collective-permute-start = (bf16[528,256]{1,0:T(8,128)(2,1)S(1)}, bf16[528,256]{1,0:T(8,128)(2,1)S(1)}, u32[]{:S(2)}, u32[]{:S(2)}) collective-permute-start(bf16[528,256]{1,0:T(8,128)(2,1)S(1)} %fusion.1.rest_0_), channel_id=1, source_target_pairs={{0,2},{2,4},{4,6},{6,8},{8,10},{10,12},{12,14},{14,0},{1,3},{3,5},... | collective-permute-start | bytes 811016 | tf_op jit(solution)/shard_map/ppermute | solution.py:343
  23.9 18.5 %collective-permute-start.1 = (bf16[528,256]{1,0:T(8,128)(2,1)S(1)}, bf16[528,256]{1,0:T(8,128)(2,1)S(1)}, u32[]{:S(2)}, u32[]{:S(2)}) collective-permute-start(bf16[528,256]{1,0:T(8,128)(2,1)S(1)} %fusion.1.rest_0_), channel_id=1, source_target_pairs={{0,4},{2,6},{4,8},{6,10},{8,12},{10,14},{12,0},{14,2},{1,5},{3,7},... | collective-permute-start | bytes 811016 | tf_op jit(solution)/shard_map/ppermute | solution.py:343
  27.0 33.8 %collective-permute-start.2 = (bf16[528,256]{1,0:T(8,128)(2,1)S(1)}, bf16[528,256]{1,0:T(8,128)(2,1)S(1)}, u32[]{:S(2)}, u32[]{:S(2)}) collective-permute-start(bf16[528,256]{1,0:T(8,128)(2,1)S(1)} %fusion.1.rest_0_), channel_id=1, source_target_pairs={{0,6},{2,8},{4,10},{6,12},{8,14},{10,0},{12,2},{14,4},{1,7},{3,9},... | collective-permute-start | bytes 811016 | tf_op jit(solution)/shard_map/ppermute | solution.py:343
  30.6 37.7 %collective-permute-start.3 = (bf16[528,256]{1,0:T(8,128)(2,1)S(1)}, bf16[528,256]{1,0:T(8,128)(2,1)S(1)}, u32[]{:S(2)}, u32[]{:S(2)}) collective-permute-start(bf16[528,256]{1,0:T(8,128)(2,1)S(1)} %fusion.1.rest_0_), channel_id=1, source_target_pairs={{0,8},{2,10},{4,12},{6,14},{8,0},{10,2},{12,4},{14,6},{1,9},{3,11}... | collective-permute-start | bytes 811016 | tf_op jit(solution)/shard_map/ppermute | solution.py:343
  31.3 37.4 %collective-permute-start.4 = (bf16[528,256]{1,0:T(8,128)(2,1)S(1)}, bf16[528,256]{1,0:T(8,128)(2,1)S(1)}, u32[]{:S(2)}, u32[]{:S(2)}) collective-permute-start(bf16[528,256]{1,0:T(8,128)(2,1)S(1)} %fusion.1.rest_0_), channel_id=1, source_target_pairs={{0,10},{2,12},{4,14},{6,0},{8,2},{10,4},{12,6},{14,8},{1,11},{3,13... | collective-permute-start | bytes 811016 | tf_op jit(solution)/shard_map/ppermute | solution.py:343
  36.0 40.4 %collective-permute-start.5 = (bf16[528,256]{1,0:T(8,128)(2,1)S(1)}, bf16[528,256]{1,0:T(8,128)(2,1)S(1)}, u32[]{:S(2)}, u32[]{:S(2)}) collective-permute-start(bf16[528,256]{1,0:T(8,128)(2,1)S(1)} %fusion.1.rest_0_), channel_id=1, source_target_pairs={{0,12},{2,14},{4,0},{6,2},{8,4},{10,6},{12,8},{14,10},{1,13},{3,15... | collective-permute-start | bytes 811016 | tf_op jit(solution)/shard_map/ppermute | solution.py:343
  42.4 36.8 %collective-permute-start.6 = (bf16[528,256]{1,0:T(8,128)(2,1)S(1)}, bf16[528,256]{1,0:T(8,128)(2,1)S(1)}, u32[]{:S(2)}, u32[]{:S(2)}) collective-permute-start(bf16[528,256]{1,0:T(8,128)(2,1)S(1)} %fusion.1.rest_0_), channel_id=1, source_target_pairs={{0,14},{2,0},{4,2},{6,4},{8,6},{10,8},{12,10},{14,12},{1,15},{3,1}... | collective-permute-start | bytes 811016 | tf_op jit(solution)/shard_map/ppermute | solution.py:343
  94.5 9.2 %collective-permute-start.7 = (bf16[64,128,256]{2,1,0:T(8,128)(2,1)S(1)}, bf16[64,128,256]{2,1,0:T(8,128)(2,1)S(1)}, u32[]{:S(2)}, u32[]{:S(2)}) collective-permute-start(bf16[64,128,256]{2,1,0:T(8,128)(2,1)S(1)} %hidden_for_other_core.1), channel_id=1, source_target_pairs={{0,1},{1,0},{2,3},{3,2},{4,5},{5,4},{6,7},{7,6},{8,9},{9,8},{10,11... | collective-permute-start | bytes 12582920 | tf_op jit(solution)/shard_map/ppermute | solution.py:339
  113.1 7.8 %collective-permute-start.8 = (bf16[64,128,256]{2,1,0:T(8,128)(2,1)}, bf16[64,128,256]{2,1,0:T(8,128)(2,1)}, u32[]{:S(2)}, u32[]{:S(2)}) collective-permute-start(bf16[64,128,256]{2,1,0:T(8,128)(2,1)} %in_order_in_place.1.mine), channel_id=1, source_target_pairs={{0,1},{1,0},{2,3},{3,2},{4,5},{5,4},{6,7},{7,6},{8,9},{9,8},{10,11... | collective-permute-start | bytes 12582920 | tf_op jit(solution)/shard_map/ppermute | solution.py:339
  113.7 68.6 %all-to-all-start.1 = ((bf16[16,512,256]{2,1,0:T(8,128)(2,1)}), bf16[16,512,256]{2,1,0:T(8,128)(2,1)}, u32[]{:S(2)}, u32[]{:S(2)}) async-start(bf16[16,512,256]{2,1,0:T(8,128)(2,1)} %bitcast.17), calls=%async_computation.1 | async-start | bytes 8388608 | tf_op jit(solution)/shard_map/all_to_all | solution.py:399
  135.7 14.2 %collective-permute-start.9 = (bf16[512,256]{1,0:T(8,128)(2,1)}, bf16[512,256]{1,0:T(8,128)(2,1)S(1)}, u32[]{:S(2)}, u32[]{:S(2)}) collective-permute-start(bf16[512,256]{1,0:T(8,128)(2,1)} %get-tuple-element.12), channel_id=1, source_target_pairs={{0,8},{2,10},{4,12},{6,14},{8,0},{10,2},{12,4},{14,6},{1,9},{3,11}... | collective-permute-start | bytes 786440 | tf_op jit(solution)/shard_map/ppermute | solution.py:405
  140.1 32.3 %collective-permute-start.10 = (bf16[512,256]{1,0:T(8,128)(2,1)}, bf16[512,256]{1,0:T(8,128)(2,1)S(1)}, u32[]{:S(2)}, u32[]{:S(2)}) collective-permute-start(bf16[512,256]{1,0:T(8,128)(2,1)} %get-tuple-element.13), channel_id=1, source_target_pairs={{0,6},{2,8},{4,10},{6,12},{8,14},{10,0},{12,2},{14,4},{1,7},{3,9},... | collective-permute-start | bytes 786440 | tf_op jit(solution)/shard_map/ppermute | solution.py:405
  140.1 32.3 %collective-permute-start.11 = (bf16[512,256]{1,0:T(8,128)(2,1)}, bf16[512,256]{1,0:T(8,128)(2,1)S(1)}, u32[]{:S(2)}, u32[]{:S(2)}) collective-permute-start(bf16[512,256]{1,0:T(8,128)(2,1)} %get-tuple-element.14), channel_id=1, source_target_pairs={{0,10},{2,12},{4,14},{6,0},{8,2},{10,4},{12,6},{14,8},{1,11},{3,13... | collective-permute-start | bytes 786440 | tf_op jit(solution)/shard_map/ppermute | solution.py:405
  144.6 31.0 %collective-permute-start.12 = (bf16[512,256]{1,0:T(8,128)(2,1)S(1)}, bf16[512,256]{1,0:T(8,128)(2,1)S(1)}, u32[]{:S(2)}, u32[]{:S(2)}) collective-permute-start(bf16[512,256]{1,0:T(8,128)(2,1)S(1)} %get-tuple-element.15), channel_id=1, source_target_pairs={{0,4},{2,6},{4,8},{6,10},{8,12},{10,14},{12,0},{14,2},{1,5},{3,7},... | collective-permute-start | bytes 786440 | tf_op jit(solution)/shard_map/ppermute | solution.py:405
  145.5 35.2 %collective-permute-start.13 = (bf16[512,256]{1,0:T(8,128)(2,1)S(1)}, bf16[512,256]{1,0:T(8,128)(2,1)S(1)}, u32[]{:S(2)}, u32[]{:S(2)}) collective-permute-start(bf16[512,256]{1,0:T(8,128)(2,1)S(1)} %get-tuple-element.16), channel_id=1, source_target_pairs={{0,12},{2,14},{4,0},{6,2},{8,4},{10,6},{12,8},{14,10},{1,13},{3,15... | collective-permute-start | bytes 786440 | tf_op jit(solution)/shard_map/ppermute | solution.py:405
  159.3 23.0 %collective-permute-start.16 = (f32[128,256]{1,0:T(8,128)}, f32[128,256]{1,0:T(8,128)S(1)}, u32[]{:S(2)}, u32[]{:S(2)}) collective-permute-start(f32[128,256]{1,0:T(8,128)} %dynamic-slice_bitcast_fusion), channel_id=1, source_target_pairs={{0,1},{1,0},{2,3},{3,2},{4,5},{5,4},{6,7},{7,6},{8,9},{9,8},{10,11... | collective-permute-start | bytes 393224 | tf_op jit(solution)/shard_map/ppermute | solution.py:339
  196.3 13.0 %collective-permute-start.18 = (f32[8,256]{1,0:T(8,128)S(1)}, f32[8,256]{1,0:T(8,128)S(1)}, u32[]{:S(2)}, u32[]{:S(2)}) collective-permute-start(f32[8,256]{1,0:T(8,128)S(1)} %add.37), channel_id=1, source_target_pairs={{0,4},{2,6},{4,0},{6,2},{8,12},{10,14},{12,8},{14,10},{1,5},{3,7},... | collective-permute-start | bytes 24584 | tf_op jit(solution)/shard_map/ppermute | solution.py:352
  198.7 10.7 %collective-permute-start.19 = (f32[8,256]{1,0:T(8,128)S(1)}, f32[8,256]{1,0:T(8,128)S(1)}, u32[]{:S(2)}, u32[]{:S(2)}) collective-permute-start(f32[8,256]{1,0:T(8,128)S(1)} %add.37), channel_id=1, source_target_pairs={{0,8},{2,10},{4,12},{6,14},{8,0},{10,2},{12,4},{14,6},{1,9},{3,11}... | collective-permute-start | bytes 24584 | tf_op jit(solution)/shard_map/ppermute | solution.py:352
  202.3 7.1 %collective-permute-start.20 = (f32[8,256]{1,0:T(8,128)S(1)}, f32[8,256]{1,0:T(8,128)S(1)}, u32[]{:S(2)}, u32[]{:S(2)}) collective-permute-start(f32[8,256]{1,0:T(8,128)S(1)} %add.37), channel_id=1, source_target_pairs={{0,12},{2,14},{4,8},{6,10},{8,4},{10,6},{12,0},{14,2},{1,13},{3,15... | collective-permute-start | bytes 24584 | tf_op jit(solution)/shard_map/ppermute | solution.py:352
  206.6 18.7 %collective-permute-start.14 = (bf16[512,256]{1,0:T(8,128)(2,1)S(1)}, bf16[512,256]{1,0:T(8,128)(2,1)S(1)}, u32[]{:S(2)}, u32[]{:S(2)}) collective-permute-start(bf16[512,256]{1,0:T(8,128)(2,1)S(1)} %get-tuple-element.17), channel_id=1, source_target_pairs={{0,2},{2,4},{4,6},{6,8},{8,10},{10,12},{12,14},{14,0},{1,3},{3,5},... | collective-permute-start | bytes 786440 | tf_op jit(solution)/shard_map/ppermute | solution.py:405
  207.5 17.7 %collective-permute-start.15 = (bf16[512,256]{1,0:T(8,128)(2,1)S(1)}, bf16[512,256]{1,0:T(8,128)(2,1)S(1)}, u32[]{:S(2)}, u32[]{:S(2)}) collective-permute-start(bf16[512,256]{1,0:T(8,128)(2,1)S(1)} %get-tuple-element.18), channel_id=1, source_target_pairs={{0,14},{2,0},{4,2},{6,4},{8,6},{10,8},{12,10},{14,12},{1,15},{3,1}... | collective-permute-start | bytes 786440 | tf_op jit(solution)/shard_map/ppermute | solution.py:405
  219.3 7.1 %collective-permute-start.21 = (f32[128,256]{1,0:T(8,128)S(1)}, f32[128,256]{1,0:T(8,128)S(1)}, u32[]{:S(2)}, u32[]{:S(2)}) collective-permute-start(f32[128,256]{1,0:T(8,128)S(1)} %bitcast.23), channel_id=1, source_target_pairs={{0,1},{1,0},{2,3},{3,2},{4,5},{5,4},{6,7},{7,6},{8,9},{9,8},{10,11... | collective-permute-start | bytes 393224 | tf_op jit(solution)/shard_map/ppermute | solution.py:339
  (15 other events, 294.2 us)
Sparse Core Ops, SparseCore 0:
  24.6 88.4 all-gather.1
